TPU v7x, 32 devices: a whole 2x2x4 slice. The times are simulated.
32 devices in a mesh: dp: 8 (over z, x), tensor: 4 (over y, core).
Axes of the slice: x: 2, y: 2, z: 4, core: 2. Of those that a mesh axis runs over, the one named last changes fastest.
Arguments:
- tokens: bfloat16 [32, 512, 512], P('dp', 'tensor'), may hold values from -6 to 6
- valid: int32 [32], P('dp'), may hold values from 2 to 8, as said below
- w_qkv: bfloat16 [512, 1536], P(None, ('dp', 'tensor')), may hold values from -0.25 to 0.25
- w_out: bfloat16 [512, 512], P(None, ('dp', 'tensor')), may hold values from -1 to 1
- vectors: bfloat16 [12, 512], P(None, ('dp', 'tensor')), may hold values from -1.5 to 1.5, as said below
- w_up: bfloat16 [512, 2048], P('dp', 'tensor'), may hold values from -0.25 to 0.25
- w_down: bfloat16 [2048, 512], P('tensor', 'dp'), may hold values from -0.25 to 0.25
- cotangent: bfloat16 [32, 512, 512], P('dp', 'tensor'), may hold values from -6 to 6
Outputs:
- output: bfloat16 [32, 512, 512], P('dp', 'tensor')
- grad_tokens: float32 [32, 512, 512], P('dp', 'tensor')
- grad_w_qkv: float32 [512, 1536], P(None, ('dp', 'tensor'))
- grad_w_out: float32 [512, 512], P(None, ('dp', 'tensor'))
- grad_vectors: float32 [12, 512], P(None, ('dp', 'tensor'))
- grad_w_up: float32 [512, 2048], P('dp', 'tensor')
- grad_w_down: float32 [2048, 512], P('tensor', 'dp')
Inputs may be any that keep to these rules, and one draw needn't show every extreme that they name: In every group of 4 consecutive clips one clip is valid over all 64 time rows. `vectors`: rows 0 and 5 lie near one, the others about zero.
All inputs are finite; a program needn't handle non-finite values.
Results may differ from a plain program's by a relative error of at most 0.014.
Values may be sent and summed in bfloat16 or wider, within the bound.
No kernel may reach another device: no remote copies, remote signals or barrier semaphores. Data moves between devices by JAX's collectives and lax.ppermute only.
A program may use at most 128 MiB of HBM per device.

v0:
```python
import jax
import jax.numpy as jnp
from jax import lax
from jax.sharding import PartitionSpec as P

D = 512
FF = 2048
HEADS = 16
FREQ = 8
WINDOW = 4
SHIFT = 2
ROW_UNIT = 8


norm_eps = 1e-06
masked_score = -1000000000.0
inv_root_two = 0.7071067811865476
inv_root_tau = 0.3989422804014327


def extended_2(block, sides, width):
    for axis, dim in sides:
        count = lax.axis_size(axis)
        forward = [(i, i + 1) for i in range(count - 1)]
        backward = [(target, source) for source, target in forward]
        low = lax.ppermute(
            lax.slice_in_dim(block, block.shape[dim] - width, None, axis=dim), axis, forward
        )
        high = lax.ppermute(lax.slice_in_dim(block, 0, width, axis=dim), axis, backward)
        block = jnp.concatenate([low, block, high], axis=dim)
    return block


def in_blocks(array, dim, peers):
    before, after = (array.shape[:dim], array.shape[dim + 1 :])
    return jnp.moveaxis(array.reshape(*before, peers, -1, *after), dim, 0)


def sum_at_owner(array, axis, dim):
    tiles = in_blocks(array, dim, lax.axis_size(axis))
    arrived = lax.all_to_all(tiles, axis, split_axis=0, concat_axis=0, tiled=True)
    return arrived.astype(jnp.float32).sum(axis=0)


def norm_parts(values):
    row_mean = jnp.mean(values, axis=-1, keepdims=True)
    centred = values - row_mean
    variance = jnp.mean(centred * centred, axis=-1, keepdims=True)
    inverse = lax.rsqrt(variance + norm_eps)
    return (centred * inverse, inverse)


def norm_back(grad_normed, scaled, inverse, gain):
    grad_hat = grad_normed * gain
    centre_term = jnp.mean(grad_hat, axis=-1, keepdims=True)
    slope_term = jnp.mean(grad_hat * scaled, axis=-1, keepdims=True)
    return inverse * (grad_hat - centre_term - scaled * slope_term)


def gelu_slope(values):
    return (
        0.5 * (1.0 + lax.erf(values * inv_root_two))
        + values * jnp.exp(-0.5 * values * values) * inv_root_tau
    )


def contract_last(first_arr, second_arr):
    return lax.dot_general(
        first_arr,
        second_arr,
        (((first_arr.ndim - 1,), (1,)), ((), ())),
        preferred_element_type=jnp.float32,
    )


def contract_rows(first_arr, second_arr):
    return lax.dot_general(
        first_arr, second_arr, (((0,), (0,)), ((), ())), preferred_element_type=jnp.float32
    )


def column_sum(values):
    return jnp.sum(values, axis=tuple(range(values.ndim - 1)), dtype=jnp.float32)


def pad_columns(values):
    return jnp.pad(values, ((0, 0), (0, 0), (SHIFT, SHIFT), (0, 0)))


def split_windows(values):
    group_count, row_count, col_count, channels = values.shape
    shaped = values.reshape(
        group_count, row_count // WINDOW, WINDOW, col_count // WINDOW, WINDOW, channels
    )
    shaped = shaped.transpose(0, 1, 3, 2, 4, 5)
    return shaped.reshape(
        group_count, row_count // WINDOW * (col_count // WINDOW), WINDOW * WINDOW, channels
    )


def join_windows(values, row_count, col_count):
    group_count = values.shape[0]
    channels = values.shape[-1]
    shaped = values.reshape(
        group_count, row_count // WINDOW, col_count // WINDOW, WINDOW, WINDOW, channels
    )
    shaped = shaped.transpose(0, 1, 3, 2, 4, 5)
    return shaped.reshape(group_count, row_count, col_count, channels)


def head_split(values):
    return values.reshape(values.shape[:3] + (HEADS, D // HEADS))


def key_window_mask(limit_rows, first_time, time_count):
    time_index = first_time - SHIFT + jnp.arange(time_count + 2 * SHIFT)
    freq_index = jnp.arange(FREQ + 2 * SHIFT) - SHIFT
    time_ok = (time_index[None, :] >= 0) & (time_index[None, :] < limit_rows[:, None])
    freq_ok = (freq_index >= 0) & (freq_index < FREQ)
    key_ok = (time_ok[:, :, None] & freq_ok[None, None, :]).astype(jnp.int32)[..., None]
    return (split_windows(key_ok)[..., 0] == 1)[:, :, None, None, :]


def window_scores(query_heads, key_heads, key_windows):
    raw_scores = jnp.einsum(
        "cwqhe,cwkhe->cwhqk", query_heads, key_heads, preferred_element_type=jnp.float32
    ) * (D // HEADS) ** (-0.5)
    return jnp.where(key_windows, raw_scores, masked_score)


def attend_forward(query_heads, key_heads, value_heads, key_windows):
    scores = window_scores(query_heads, key_heads, key_windows)
    top_score = jnp.max(scores, axis=-1, keepdims=True)
    exponent_vals = jnp.exp(scores - top_score)
    row_total = jnp.sum(exponent_vals, axis=-1, keepdims=True)
    log_total = top_score + jnp.log(row_total)
    probs_low = (exponent_vals / row_total).astype(jnp.bfloat16)
    mixed_win = jnp.einsum(
        "cwhqk,cwkhe->cwqhe", probs_low, value_heads, preferred_element_type=jnp.float32
    )
    return (mixed_win, log_total, probs_low)


def attend_backward(
    grad_mixed_heads, query_heads, key_heads, value_heads, key_windows, log_total, probs_low
):
    score_scale = (D // HEADS) ** (-0.5)
    probs = jnp.exp(window_scores(query_heads, key_heads, key_windows) - log_total)
    grad_probs = jnp.einsum(
        "cwqhe,cwkhe->cwhqk", grad_mixed_heads, value_heads, preferred_element_type=jnp.float32
    )
    row_dot = jnp.sum(probs * grad_probs, axis=-1, keepdims=True)
    grad_scores = jnp.where(key_windows, probs * (grad_probs - row_dot), 0.0).astype(jnp.bfloat16)
    grad_query = (
        jnp.einsum("cwhqk,cwkhe->cwqhe", grad_scores, key_heads, preferred_element_type=jnp.float32)
        * score_scale
    )
    grad_key = (
        jnp.einsum(
            "cwhqk,cwqhe->cwkhe", grad_scores, query_heads, preferred_element_type=jnp.float32
        )
        * score_scale
    )
    grad_value = jnp.einsum(
        "cwhqk,cwqhe->cwkhe", probs_low, grad_mixed_heads, preferred_element_type=jnp.float32
    )
    return (grad_query, grad_key, grad_value)


def shards(tokens, valid, w_qkv, w_out, vectors, w_up, w_down, cotangent):
    clip_count, local_rows = (tokens.shape[0], tokens.shape[1])
    local_time = local_rows // FREQ
    padded_time = local_time + 2 * SHIFT
    padded_freq = FREQ + 2 * SHIFT
    flat_rows = clip_count * local_rows
    tensor_rank = lax.axis_index("tensor")
    qkv_full, out_full, vector_full = (
        lax.all_gather(w_qkv, ("dp", "tensor"), axis=1, tiled=True),
        lax.all_gather(w_out, ("dp", "tensor"), axis=1, tiled=True),
        lax.all_gather(vectors, ("dp", "tensor"), axis=1, tiled=True),
    )
    up_part, down_part = (
        lax.all_gather(w_up, "dp", axis=0, tiled=True),
        lax.all_gather(w_down, "dp", axis=1, tiled=True),
    )
    vector_rows = vector_full.astype(jnp.float32)
    hidden_part = up_part.shape[1]
    up_bias = vector_rows[8:].reshape(-1)
    limit_rows = valid * ROW_UNIT
    own_time = tensor_rank * local_time + jnp.arange(local_time)
    keep_rows = (own_time[None, :] < limit_rows[:, None]).astype(jnp.float32)
    keep = jnp.repeat(keep_rows, FREQ, axis=1)[:, :, None]
    token_values = tokens.astype(jnp.float32)
    scaled_first, inverse_first = norm_parts(token_values)
    normed = (scaled_first * vector_rows[0] + vector_rows[1]).astype(jnp.bfloat16)
    qkv_bias = jnp.concatenate([vector_rows[2], jnp.zeros_like(vector_rows[2]), vector_rows[3]])
    projected = (jnp.dot(normed, qkv_full, preferred_element_type=jnp.float32) + qkv_bias).astype(
        jnp.bfloat16
    )
    clip_grid = projected.reshape(clip_count, local_time, FREQ, 3 * D)
    extended = extended_2(clip_grid[..., D:], (("tensor", 1),), SHIFT)
    query_grid = jnp.pad(clip_grid[..., :D], ((0, 0), (SHIFT, SHIFT), (0, 0), (0, 0)))
    query_win = split_windows(pad_columns(query_grid))
    keyval_win = split_windows(pad_columns(extended))
    window_shape = query_win.shape
    query_heads = head_split(query_win)
    key_heads = head_split(keyval_win[..., :D])
    value_heads = head_split(keyval_win[..., D:])
    key_windows = key_window_mask(limit_rows, tensor_rank * local_time, local_time)
    mixed_win, log_total, probs_low = attend_forward(
        query_heads, key_heads, value_heads, key_windows
    )
    mixed_grid = join_windows(mixed_win.reshape(window_shape), padded_time, padded_freq)
    mixed_low = (
        mixed_grid[:, SHIFT : SHIFT + local_time, SHIFT : SHIFT + FREQ]
        .reshape(clip_count, local_rows, D)
        .astype(jnp.bfloat16)
    )
    attended = jnp.dot(mixed_low, out_full, preferred_element_type=jnp.float32) + vector_rows[4]
    residual = token_values + attended
    scaled_second, inverse_second = norm_parts(residual)
    second = (scaled_second * vector_rows[5] + vector_rows[6]).astype(jnp.bfloat16)
    flat_second = second.reshape(flat_rows, D)
    grad_out = cotangent.astype(jnp.float32) * keep
    grad_branch_low = grad_out.astype(jnp.bfloat16)
    flat_grad = grad_branch_low.reshape(flat_rows, D)
    up_columns = lax.dynamic_slice_in_dim(up_bias, tensor_rank * hidden_part, hidden_part)
    row_piece = lax.all_gather(flat_second, "tensor", axis=0, tiled=True)
    pre_act = jnp.dot(row_piece, up_part, preferred_element_type=jnp.float32) + up_columns
    gathered = row_piece
    hidden_low = jax.nn.gelu(pre_act, approximate=False).astype(jnp.bfloat16)
    branch = lax.psum_scatter(
        jnp.dot(hidden_low, down_part, preferred_element_type=jnp.float32).astype(jnp.bfloat16),
        "tensor",
        scatter_dimension=0,
        tiled=True,
    ).astype(jnp.float32)
    row_piece = lax.all_gather(flat_grad, "tensor", axis=0, tiled=True)
    grad_hidden = contract_last(row_piece, down_part)
    grad_pre = (grad_hidden * gelu_slope(pre_act)).astype(jnp.bfloat16)
    down_grad = contract_rows(hidden_low, row_piece)
    up_grad = contract_rows(gathered, grad_pre)
    up_bias_grad = lax.dynamic_update_slice_in_dim(
        jnp.zeros((FF,), jnp.float32), column_sum(grad_pre), tensor_rank * hidden_part, 0
    )
    grad_second = lax.psum_scatter(
        contract_last(grad_pre, up_part).astype(jnp.bfloat16),
        "tensor",
        scatter_dimension=0,
        tiled=True,
    ).astype(jnp.float32)
    up_grad, down_grad = (
        sum_at_owner(up_grad.astype(jnp.bfloat16), "dp", 0),
        sum_at_owner(down_grad.astype(jnp.bfloat16), "dp", 1),
    )
    branch_rows = branch.reshape(clip_count, local_rows, D) + vector_rows[7]
    output = ((residual + branch_rows) * keep).astype(jnp.bfloat16)
    grad_second = grad_second.reshape(clip_count, local_rows, D)
    gain_second_grad = column_sum(grad_second * scaled_second)
    shift_second_grad = column_sum(grad_second)
    grad_resid = grad_out + norm_back(grad_second, scaled_second, inverse_second, vector_rows[5])
    grad_att_low = grad_resid.astype(jnp.bfloat16)
    out_bias_grad = column_sum(grad_att_low)
    out_grad = contract_rows(mixed_low.reshape(flat_rows, D), grad_att_low.reshape(flat_rows, D))
    grad_mixed = contract_last(grad_att_low, out_full).astype(jnp.bfloat16)
    grad_mixed_grid = jnp.pad(
        grad_mixed.reshape(clip_count, local_time, FREQ, D),
        ((0, 0), (SHIFT, SHIFT), (0, 0), (0, 0)),
    )
    grad_mixed_heads = head_split(split_windows(pad_columns(grad_mixed_grid)))
    grad_query, grad_key, grad_value = attend_backward(
        grad_mixed_heads, query_heads, key_heads, value_heads, key_windows, log_total, probs_low
    )
    grad_query_grid = join_windows(grad_query.reshape(window_shape), padded_time, padded_freq)
    grad_query_grid = grad_query_grid[:, SHIFT : SHIFT + local_time, SHIFT : SHIFT + FREQ]
    grad_keyval = jnp.concatenate(
        [grad_key.reshape(window_shape), grad_value.reshape(window_shape)], axis=-1
    )
    grad_keyval_grid = join_windows(grad_keyval, padded_time, padded_freq)[
        :, :, SHIFT : SHIFT + FREQ
    ]
    rims = jnp.concatenate(
        [grad_keyval_grid[:, :SHIFT], grad_keyval_grid[:, local_time + SHIFT :]], axis=1
    )
    arrived = extended_2(rims.astype(jnp.bfloat16), (("tensor", 1),), SHIFT).astype(rims.dtype)
    from_lower = jnp.pad(arrived[:, :SHIFT], ((0, 0), (0, local_time - SHIFT), (0, 0), (0, 0)))
    from_upper = jnp.pad(arrived[:, 3 * SHIFT :], ((0, 0), (local_time - SHIFT, 0), (0, 0), (0, 0)))
    grad_keyval_own = grad_keyval_grid[:, SHIFT : SHIFT + local_time] + from_lower + from_upper
    grad_proj = (
        jnp.concatenate([grad_query_grid, grad_keyval_own], axis=-1)
        .reshape(clip_count, local_rows, 3 * D)
        .astype(jnp.bfloat16)
    )
    proj_bias_grad = column_sum(grad_proj)
    qkv_grad = contract_rows(normed.reshape(flat_rows, D), grad_proj.reshape(flat_rows, 3 * D))
    grad_normed = contract_last(grad_proj, qkv_full)
    gain_first_grad = column_sum(grad_normed * scaled_first)
    shift_first_grad = column_sum(grad_normed)
    grad_tokens = grad_resid + norm_back(grad_normed, scaled_first, inverse_first, vector_rows[0])
    small_rows = jnp.stack(
        [
            gain_first_grad,
            shift_first_grad,
            proj_bias_grad[:D],
            proj_bias_grad[2 * D :],
            out_bias_grad,
            gain_second_grad,
            shift_second_grad,
            column_sum(grad_branch_low),
        ]
    )
    vector_grad = jnp.concatenate([small_rows, up_bias_grad.reshape(-1, D)], axis=0)
    qkv_grad, out_grad, vector_grad = (
        lax.psum_scatter(qkv_grad, ("dp", "tensor"), scatter_dimension=1, tiled=True),
        lax.psum_scatter(out_grad, ("dp", "tensor"), scatter_dimension=1, tiled=True),
        lax.psum_scatter(vector_grad, ("dp", "tensor"), scatter_dimension=1, tiled=True),
    )
    return (output, grad_tokens, qkv_grad, out_grad, vector_grad, up_grad, down_grad)


def solution(mesh):
    placed = (
        P("dp", "tensor", None),
        P("dp"),
        P(None, ("dp", "tensor")),
        P(None, ("dp", "tensor")),
        P(None, ("dp", "tensor")),
        P("dp", "tensor"),
        P("tensor", "dp"),
        P("dp", "tensor", None),
    )
    return jax.shard_map(
        shards,
        mesh=mesh,
        in_specs=placed,
        out_specs=(
            P("dp", "tensor", None),
            P("dp", "tensor", None),
            P(None, ("dp", "tensor")),
            P(None, ("dp", "tensor")),
            P(None, ("dp", "tensor")),
            P("dp", "tensor"),
            P("tensor", "dp"),
        ),
        check_vma=False,
    )
```

profile of v0, /device:TPU:0, one launch (start us, length us, event | category | flops | bytes accessed | tf_op | source)
XLA Modules:
  0.0 798.5 jit_solution(16993738019945920245)
XLA Ops:
  9.7 43.7 %all_gather.21 = bf16[12,512]{0,1:T(8,128)(2,1)S(1)} all-gather(bf16[12,16]{0,1:T(8,128)(2,1)S(1)} %copy.84), channel_id=1, replica_groups=mesh['dp'=8,'tensor'=4] {'dp','tensor'}, dimensions={1}, use_global_device_ids=true | all-gather | bytes 12672 | tf_op jit(solution)/shard_map/all_gather | solution.py:180
  57.2 11.4 %all-gather.4.cloned.1.call-done = bf16[512,1536]{0,1:T(8,128)(2,1)} async-done(((bf16[512,48]{0,1:T(8,128)(2,1)}), bf16[512,1536]{0,1:T(8,128)(2,1)}) %all-gather.4.cloned.1.call-update) | async-done | bytes 1572880 | tf_op jit(solution)/shard_map/all_gather | solution.py:178
  76.0 41.6 %all_gather.23 = bf16[512,512]{0,1:T(8,128)(2,1)S(1)} all-gather(bf16[512,16]{0,1:T(8,128)(2,1)S(1)} %copy-done.26), channel_id=1, replica_groups=mesh['dp'=8,'tensor'=4] {'dp','tensor'}, dimensions={1}, use_global_device_ids=true | all-gather | bytes 540672 | tf_op jit(solution)/shard_map/all_gather | solution.py:179
  133.8 8.1 %fusion.21 = (f32[4,15,16,16]{3,2,1,0:T(8,128)S(1)}, f32[4,15,16,16,16]{3,4,2,1,0:T(8,128)S(1)}) fusion(pred[4,15,16]{2,1,0:T(8,128)(4,1)S(1)} %copy.90, bf16[4,15,16,16,32]{4,3,0,2,1:T(8,128)(2,1)} %reshape.264, bf16[4,15,16,16,32]{4,3,2,1,0:T(8,128)(2,1)} %reshape_reshape.13), kind=kOutput, calls=%fused_computation.40 | convolution fusion | flops 16450560 | bytes 3011520 | tf_op jit(solution)/shard_map/cwqhe,cwkhe->cwhqk/dot_general | solution.py:125
  142.0 3.5 fusion.2
  147.1 4.7 convert_bitcast_fusion
  154.8 5.5 reshape_reshape.14
  165.5 31.4 %all_gather.25 = bf16[512,512]{1,0:T(8,128)(2,1)S(1)} all-gather(bf16[64,512]{1,0:T(8,128)(2,1)S(1)} %copy-done.22), channel_id=1, replica_groups=mesh['dp'=8,'tensor'=4] {'dp'}, dimensions={0}, use_global_device_ids=true | all-gather | bytes 589824 | tf_op jit(solution)/shard_map/all_gather | solution.py:183
  196.8 31.3 %all_gather.26 = bf16[512,512]{0,1:T(8,128)(2,1)S(1)} all-gather(bf16[512,64]{0,1:T(8,128)(2,1)S(1)} %copy-done.23), channel_id=1, replica_groups=mesh['dp'=8,'tensor'=4] {'dp'}, dimensions={1}, use_global_device_ids=true | all-gather | bytes 589824 | tf_op jit(solution)/shard_map/all_gather | solution.py:184
  228.1 12.8 %fusion.7 = (bf16[2048,512]{1,0:T(8,128)(2,1)}, f32[2048,512]{1,0:T(8,128)}) fusion(f32[512]{0:T(512)S(1)} %dynamic_slice.3, bf16[2048,512]{1,0:T(8,128)(2,1)} %all-gather.6.cloned.1.call-done, bf16[512,512]{1,0:T(8,128)(2,1)S(1)} %all_gather.25), kind=kOutput, calls=%fused_computation.17 | convolution fusion | flops 1142947840 | bytes 8914944 | tf_op jit(solution)/shard_map/dot_general | solution.py:229
  240.9 4.6 convert_reduce_fusion
  249.6 4.4 convolution_convert_fusion.1
  255.7 21.7 %reduce-scatter.10.cloned.1.call-done = bf16[512,512]{1,0:T(8,128)(2,1)} async-done(((bf16[2048,512]{1,0:T(8,128)(2,1)}), bf16[512,512]{1,0:T(8,128)(2,1)}) %reduce-scatter.10.cloned.1.call-update) | async-done | bytes 524304 | tf_op jit(solution)/shard_map/reduce_scatter | solution.py:246
  281.5 29.9 %reduce-scatter.8.cloned.1.call-done = bf16[512,512]{1,0:T(8,128)(2,1)} async-done(((bf16[2048,512]{1,0:T(8,128)(2,1)}), bf16[512,512]{1,0:T(8,128)(2,1)}) %reduce-scatter.8.cloned.1.call-update) | async-done | bytes 524304 | tf_op jit(solution)/shard_map/reduce_scatter | solution.py:232
  321.0 9.8 %fusion.31 = f32[4,15,16,16,16]{3,4,2,1,0:T(8,128)} fusion(bf16[4,15,16,16,32]{4,3,0,2,1:T(8,128)(2,1)} %reshape.263, bf16[4,15,16,16,32]{4,3,2,1,0:T(8,128)(2,1)} %reshape_reshape.15), kind=kOutput, calls=%fused_computation.52 | convolution fusion | flops 15728640 | bytes 2949120 | tf_op jit(solution)/shard_map/cwqhe,cwkhe->cwhqk/dot_general | solution.py:149
  330.8 7.1 fusion.43
  337.9 10.0 %copy.113 = f32[4,15,16,16,32]{4,3,2,1,0:T(8,128)} copy(f32[4,15,16,16,32]{4,2,3,1,0:T(8,128)} %fusion.43) | data formatting | bytes 3932160 | tf_op jit(solution)/shard_map/cwhqk,cwqhe->cwkhe/transpose | solution.py:164
  347.8 7.1 concatenate.29
  354.9 15.2 %select_convert_fusion = bf16[4,15,16,16,16]{3,4,2,1,0:T(8,128)(2,1)S(1)} fusion(f32[4,15,16,16,16]{3,4,2,1,0:T(8,128)} %fusion.31, f32[4,15,16,16,16]{3,4,2,1,0:T(8,128)} %copy-done.9, f32[4,15,16,16]{3,2,1,0:T(8,128)S(1)} %copy-done.21, pred[4,15,16]{2,1,0:T(8,128)(4,1)S(1)} %copy.90), kind=kOutput, calls=%fused_computation.3 | output fusion | flops 2718735 | bytes 2520000 | tf_op jit(solution)/shard_map/sub | solution.py:153
  372.3 6.7 copy.111
  379.0 7.2 concatenate.28
  389.4 3.7 copy.114
  404.1 5.5 reshape_reshape.16
  418.8 4.2 convolution_bitcast_fusion
  423.1 4.3 convolution_convert_fusion.2
  427.4 5.5 all-to-all-start.1
  432.9 4.3 convolution_convert_fusion.3
  437.2 11.9 %all-to-all-done.1 = bf16[8,512,64]{1,2,0:T(8,128)(2,1)S(1)} async-done(((bf16[8,512,64]{1,2,0:T(8,128)(2,1)}), bf16[8,512,64]{1,2,0:T(8,128)(2,1)S(1)}, u32[]{:S(2)}, u32[]{:S(2)}) %all-to-all-start.1) | async-done | bytes 524320 | tf_op jit(solution)/shard_map/all_to_all | solution.py:41
  453.4 14.6 %all-to-all-done = bf16[8,64,512]{2,1,0:T(8,128)(2,1)S(1)} async-done(((bf16[8,64,512]{2,1,0:T(8,128)(2,1)}), bf16[8,64,512]{2,1,0:T(8,128)(2,1)S(1)}, u32[]{:S(2)}, u32[]{:S(2)}) %all-to-all-start) | async-done | bytes 524320 | tf_op jit(solution)/shard_map/all_to_all | solution.py:41
  471.3 82.8 %reduce-scatter.16.cloned.1.call-done = f32[16,12]{1,0:T(8,128)} async-done(((f32[512,12]{1,0:T(8,128)}), f32[16,12]{1,0:T(8,128)}) %reduce-scatter.16.cloned.1.call-update) | async-done | bytes 784
  555.5 132.2 %reduce-scatter.14.cloned.1.call-done = f32[512,16]{0,1:T(8,128)} async-done(((f32[512,512]{0,1:T(8,128)}), f32[512,16]{0,1:T(8,128)}) %reduce-scatter.14.cloned.1.call-update) | async-done | bytes 32784 | tf_op jit(solution)/shard_map/reduce_scatter | solution.py:315
  687.7 103.5 %reduce-scatter.12.cloned.1.call-done = f32[512,48]{0,1:T(8,128)} async-done(((f32[512,1536]{0,1:T(8,128)}), f32[512,48]{0,1:T(8,128)}) %reduce-scatter.12.cloned.1.call-update) | async-done | bytes 98320 | tf_op jit(solution)/shard_map/reduce_scatter | solution.py:314
  (191 shorter events, 92.7 us)
Async XLA Ops:
  7.2 61.5 %all-gather.4.cloned.1.call-start = ((), (), s32[]{:S(2)}) async-start(), calls=%async_computation.7 | async-start | bytes 1622016 | tf_op jit(solution)/shard_map/all_gather | solution.py:178
  7.9 220.2 %all-gather.6.cloned.1.call-start = ((), (), s32[]{:S(2)}) async-start(), calls=%async_computation.8 | async-start | bytes 2621440 | tf_op jit(solution)/shard_map/all_gather | solution.py:228
  54.6 16.8 %copy-start.33 = (f32[512]{0:T(512)}, f32[512]{0:T(512)S(1)}, u32[]{:S(2)}) copy-start(f32[512]{0:T(512)S(1)} %get-tuple-element.22) | copy-start | bytes 6148
  54.6 16.8 %copy-start.36 = (f32[512]{0:T(512)}, f32[512]{0:T(512)S(1)}, u32[]{:S(2)}) copy-start(f32[512]{0:T(512)S(1)} %get-tuple-element.21) | copy-start | bytes 6148
  55.8 15.8 %copy-start.24 = (f32[4,128]{1,0:T(4,128)}, f32[4,128]{1,0:T(4,128)S(1)}, u32[]{:S(2)}) copy-start(f32[4,128]{1,0:T(4,128)S(1)} %broadcast_multiply_fusion.4) | copy-start | bytes 6148
  55.9 20.1 %copy-start.26 = (bf16[512,16]{0,1:T(8,128)(2,1)S(1)}, bf16[512,16]{0,1:T(8,128)(2,1)}, u32[]{:S(2)}) copy-start(bf16[512,16]{0,1:T(8,128)(2,1)} %param.11) | copy-start | bytes 49156
  57.2 60.4 %copy-start.30 = (f32[4,128]{1,0:T(4,128)}, f32[4,128]{1,0:T(4,128)S(1)}, u32[]{:S(2)}) copy-start(f32[4,128]{1,0:T(4,128)S(1)} %add_rsqrt_fusion.1) | copy-start | bytes 6148
  71.6 52.0 %collective-permute-start.1 = (bf16[4,2,8,1024]{3,0,2,1:T(4,128)(2,1)S(1)}, bf16[4,2,8,1024]{3,0,2,1:T(4,128)(2,1)S(1)}, u32[]{:S(2)}, u32[]{:S(2)}) collective-permute-start(bf16[4,2,8,1024]{3,0,2,1:T(4,128)(2,1)S(1)} %copy.130), channel_id=1, source_target_pairs={{1,0},{2,1},{3,2},{5,4},{6,5},{7,6},{9,8},{10,9},{11,10},{13,12},{... | collective-permute-start | bytes 393224 | tf_op jit(solution)/shard_map/ppermute | solution.py:29
  72.9 50.7 %collective-permute-start = (bf16[4,2,8,1024]{3,0,2,1:T(4,128)(2,1)S(1)}, bf16[4,2,8,1024]{3,0,2,1:T(4,128)(2,1)S(1)}, u32[]{:S(2)}, u32[]{:S(2)}) collective-permute-start(bf16[4,2,8,1024]{3,0,2,1:T(4,128)(2,1)S(1)} %copy.128), channel_id=1, source_target_pairs={{0,1},{1,2},{2,3},{4,5},{5,6},{6,7},{8,9},{9,10},{10,11},{12,13},{... | collective-permute-start | bytes 393224 | tf_op jit(solution)/shard_map/ppermute | solution.py:26
  117.6 44.2 %copy-start.10 = (bf16[512,512]{0,1:T(8,128)(2,1)}, bf16[512,512]{0,1:T(8,128)(2,1)S(1)}, u32[]{:S(2)}) copy-start(bf16[512,512]{0,1:T(8,128)(2,1)S(1)} %all_gather.23) | copy-start | bytes 1572868
  142.0 5.1 copy-start.4
  147.1 4.7 copy-start.16
  154.8 7.1 copy-start.8
  161.9 35.0 %copy-start.23 = (bf16[512,64]{0,1:T(8,128)(2,1)S(1)}, bf16[512,64]{0,1:T(8,128)(2,1)}, u32[]{:S(2)}) copy-start(bf16[512,64]{0,1:T(8,128)(2,1)} %param.14) | copy-start | bytes 196612
  163.8 77.1 %all-gather.8.cloned.1.call-start = ((), (), s32[]{:S(2)}) async-start(), calls=%async_computation.10 | async-start | bytes 2621440 | tf_op jit(solution)/shard_map/all_gather | solution.py:238
  165.1 112.3 %reduce-scatter.10.cloned.1.call-start = ((), (), s32[]{:S(2)}) async-start(), calls=%async_computation.11 | async-start | bytes 2621440 | tf_op jit(solution)/shard_map/reduce_scatter | solution.py:246
  228.1 12.8 %copy-start.20 = (bf16[512,512]{0,1:T(8,128)(2,1)}, bf16[512,512]{0,1:T(8,128)(2,1)S(1)}, u32[]{:S(2)}) copy-start(bf16[512,512]{0,1:T(8,128)(2,1)S(1)} %all_gather.26) | copy-start | bytes 1572868
  249.5 61.9 %reduce-scatter.8.cloned.1.call-start = ((), (), s32[]{:S(2)}) async-start(), calls=%async_computation.9 | async-start | bytes 2621440 | tf_op jit(solution)/shard_map/reduce_scatter | solution.py:232
  254.0 300.1 %reduce-scatter.16.cloned.1.call-start = ((), (), s32[]{:S(2)}) async-start(), calls=%async_computation.14 | async-start | bytes 270336
  321.0 9.8 %copy-start.7 = (bf16[4,15,16,16,32]{4,3,2,1,0:T(8,128)(2,1)S(1)}, bf16[4,15,16,16,32]{4,3,2,1,0:T(8,128)(2,1)}, u32[]{:S(2)}) copy-start(bf16[4,15,16,16,32]{4,3,2,1,0:T(8,128)(2,1)} %reshape_reshape.15) | copy-start | bytes 2949124
  321.0 9.8 %copy-start.15 = (f32[4,15,16,16]{3,2,1,0:T(8,128)S(1)}, f32[4,15,16,16]{3,2,1,0:T(8,128)}, u32[]{:S(2)}) copy-start(f32[4,15,16,16]{3,2,1,0:T(8,128)} %copy-done.13) | copy-start | bytes 184324
  321.0 9.8 %copy-start.18 = (f32[4,15,16,16]{3,2,1,0:T(8,128)S(1)}, f32[4,15,16,16]{3,2,1,0:T(8,128)}, u32[]{:S(2)}) copy-start(f32[4,15,16,16]{3,2,1,0:T(8,128)} %copy-done.16) | copy-start | bytes 184324
  347.8 7.1 copy-start.21
  354.9 15.2 %copy-start.3 = (bf16[4,15,16,16,32]{4,3,2,1,0:T(8,128)(2,1)S(1)}, bf16[4,15,16,16,32]{4,3,2,1,0:T(8,128)(2,1)}, u32[]{:S(2)}) copy-start(bf16[4,15,16,16,32]{4,3,2,1,0:T(8,128)(2,1)} %reshape_reshape.13) | copy-start | bytes 2949124
  389.4 8.4 %copy-start.6 = (bf16[4,15,16,16,16]{3,4,2,1,0:T(8,128)(2,1)S(1)}, bf16[4,15,16,16,16]{3,4,2,1,0:T(8,128)(2,1)}, u32[]{:S(2)}) copy-start(bf16[4,15,16,16,16]{3,4,2,1,0:T(8,128)(2,1)} %copy-done.5) | copy-start | bytes 1474564
  393.1 8.0 %copy-start = (f32[4,5,4,3,4,1024]{5,0,4,3,2,1:T(4,128)}, f32[4,5,4,3,4,1024]{5,0,4,3,2,1:T(4,128)S(1)}, u32[]{:S(2)}) copy-start(f32[4,5,4,3,4,1024]{5,0,4,3,2,1:T(4,128)S(1)} %copy.114) | copy-start | bytes 11796484
  394.3 16.8 %collective-permute-start.2 = (bf16[4,2,8,1024]{3,0,2,1:T(4,128)(2,1)S(1)}, bf16[4,2,8,1024]{3,0,2,1:T(4,128)(2,1)S(1)}, u32[]{:S(2)}, u32[]{:S(2)}) collective-permute-start(bf16[4,2,8,1024]{3,0,2,1:T(4,128)(2,1)S(1)} %get-tuple-element.29), channel_id=1, source_target_pairs={{0,1},{1,2},{2,3},{4,5},{5,6},{6,7},{8,9},{9,10},{10,11},{12,13},{... | collective-permute-start | bytes 393224 | tf_op jit(solution)/shard_map/ppermute | solution.py:26
  396.4 14.7 %collective-permute-start.3 = (bf16[4,2,8,1024]{3,0,2,1:T(4,128)(2,1)S(1)}, bf16[4,2,8,1024]{3,0,2,1:T(4,128)(2,1)}, u32[]{:S(2)}, u32[]{:S(2)}) collective-permute-start(bf16[4,2,8,1024]{3,0,2,1:T(4,128)(2,1)S(1)} %get-tuple-element.30), channel_id=1, source_target_pairs={{1,0},{2,1},{3,2},{5,4},{6,5},{7,6},{9,8},{10,9},{11,10},{13,12},{... | collective-permute-start | bytes 393224 | tf_op jit(solution)/shard_map/ppermute | solution.py:29
  417.2 270.6 %reduce-scatter.14.cloned.1.call-start = ((), (), s32[]{:S(2)}) async-start(), calls=%async_computation.13 | async-start | bytes 1081344 | tf_op jit(solution)/shard_map/reduce_scatter | solution.py:315
  418.8 372.4 %reduce-scatter.12.cloned.1.call-start = ((), (), s32[]{:S(2)}) async-start(), calls=%async_computation.12 | async-start | bytes 3244032 | tf_op jit(solution)/shard_map/reduce_scatter | solution.py:314
  427.4 21.7 %all-to-all-start.1 = ((bf16[8,512,64]{1,2,0:T(8,128)(2,1)}), bf16[8,512,64]{1,2,0:T(8,128)(2,1)S(1)}, u32[]{:S(2)}, u32[]{:S(2)}) async-start(bf16[8,512,64]{1,2,0:T(8,128)(2,1)} %bitcast.41), calls=%async_computation.5 | async-start | bytes 1048576 | tf_op jit(solution)/shard_map/all_to_all | solution.py:41
  449.1 18.8 %all-to-all-start = ((bf16[8,64,512]{2,1,0:T(8,128)(2,1)}), bf16[8,64,512]{2,1,0:T(8,128)(2,1)S(1)}, u32[]{:S(2)}, u32[]{:S(2)}) async-start(bf16[8,64,512]{2,1,0:T(8,128)(2,1)} %bitcast.39), calls=%async_computation.4 | async-start | bytes 1048576 | tf_op jit(solution)/shard_map/all_to_all | solution.py:41
  (21 other events, 62.5 us)
Sparse Core Ops, SparseCore 0:
  10.9 57.7 all-gather.3
  163.9 18.6 all-gather.5
  184.8 22.5 all-gather.7
  249.7 27.7 reduce-scatter.9
  279.9 31.3 reduce-scatter.7
  417.3 136.7 reduce-scatter.15
  557.0 130.6 reduce-scatter.13
  693.7 97.4 reduce-scatter.11
where the time goes:
time: 805 us; the launch traced here: 799 us
  waiting for transfers between devices  409 us (51%)
  blocking collectives  148 us (18%)
  local copies, waits for them, and re-layouts  83.3 us (10%)
  matrix products  80.9 us (10%)
  other arithmetic  44.9 us (6%)
  starting transfers between devices  17.1 us (2%)
  between operations  15.5 us (2%)
    reduce_scatter x1, waiting for transfers between devices, shards(): lax.psum_scatter(out_grad, ('dp', 'tensor'), scatter_dimension=1, tiled=T...  132 us
    reduce_scatter x1, waiting for transfers between devices, shards(): lax.psum_scatter(qkv_grad, ('dp', 'tensor'), scatter_dimension=1, tiled=T...  103 us
    unnamed x9, waiting for transfers between devices  83.6 us
    all_gather x1, blocking collectives, shards(): lax.all_gather(vectors, ('dp', 'tensor'), axis=1, tiled=True)  43.7 us
    all_gather x1, blocking collectives, shards(): lax.all_gather(w_out, ('dp', 'tensor'), axis=1, tiled=True)  41.6 us
    all_gather x1, blocking collectives, shards(): lax.all_gather(w_up, 'dp', axis=0, tiled=True)  31.4 us
    all_gather x1, blocking collectives, shards(): lax.all_gather(w_down, 'dp', axis=1, tiled=True)  31.3 us
    reduce_scatter x1, waiting for transfers between devices, shards(): lax.psum_scatter(jnp.dot(hidden_low, down_part, preferred_element_type=jn...  29.9 us
  transfers between devices with their start and end apart: 14, of which 8 were waited for; matrix products, arithmetic and copies ran while one was open for 9% of the time, Pallas kernels for 0%

commit v1 on v0

v1 whole, which is shorter than its diff:
```python
import functools

import jax
import jax.numpy as jnp
from jax import lax
from jax.experimental import pallas as pl
from jax.experimental.pallas import tpu as pltpu
from jax.sharding import PartitionSpec as P

D = 512
FF = 2048
HEADS = 16
HEAD = D // HEADS
FREQ = 8
WINDOW = 4
SHIFT = 2
ROW_UNIT = 8

EPS = 1e-06
MASKED = -1000000000.0
SCALE = HEAD ** (-0.5)
INV_ROOT_TWO = 0.7071067811865476
INV_ROOT_TAU = 0.3989422804014327

BOTH = ("dp", "tensor")
SLOTS = 32
NEAR = SLOTS // 2
PIECE = 4
QKV_ROWS = 3 * D // SLOTS
OUT_ROWS = D // SLOTS
A_ROWS = QKV_ROWS + OUT_ROWS
CHUNKS = FF // D
UP_ROWS = D * CHUNKS // SLOTS
B_ROWS = OUT_ROWS + UP_ROWS

CLIPS = 4
OWN = 128
EDGE = 16
OWN_ALL = CLIPS * OWN
ROWS = OWN_ALL + CLIPS * 2 * EDGE
BAND = 2 * EDGE
BANDS = OWN // BAND + 1
HALF = D // 2
HALF_HEADS = HALF // HEAD
STEP = 128
SUB = 32

bf16 = jnp.bfloat16
f32 = jnp.float32


def nn(a, b):
    return lax.dot_general(a, b, (((1,), (0,)), ((), ())), preferred_element_type=f32)


def nt(a, b):
    return lax.dot_general(a, b, (((1,), (1,)), ((), ())), preferred_element_type=f32)


def tn(a, b):
    return lax.dot_general(a, b, (((0,), (0,)), ((), ())), preferred_element_type=f32)


def rows_at(start, size):
    return pl.ds(pl.multiple_of(start, size), size)


def norm_parts(values):
    mean = jnp.mean(values, axis=-1, keepdims=True)
    centred = values - mean
    variance = jnp.mean(centred * centred, axis=-1, keepdims=True)
    inverse = lax.rsqrt(variance + EPS)
    return centred * inverse, inverse


def norm_back(grad, scaled, inverse, gain):
    grad_hat = grad * gain
    centre = jnp.mean(grad_hat, axis=-1, keepdims=True)
    slope = jnp.mean(grad_hat * scaled, axis=-1, keepdims=True)
    return inverse * (grad_hat - centre - scaled * slope)


def band_rows(band):
    clip = band // BANDS
    place = band % BANDS
    first = jnp.where(place == 0, OWN_ALL + clip * BAND, clip * OWN + place * BAND - EDGE)
    last = jnp.where(place == BANDS - 1, OWN_ALL + clip * BAND + EDGE, clip * OWN + place * BAND)
    return rows_at(first, EDGE), rows_at(last, EDGE)


def load_band(ref, places, columns):
    return jnp.concatenate([ref[places[0], columns], ref[places[1], columns]], axis=0)


def find(pieces, slot):
    size = pieces[0].shape[0]
    return pieces[slot // size], slot % size


def weight_block(owner):
    return rows_at(owner // CHUNKS * UP_ROWS, UP_ROWS), rows_at(owner % CHUNKS * D, D)


def pack_kernel(qkv_ref, vec_ref, out_ref, up_ref, block_ref):
    block_ref[:QKV_ROWS, :] = qkv_ref[...]
    block_ref[QKV_ROWS:A_ROWS, :] = jnp.zeros((OUT_ROWS, D), bf16)
    block_ref[QKV_ROWS:A_ROWS, : vec_ref.shape[1]] = vec_ref[...]
    block_ref[A_ROWS : A_ROWS + OUT_ROWS, :] = out_ref[...]
    block_ref[A_ROWS + OUT_ROWS :, :] = up_ref[...]


def head_lanes():
    row = lax.broadcasted_iota(jnp.int32, (HALF, HALF), 0) // HEAD
    lane = lax.broadcasted_iota(jnp.int32, (HALF, HALF), 1) // HEAD
    return jnp.where(row == lane, 1.0, 0.0)


def by_head(rows, lanes):
    return jnp.concatenate([rows] * HALF_HEADS, axis=0) * lanes


def flip_heads(wide):
    turned = wide.T
    return jnp.concatenate([turned[head * BAND : (head + 1) * BAND] for head in range(HALF_HEADS)], axis=1)


def attend_kernel(
    own_ref, keep_ref, x_ref, *refs,
):
    a_refs, refs = refs[:-10], refs[-10:]
    proj_ref, prob_ref, mixed_ref, scaled_ref, wqkv_ref, vec_ref, column_vec, lanes_ref, pair_ref, normed_ref = refs
    for slot in range(SLOTS):
        owner = own_ref[slot]
        a_ref, held = find(a_refs, slot)
        wqkv_ref[rows_at(owner * QKV_ROWS, QKV_ROWS), :] = a_ref[held, :QKV_ROWS, :]
        column_vec[rows_at(owner * OUT_ROWS, OUT_ROWS), :] = a_ref[held, QKV_ROWS:A_ROWS, :128].astype(f32)
    vec_ref[...] = column_vec[...].T[:16, :]
    lanes_ref[...] = head_lanes().astype(bf16)
    key_group = (lax.broadcasted_iota(jnp.int32, (BAND, HALF), 0) % FREQ + SHIFT) // WINDOW
    query_group = (lax.broadcasted_iota(jnp.int32, (BAND, HALF), 1) % FREQ + SHIFT) // WINDOW
    pair_ref[...] = jnp.where(key_group == query_group, 1.0, 0.0)

    def scale(step, carry):
        here = rows_at(step * SUB, SUB)
        scaled, _ = norm_parts(x_ref[here, :].astype(f32))
        scaled_ref[here, :] = scaled.astype(bf16)
        normed_ref[here, :] = (scaled * vec_ref[0:1, :] + vec_ref[1:2, :]).astype(bf16)
        return carry

    lax.fori_loop(0, ROWS // SUB, scale, 0, unroll=4)
    for part in range(3):
        columns = slice(part * D, (part + 1) * D)
        part_out = nt(normed_ref[...], wqkv_ref[columns, :])
        if part != 1:
            bias = 2 if part == 0 else 3
            part_out = part_out + vec_ref[bias : bias + 1, :]
        proj_ref[:, columns] = part_out.astype(bf16)

    def score(band, carry):
        places = band_rows(band)
        key_ok = load_band(keep_ref, places, slice(None))
        key_ok = jnp.concatenate([key_ok, key_ok], axis=1) * pair_ref[...] > 0.5
        for half in range(2):
            low = half * HALF
            query = load_band(proj_ref, places, slice(low, low + HALF))
            key = load_band(proj_ref, places, slice(D + low, D + low + HALF))
            scores = nt(key, by_head(query, lanes_ref[...])) * SCALE
            scores = jnp.where(key_ok, scores, MASKED)
            exponent = jnp.exp(scores - jnp.max(scores, axis=0, keepdims=True))
            prob_ref[band, half] = exponent / jnp.sum(exponent, axis=0, keepdims=True)
        return carry

    lax.fori_loop(0, CLIPS * BANDS, score, 0, unroll=10)

    def mix(band, carry):
        places = band_rows(band)
        for half in range(2):
            low = half * HALF
            value = load_band(proj_ref, places, slice(2 * D + low, 2 * D + low + HALF))
            probs = flip_heads(prob_ref[band, half].astype(bf16))
            mixed = nn(probs, by_head(value, lanes_ref[...])).astype(bf16)
            mixed_ref[places[0], low : low + HALF] = mixed[:EDGE]
            mixed_ref[places[1], low : low + HALF] = mixed[EDGE:]
        return carry

    lax.fori_loop(0, CLIPS * BANDS, mix, 0, unroll=10)


def together(*works):
    for _ in range(4):
        for work in works:
            next(work)


def write_grads(own_ref, pieces, block_ref):
    for slot in range(SLOTS):
        grads_ref, held = find(pieces, slot)
        grads_ref[held] = block_ref[weight_block(own_ref[slot])]


def up_kernel(
    own_ref, own_down_ref, keep_ref, cot_ref, x_ref, mixed_ref, vec_ref, *refs,
):
    b_refs, refs = refs[:-14], refs[-14:]
    (
        kept_ref, sent_ref, resid_ref, hid_ref, slope_ref, second_ref, branch_low, up_ref, wout_ref,
        gdown_ref, pre_ref, branch_t, attended_ref, normed_ref,
    ) = refs
    for slot in range(SLOTS):
        owner = own_ref[slot]
        b_ref, held = find(b_refs, slot)
        low = b_ref.shape[1] - B_ROWS
        wout_ref[rows_at(owner * OUT_ROWS, OUT_ROWS), :] = b_ref[held, low : low + OUT_ROWS, :]
        up_ref[weight_block(owner)] = b_ref[held, low + OUT_ROWS :, :]

    attended_ref[...] = nt(mixed_ref[...], wout_ref[...])

    def begin(step, carry):
        here = rows_at(step * SUB, SUB)
        residual = x_ref[here, :].astype(f32) + (attended_ref[here, :] + vec_ref[4:5, :])
        resid_ref[here, :] = residual
        scaled, _ = norm_parts(residual)
        second = (scaled * vec_ref[5:6, :] + vec_ref[6:7, :]).astype(bf16)
        second_ref[here, :] = second
        normed_ref[here, :] = second
        wide = jnp.concatenate([keep_ref[here, :]] * (D // 128), axis=1)
        branch_low[here, :] = (cot_ref[here, :].astype(f32) * wide).astype(bf16)
        return carry

    lax.fori_loop(0, ROWS // SUB, begin, 0, unroll=4)
    branch_t[...] = branch_low[:OWN_ALL, :].T

    def products(chunk):
        for quarter in range(4):
            columns = slice(chunk * D + quarter * 128, chunk * D + (quarter + 1) * 128)
            pre_ref[:, columns] = nn(normed_ref[...], up_ref[:, columns])
            yield

    def slopes(chunk):
        columns = slice(chunk * D, (chunk + 1) * D)
        for step in range(ROWS // 16):
            here = slice(step * 16, step * 16 + 16)
            pre = pre_ref[here, columns] + vec_ref[8 + chunk : 9 + chunk, :]
            phi = 0.5 + 0.5 * lax.erf(pre * INV_ROOT_TWO)
            slope_ref[here, columns] = (phi + pre * (jnp.exp(-0.5 * pre * pre) * INV_ROOT_TAU)).astype(bf16)
            hid_ref[here, columns] = (pre * phi).astype(bf16)
            if step % 10 == 9:
                yield

    def weights(chunk):
        for half in range(2):
            columns = slice(chunk * D + half * HALF, chunk * D + (half + 1) * HALF)
            gdown_ref[:, columns] = nn(branch_t[...], hid_ref[:OWN_ALL, columns]).astype(bf16)
            yield
            yield

    together(products(0))
    together(products(1), slopes(0))
    for chunk in range(2, CHUNKS):
        together(products(chunk), slopes(chunk - 1), weights(chunk - 2))
    together(slopes(CHUNKS - 1), weights(CHUNKS - 2))
    together(weights(CHUNKS - 1))
    write_grads(own_down_ref, (kept_ref, sent_ref), gdown_ref)


def down_kernel(
    own_ref, own_down_ref, hid_ref, slope_ref, second_ref, branch_low, up_ref, *refs,
):
    c_refs, refs = refs[:-10], refs[-10:]
    (
        kept_ref, sent_ref, branch_ref, gsec_ref, colsum_ref,
        down_ref, gup_ref, ghid_ref, gpre_ref, second_t,
    ) = refs
    for slot in range(SLOTS):
        c_ref, held = find(c_refs, slot)
        down_ref[weight_block(own_down_ref[slot])] = c_ref[held]
    second_t[:D, :] = second_ref[:OWN_ALL, :].T
    second_t[D:, :] = jnp.ones((16, OWN_ALL), bf16)

    def products(chunk):
        for half in range(2):
            columns = slice(chunk * D + half * HALF, chunk * D + (half + 1) * HALF)
            ghid_ref[:, columns] = nn(branch_low[...], down_ref[:, columns])
            yield
            yield

    def slopes(chunk):
        columns = slice(chunk * D, (chunk + 1) * D)
        for step in range(ROWS // 16):
            here = slice(step * 16, step * 16 + 16)
            gpre_ref[here, columns] = (ghid_ref[here, columns] * slope_ref[here, columns].astype(f32)).astype(bf16)
            if step % 10 == 9:
                yield

    def weights(chunk):
        for half in range(2):
            columns = slice(chunk * D + half * HALF, chunk * D + (half + 1) * HALF)
            gup = nn(second_t[...], gpre_ref[:OWN_ALL, columns])
            gup_ref[:, columns] = gup[:D].astype(bf16)
            colsum_ref[chunk : chunk + 1, half * HALF : (half + 1) * HALF] = gup[D : D + 1]
            yield
            yield

    together(products(0))
    together(products(1), slopes(0))
    for chunk in range(2, CHUNKS):
        together(products(chunk), slopes(chunk - 1), weights(chunk - 2))
    together(slopes(CHUNKS - 1), weights(CHUNKS - 2))
    together(weights(CHUNKS - 1))
    branch_ref[...] = nt(hid_ref[:OWN_ALL, :], down_ref[...])
    gsec_ref[...] = nt(gpre_ref[...], up_ref[...])
    write_grads(own_ref, (kept_ref, sent_ref), gup_ref)


def finish_kernel(
    own_ref, keep_ref, cot_ref, mixed_ref, resid_ref, branch_ref, gsec_ref, wout_ref, vec_ref,
    out_ref, gres_ref, kept_ref, sent_ref, gmix_ref, sums_ref,
    gatt_ref, gout_ref,
):
    def rows(step, totals):
        here = rows_at(step * SUB, SUB)
        own = jnp.where(step < OWN_ALL // SUB, 1.0, 0.0)
        wide = jnp.concatenate([keep_ref[here, :]] * (D // 128), axis=1)
        scaled, inverse = norm_parts(resid_ref[here, :])
        grad_out = cot_ref[here, :].astype(f32) * wide
        gsec = gsec_ref[here, :]
        gres = grad_out + norm_back(gsec, scaled, inverse, vec_ref[5:6, :])
        gres_ref[here, :] = gres
        gatt = gres.astype(bf16)
        gatt_ref[here, :] = gatt
        parts = (gatt.astype(f32), gsec * scaled, gsec, grad_out.astype(bf16).astype(f32))
        return tuple(t + own * p.reshape(SUB // 8, 8, D).sum(axis=0) for t, p in zip(totals, parts))

    totals = lax.fori_loop(0, ROWS // SUB, rows, (jnp.zeros((8, D), f32),) * 4, unroll=4)
    for place, total in enumerate(totals):
        sums_ref[place : place + 1, :] = jnp.sum(total, axis=0, keepdims=True)
    gmix_ref[...] = nn(gatt_ref[...], wout_ref[...]).astype(bf16)
    gout_ref[...] = nn(gatt_ref[:OWN_ALL, :].T, mixed_ref[:OWN_ALL, :]).astype(bf16)
    for slot in range(SLOTS):
        grads_ref, held = find((kept_ref, sent_ref), slot)
        grads_ref[held] = gout_ref[rows_at(own_ref[slot] * OUT_ROWS, OUT_ROWS), :]

    def outputs(step, carry):
        here = rows_at(step * SUB, SUB)
        wide = jnp.concatenate([keep_ref[here, :]] * (D // 128), axis=1)
        out_ref[here, :] = (wide * (resid_ref[here, :] + (branch_ref[here, :] + vec_ref[7:8, :]))).astype(bf16)
        return carry

    lax.fori_loop(0, OWN_ALL // SUB, outputs, 0, unroll=4)


def back_kernel(
    own_ref, gmix_ref, proj_ref, prob_ref, scaled_ref, wqkv_ref, vec_ref, sums_ref, colsum_ref,
    gproj_ref, kept_ref, sent_ref,
    lanes_ref, gscore_ref, gqkv_ref, gvec_ref, column_vec,
):
    lanes_ref[...] = head_lanes().astype(bf16)

    def score(band, carry):
        places = band_rows(band)
        for half in range(2):
            low = half * HALF
            value = load_band(proj_ref, places, slice(2 * D + low, 2 * D + low + HALF))
            grad = load_band(gmix_ref, places, slice(low, low + HALF))
            probs = prob_ref[band, half]
            grad_probs = nt(value, by_head(grad, lanes_ref[...]))
            row_dot = jnp.sum(probs * grad_probs, axis=0, keepdims=True)
            gscore_ref[band, half] = (probs * (grad_probs - row_dot)).astype(bf16)
        return carry

    lax.fori_loop(0, CLIPS * BANDS, score, 0, unroll=10)

    def mix(band, carry):
        places = band_rows(band)
        for half in range(2):
            low = half * HALF
            query = load_band(proj_ref, places, slice(low, low + HALF))
            key = load_band(proj_ref, places, slice(D + low, D + low + HALF))
            grad = load_band(gmix_ref, places, slice(low, low + HALF))
            grad_scores = gscore_ref[band, half]
            grad_key = nn(grad_scores, by_head(query, lanes_ref[...])) * SCALE
            grad_value = nn(prob_ref[band, half].astype(bf16), by_head(grad, lanes_ref[...]))
            grad_query = nn(flip_heads(grad_scores), by_head(key, lanes_ref[...])) * SCALE
            for part, values in enumerate((grad_query, grad_key, grad_value)):
                values = values.astype(bf16)
                gproj_ref[places[0], part * D + low : part * D + low + HALF] = values[:EDGE]
                gproj_ref[places[1], part * D + low : part * D + low + HALF] = values[EDGE:]
        return carry

    lax.fori_loop(0, CLIPS * BANDS, mix, 0, unroll=10)

    def add_rows(step, totals):
        here = rows_at(step * SUB, SUB)
        return totals + gproj_ref[here, :].astype(f32).reshape(SUB // 8, 8, 3 * D).sum(axis=0)

    totals = lax.fori_loop(0, OWN_ALL // SUB, add_rows, jnp.zeros((8, 3 * D), f32))
    totals = jnp.sum(totals, axis=0, keepdims=True)
    gvec_ref[...] = jnp.zeros_like(gvec_ref)
    gain_grad = jnp.zeros((8, D), f32)
    shift_grad = jnp.zeros((1, D), f32)
    for part in range(3):
        gproj_t = gproj_ref[:OWN_ALL, part * D : (part + 1) * D].T
        product = nn(gproj_t, scaled_ref[:OWN_ALL, :])
        total = totals[:, part * D : (part + 1) * D]
        weight = wqkv_ref[part * D : (part + 1) * D, :]
        both = product * weight.astype(f32)
        gain_grad = gain_grad + both.reshape(D // 8, 8, D).sum(axis=0)
        high = total.astype(bf16)
        rest = (total - high.astype(f32)).astype(bf16)
        shift_grad = shift_grad + nn(high, weight) + nn(rest, weight)
        column = jnp.broadcast_to(total, (8, D)).T[:, 0:1]
        gqkv = product * vec_ref[0:1, :] + column * vec_ref[1:2, :]
        gqkv_ref[part * D : (part + 1) * D, :] = gqkv.astype(bf16)
    gvec_ref[0:1, :] = jnp.sum(gain_grad, axis=0, keepdims=True)
    gvec_ref[1:2, :] = shift_grad
    gvec_ref[2:3, :] = totals[:, :D]
    gvec_ref[3:4, :] = totals[:, 2 * D :]
    gvec_ref[4:8, :] = sums_ref[0:4, :]
    gvec_ref[8:12, :] = colsum_ref[0:4, :]
    column_vec[...] = gvec_ref[...].T.astype(bf16)
    for slot in range(SLOTS):
        owner = own_ref[slot]
        grads_ref, held = find((kept_ref, sent_ref), slot)
        grads_ref[held, :QKV_ROWS, :] = gqkv_ref[rows_at(owner * QKV_ROWS, QKV_ROWS), :]
        grads_ref[held, QKV_ROWS:, :128] = column_vec[rows_at(owner * OUT_ROWS, OUT_ROWS), :]
        grads_ref[held, QKV_ROWS:, 128:] = jnp.zeros((OUT_ROWS, D - 128), bf16)


def token_kernel( gproj_ref, x_ref, gres_ref, wqkv_ref, vec_ref, gtok_ref):
    def rows(step, carry):
        here = rows_at(step * STEP, STEP)
        gnormed = nn(gproj_ref[here, :D], wqkv_ref[:D, :])
        for part in range(1, 3):
            gnormed += nn(gproj_ref[here, part * D : (part + 1) * D], wqkv_ref[part * D : (part + 1) * D, :])
        scaled, inverse = norm_parts(x_ref[here, :].astype(f32))
        gtok_ref[here, :] = gres_ref[here, :] + norm_back(gnormed, scaled, inverse, vec_ref[0:1, :])
        return carry

    lax.fori_loop(0, OWN_ALL // STEP, rows, 0)


def call(kernel, args, outs, scratch, micros, mib):
    smem, vmem = pl.BlockSpec(memory_space=pltpu.SMEM), pl.BlockSpec(memory_space=pltpu.VMEM)
    return pl.pallas_call(
        kernel,
        out_shape=[jax.ShapeDtypeStruct(s, t) for s, t in outs],
        in_specs=[smem if a.dtype == jnp.int32 else vmem for a in args],
        out_specs=[vmem] * len(outs),
        scratch_shapes=[pltpu.VMEM(s, t) for s, t in scratch],
        compiler_params=pltpu.CompilerParams(vmem_limit_bytes=mib * 1024 * 1024),
        cost_estimate=pl.CostEstimate(flops=int(micros * 1.1e9), bytes_accessed=2**20, transcendentals=0),
    )(*args)


def swap(array, mask, other=None):
    count = lax.axis_size("dp") * lax.axis_size("tensor")
    masks = (mask, mask if other is None else other)
    return lax.ppermute(array, BOTH, [(device, device ^ masks[device % 2]) for device in range(count)])


ALONG_Z, ALONG_Y, ALONG_X, CORES = (8, 16, 24), 2, 4, 1
ALONG_XY = (ALONG_Y, ALONG_X, ALONG_Y ^ ALONG_X)


def owners(device, swapped, line_first=True):
    def one(second_core):
        first = ALONG_X if second_core and swapped else ALONG_Y
        plane = [0, first, first ^ ALONG_XY[2], ALONG_XY[2]]
        if line_first:
            return [m ^ o for o in plane for m in (0, *ALONG_Z)]
        line = [0, ALONG_Z[second_core], ALONG_Z[1 - second_core], ALONG_Z[2]]
        return [m ^ o for o in line for m in plane]

    core = device % 2
    first = jnp.where(core == 0, jnp.array(one(0)), jnp.array(one(1)))
    second = jnp.where(core == 0, jnp.array(one(1)), jnp.array(one(0))) ^ CORES
    return (device ^ jnp.concatenate([first, second])).astype(jnp.int32)


def gather(held, phase):
    return [held] + [swap(held, mask) for mask in phase]


def both_cores(pieces):
    return pieces + [swap(piece, CORES) for piece in pieces]


def wide(array):
    return array.astype(f32)


def scatter_sum(pieces, phase):
    total = pieces[0]
    for piece, mask in zip(pieces[1:], phase):
        total = total + wide(swap(piece.astype(bf16), mask))
    return total


def singles(piece):
    return [piece[i : i + 1] for i in range(PIECE)]


def after(array, *others):
    return lax.optimization_barrier((array,) + others)[0]


def neighbours(array, axis_name, width):
    count = lax.axis_size(axis_name)
    up = [(i, i + 1) for i in range(count - 1)]
    low = lax.ppermute(array[..., -width:, :], axis_name, up)
    high = lax.ppermute(array[..., :width, :], axis_name, [(b, a) for a, b in up])
    return low, high


def shards(tokens, valid, w_qkv, w_out, vectors, w_up, w_down, cotangent):
    devices_dp, devices_t = lax.axis_size("dp"), lax.axis_size("tensor")
    near = devices_dp == 8 and devices_t == 4
    rank = lax.axis_index("tensor")

    own_time = jnp.broadcast_to((jnp.arange(OWN) // FREQ)[None], (CLIPS, OWN)).reshape(-1)
    edge_time = jnp.arange(BAND) // FREQ + jnp.where(jnp.arange(BAND) < EDGE, -SHIFT, OWN // FREQ - SHIFT)
    edge_time = jnp.broadcast_to(edge_time[None], (CLIPS, BAND)).reshape(-1)
    time = jnp.concatenate([own_time, edge_time]) + rank * (OWN // FREQ)
    limit = valid * ROW_UNIT
    limit = jnp.concatenate([jnp.repeat(limit, OWN), jnp.repeat(limit, BAND)])
    keep = jnp.where((time >= 0) & (time < limit), 1.0, 0.0).astype(f32)
    keep = jnp.broadcast_to(keep[:, None], (ROWS, 128))

    if near:
        device = lax.axis_index("dp") * devices_t + rank
        own_near, own_far, own_down = owners(device, False), owners(device, True), owners(device, True, False)
        (block,) = call(
            pack_kernel, [w_qkv.T, vectors.T, w_out.T, w_up], [((A_ROWS + B_ROWS, D), bf16)], [], 1, 4,
        )
        edges = neighbours(jnp.stack([tokens, cotangent]), "tensor", EDGE)
        line = gather(block[None], ALONG_Z)
        down = w_down.T[None]
        down = jnp.concatenate([down, swap(down, ALONG_Y, ALONG_X)], axis=0)
        down = [down, swap(down, ALONG_X, ALONG_Y)]
        line, down, edges = lax.optimization_barrier((line, down, edges))
        line, down = jnp.concatenate(line, axis=0), jnp.concatenate(down, axis=0)
        near_pieces = swap(line, ALONG_Y, ALONG_X)
        down = [down, swap(down, ALONG_Z[0], ALONG_Z[1])]
        near_pieces, down = lax.optimization_barrier((near_pieces, down))
        down = jnp.concatenate(down, axis=0)
        near_pieces = jnp.concatenate([line, near_pieces], axis=0)
        a_far = swap(near_pieces[:, :A_ROWS], ALONG_X, ALONG_Y)
        b_far = swap(near_pieces[:, A_ROWS:], ALONG_X, ALONG_Y)
        pieces = both_cores([near_pieces])
        a_pieces = [pieces[0], a_far, pieces[1], swap(a_far, CORES)]
        c_pieces = [down, swap(down, ALONG_Z[1], ALONG_Z[0])]
    else:
        own_near = own_far = own_down = jnp.arange(SLOTS, dtype=jnp.int32)
        edges = neighbours(jnp.stack([tokens, cotangent]), "tensor", EDGE)
        qkv, out, vec = (lax.all_gather(a, BOTH, axis=1, tiled=True).T for a in (w_qkv, w_out, vectors))
        vec = jnp.pad(vec, ((0, 0), (0, D - vec.shape[1])))
        up = lax.all_gather(lax.all_gather(w_up, "dp", axis=0, tiled=True), "tensor", axis=1, tiled=True)
        down = lax.all_gather(lax.all_gather(w_down, "dp", axis=1, tiled=True), "tensor", axis=0, tiled=True).T
        up, down = (
            a.reshape(SLOTS // CHUNKS, UP_ROWS, CHUNKS, D).transpose(0, 2, 1, 3).reshape(SLOTS, UP_ROWS, D)
            for a in (up, down)
        )
        a_slots = jnp.concatenate([a.reshape(SLOTS, -1, D) for a in (qkv, vec)], axis=1)
        b_slots = jnp.concatenate([out.reshape(SLOTS, -1, D), up], axis=1)
        a_pieces, b_pieces, c_pieces = (
            [a[i : i + PIECE] for i in range(0, SLOTS, PIECE)] for a in (a_slots, b_slots, down)
        )

    edges = jnp.concatenate(edges, axis=2).reshape(2, CLIPS * BAND, D)
    x = jnp.concatenate([tokens.reshape(OWN_ALL, D), edges[0]], axis=0)
    cot = jnp.concatenate([cotangent.reshape(OWN_ALL, D), edges[1]], axis=0)
    if near:
        x, *c_pieces = lax.optimization_barrier((x, *c_pieces))
    proj, probs, mixed, scaled, wqkv, vec = call(
        attend_kernel, [own_far, keep, x, *a_pieces],
        [
            ((ROWS, 3 * D), bf16), ((CLIPS * BANDS, 2, BAND, HALF), f32), ((ROWS, D), bf16), ((ROWS, D), bf16),
            ((3 * D, D), bf16), ((16, D), f32),
        ],
        [((D, 128), f32), ((HALF, HALF), bf16), ((BAND, HALF), f32), ((ROWS, D), bf16)],
        6, 20,
    )
    if near:
        b_far = after(b_far, proj)
        b_pieces = [pieces[0], b_far, pieces[1], swap(b_far, CORES)]
    dn_kept, dn_sent, resid, hid, slope, second, branch_low, up_all, wout = call(
        up_kernel, [own_far, own_down, keep, cot, x, mixed, vec, *b_pieces],
        [
            ((NEAR, UP_ROWS, D), bf16), ((NEAR, UP_ROWS, D), bf16), ((ROWS, D), f32), ((ROWS, FF), bf16),
            ((ROWS, FF), bf16), ((ROWS, D), bf16), ((ROWS, D), bf16), ((D, FF), bf16), ((D, D), bf16),
        ],
        [
            ((D, FF), bf16), ((ROWS, FF), f32), ((D, OWN_ALL), bf16), ((ROWS, D), f32), ((ROWS, D), bf16),
        ],
        8, 30,
    )
    if near:
        c_pieces = both_cores(c_pieces)
    up_kept, up_sent, branch, gsec, colsum = call(
        down_kernel, [own_far, own_down, hid, slope, second, branch_low, up_all, *c_pieces],
        [
            ((NEAR, UP_ROWS, D), bf16), ((NEAR, UP_ROWS, D), bf16), ((OWN_ALL, D), f32), ((ROWS, D), f32),
            ((8, D), f32),
        ],
        [
            ((D, FF), bf16), ((D, FF), bf16), ((ROWS, FF), f32), ((ROWS, FF), bf16), ((D + 16, OWN_ALL), bf16),
        ],
        8, 30,
    )
    if near:
        dn_sum = wide(dn_kept) + wide(after(swap(dn_sent, CORES), gsec))
        dn_far = dn_sum[NEAR // 2 :].astype(bf16)
        up_sum = wide(up_kept) + wide(swap(up_sent, CORES))
        up_far = up_sum[NEAR // 2 :].astype(bf16)
        gsec, up_far, dn_far = lax.optimization_barrier((gsec, up_far, dn_far))
    out, gres, go_kept, go_sent, gmix, sums = call(
        finish_kernel, [own_far, keep, cot, mixed, resid, branch, gsec, wout, vec],
        [
            ((OWN_ALL, D), bf16), ((ROWS, D), f32), ((NEAR, OUT_ROWS, D), bf16), ((NEAR, OUT_ROWS, D), bf16),
            ((ROWS, D), bf16), ((8, D), f32),
        ],
        [((ROWS, D), bf16), ((D, D), bf16)],
        5, 16,
    )
    if near:
        go_sum = wide(go_kept) + wide(swap(go_sent, CORES))
        go_far = go_sum[NEAR // 2 :].astype(bf16)
        gmix = after(gmix, go_far)
    gproj, at_kept, at_sent = call(
        back_kernel, [own_near, gmix, proj, probs, scaled, wqkv, vec, sums, colsum],
        [((ROWS, 3 * D), bf16), ((NEAR, A_ROWS, D), bf16), ((NEAR, A_ROWS, D), bf16)],
        [
            ((HALF, HALF), bf16), ((CLIPS * BANDS, 2, BAND, HALF), bf16), ((3 * D, D), bf16),
            ((128, D), f32), ((D, 128), bf16),
        ],
        20, 20,
    )
    if near:
        dn_arrived = swap(dn_far, ALONG_Z[1], ALONG_Z[0])
        ff_arrived = [swap(far, ALONG_X, ALONG_Y) for far in (up_far, go_far)]
        dn_arrived, ff_arrived, gproj, at_sent = lax.optimization_barrier((dn_arrived, ff_arrived, gproj, at_sent))
        dn_sum = dn_sum[: NEAR // 2] + wide(dn_arrived)
        dn_sum = dn_sum[:PIECE] + wide(swap(dn_sum[PIECE:].astype(bf16), ALONG_Z[0], ALONG_Z[1]))
        dn_sum = dn_sum[:2] + wide(swap(dn_sum[2:].astype(bf16), ALONG_X, ALONG_Y))
        dn_sum = dn_sum[0] + wide(swap(dn_sum[1:].astype(bf16), ALONG_Y, ALONG_X))[0]
        up_sum = up_sum[: NEAR // 2] + wide(ff_arrived[0])
        go_sum = go_sum[: NEAR // 2] + wide(ff_arrived[1])
        ff_sum = jnp.concatenate([up_sum, go_sum], axis=1)
        ff_arrived = swap(ff_sum[PIECE:].astype(bf16), ALONG_Y, ALONG_X)
        at_sum = wide(at_kept) + wide(swap(at_sent, CORES))
        at_rest = [at_sum[i : i + PIECE].astype(bf16) for i in range(PIECE, NEAR, PIECE)]
        gproj = after(gproj, ff_arrived)
    (gtok,) = call(
        token_kernel, [gproj, x, gres, wqkv, vec], [((OWN_ALL, D), f32)], [], 5, 12,
    )
    if near:
        ff_sum = ff_sum[:PIECE] + wide(ff_arrived)
        at_sum = at_sum[:PIECE]
        for piece, mask in zip(at_rest, ALONG_XY):
            at_sum = at_sum + wide(after(swap(piece, mask), gtok))
        ff_sum = scatter_sum(singles(ff_sum), ALONG_Z)[0]
        at_sum = scatter_sum(singles(at_sum), ALONG_Z)[0]
    if near:
        g_up, g_down = ff_sum[:UP_ROWS], dn_sum.T
        g_out = ff_sum[UP_ROWS:].T
        g_qkv = at_sum[:QKV_ROWS].T
        g_vec = at_sum[QKV_ROWS:, : vectors.shape[0]].T
    else:
        at_grads = jnp.concatenate([at_kept, at_sent], axis=0)

        def whole(array):
            blocks = array.reshape(SLOTS // CHUNKS, CHUNKS, UP_ROWS, D).transpose(0, 2, 1, 3)
            return blocks.reshape(D, FF)

        g_up = lax.psum_scatter(whole(jnp.concatenate([up_kept, up_sent], axis=0)), "dp", scatter_dimension=0, tiled=True)
        g_up = lax.psum_scatter(g_up, "tensor", scatter_dimension=1, tiled=True).astype(f32)
        g_down = lax.psum_scatter(whole(jnp.concatenate([dn_kept, dn_sent], axis=0)).T, "dp", scatter_dimension=1, tiled=True)
        g_down = lax.psum_scatter(g_down, "tensor", scatter_dimension=0, tiled=True).astype(f32)

        def owned(array, columns):
            array = array.astype(f32).reshape(-1, D)[:, :columns].T
            return lax.psum_scatter(array, BOTH, scatter_dimension=1, tiled=True)

        g_qkv = owned(at_grads[:, :QKV_ROWS], D)
        g_out = owned(jnp.concatenate([go_kept, go_sent], axis=0), D)
        g_vec = owned(at_grads[:, QKV_ROWS:], vectors.shape[0])
    shape = tokens.shape
    return (out.reshape(shape), gtok.reshape(shape), g_qkv, g_out, g_vec, g_up, g_down)


def solution(mesh):
    placed = (
        P("dp", "tensor", None),
        P("dp"),
        P(None, BOTH),
        P(None, BOTH),
        P(None, BOTH),
        P("dp", "tensor"),
        P("tensor", "dp"),
        P("dp", "tensor", None),
    )
    return jax.shard_map(
        shards,
        mesh=mesh,
        in_specs=placed,
        out_specs=(
            P("dp", "tensor", None),
            P("dp", "tensor", None),
            P(None, BOTH),
            P(None, BOTH),
            P(None, BOTH),
            P("dp", "tensor"),
            P("tensor", "dp"),
        ),
        check_vma=False,
    )
```

time: 805 us -> 142 us (0.18)
  waiting for transfers between devices: 409 us -> 54 us
  blocking collectives: 148 us -> 0 us
  matrix products: 80.9 us -> 0 us
  local copies, waits for them, and re-layouts: 83.3 us -> 9.65 us
  other arithmetic: 44.9 us -> 5.43 us
  Pallas kernels: 0 us -> 35.6 us
  starting transfers between devices: 17.1 us -> 36 us
  between operations: 15.5 us -> 1.18 us
    reduce_scatter x4 -> x0, waiting for transfers between devices: 287 us -> none  [the longest x1 132 us: shards(): lax.psum_scatter(out_grad, ('dp', 'tensor'), scatter_dimension=1, tiled=T...]
    all_gather x4 -> x0, blocking collectives: 148 us -> none  [the longest x1 43.7 us: shards(): lax.all_gather(vectors, ('dp', 'tensor'), axis=1, tiled=True)]
    unnamed x9 -> x0, waiting for transfers between devices: 83.6 us -> none
    dot_general x18 -> x0, matrix products: 80.9 us -> none  [the longest x4 14.4 us: contract_rows(): lax.dot_general(first_arr, second_arr, (((0,), (0,)), ((), ())), preferre...]
    ppermute x4 -> x37, waiting for transfers between devices: 0.01 us -> 54 us  [the longest x35 54 us: swap(): lax.ppermute(array, BOTH, [(device, device ^ masks[device % 2]) for devic...]
    pallas_call x0 -> x7, Pallas kernels: none -> 35.6 us  [call(): pl.pallas_call(kernel, out_shape=[jax.ShapeDtypeStruct(s, t) for s, t in...]
    ppermute x4 -> x37, starting transfers between devices: 7.78 us -> 36 us  [the longest x35 32.8 us: swap(): lax.ppermute(array, BOTH, [(device, device ^ masks[device % 2]) for devic...]
    all_to_all x2 -> x0, waiting for transfers between devices: 26.5 us -> none  [sum_at_owner(): lax.all_to_all(tiles, axis, split_axis=0, concat_axis=0, tiled=True)]
  transfers between devices with their start and end apart: 14 -> 37, of which waited for: 8 -> 15; matrix products, arithmetic and copies ran while one was open for 9% -> 6% of each run, Pallas kernels for 0% -> 22%
where the time goes in v1:
time: 142 us
  waiting for transfers between devices  54 us (38%)
  starting transfers between devices  36 us (25%)
  Pallas kernels  35.6 us (25%)
  local copies, waits for them, and re-layouts  9.65 us (7%)
  other arithmetic  5.43 us (4%)
    ppermute x35, waiting for transfers between devices, swap(): lax.ppermute(array, BOTH, [(device, device ^ masks[device % 2]) for devic...  54 us
    pallas_call x7, Pallas kernels, call(): pl.pallas_call(kernel, out_shape=[jax.ShapeDtypeStruct(s, t) for s, t in...  35.6 us
    ppermute x35, starting transfers between devices, swap(): lax.ppermute(array, BOTH, [(device, device ^ masks[device % 2]) for devic...  32.8 us
    unnamed x39, local copies, waits for them, and re-layouts  5.6 us
  transfers between devices with their start and end apart: 37, of which 15 were waited for; matrix products, arithmetic and copies ran while one was open for 6% of the time, Pallas kernels for 22%

profile of v1, /device:TPU:0, one launch (start us, length us, event | category | flops | bytes accessed | tf_op | source)
XLA Modules:
  0.0 141.8 jit_solution(11209132671092758371)
XLA Ops:
  3.8 5.1 %collective-permute-start.2 = (bf16[1,144,512]{2,1,0:T(8,128)(2,1)S(1)}, bf16[1,144,512]{2,1,0:T(8,128)(2,1)S(1)}, u32[]{:S(2)}, u32[]{:S(2)}) collective-permute-start(bf16[1,144,512]{2,1,0:T(8,128)(2,1)S(1)} %bitcast.36), channel_id=1, source_target_pairs={{0,24},{1,25},{2,26},{3,27},{4,28},{5,29},{6,30},{7,31},{8,16},{9,... | collective-permute-start | bytes 442376 | tf_op jit(solution)/shard_map/ppermute | solution.py:458
  9.6 1.7 %collective-permute-start.3 = (bf16[1,64,512]{2,1,0:T(8,128)(2,1)S(1)}, bf16[1,64,512]{2,1,0:T(8,128)(2,1)S(1)}, u32[]{:S(2)}, u32[]{:S(2)}) collective-permute-start(bf16[1,64,512]{2,1,0:T(8,128)(2,1)S(1)} %bitcast.51), channel_id=1, source_target_pairs={{0,2},{1,5},{2,0},{3,7},{4,6},{5,1},{6,4},{7,3},{8,10},{9,13},{10,... | collective-permute-start | bytes 196616 | tf_op jit(solution)/shard_map/ppermute | solution.py:458
  11.3 1.3 collective-permute-start.6
  13.8 1.9 %collective-permute-start.5 = (bf16[2,4,16,512]{3,2,1,0:T(8,128)(2,1)S(1)}, bf16[2,4,16,512]{3,2,1,0:T(8,128)(2,1)S(1)}, u32[]{:S(2)}, u32[]{:S(2)}) collective-permute-start(bf16[2,4,16,512]{3,2,1,0:T(8,128)(2,1)S(1)} %get-tuple-element.140), channel_id=1, source_target_pairs={{0,1},{1,2},{2,3},{4,5},{5,6},{6,7},{8,9},{9,10},{10,11},{12,13},{... | collective-permute-start | bytes 393224 | tf_op jit(solution)/shard_map/ppermute | solution.py:510
  15.7 1.6 %collective-permute-start.4 = (bf16[2,64,512]{2,1,0:T(8,128)(2,1)S(1)}, bf16[2,64,512]{2,1,0:T(8,128)(2,1)S(1)}, u32[]{:S(2)}, u32[]{:S(2)}) collective-permute-start(bf16[2,64,512]{2,1,0:T(8,128)(2,1)S(1)} %pad_maximum_fusion.6), channel_id=1, source_target_pairs={{0,4},{1,3},{2,6},{3,1},{4,0},{5,7},{6,2},{7,5},{8,12},{9,11},{10,... | collective-permute-start | bytes 393224 | tf_op jit(solution)/shard_map/ppermute | solution.py:458
  17.8 3.6 %collective-permute-done.1 = bf16[1,144,512]{2,1,0:T(8,128)(2,1)S(1)} collective-permute-done((bf16[1,144,512]{2,1,0:T(8,128)(2,1)S(1)}, bf16[1,144,512]{2,1,0:T(8,128)(2,1)S(1)}, u32[]{:S(2)}, u32[]{:S(2)}) %collective-permute-start.1) | collective-permute-done | bytes 147488 | tf_op jit(solution)/shard_map/ppermute | solution.py:458
  21.5 1.6 %collective-permute-start.7 = (bf16[4,144,512]{2,1,0:T(8,128)(2,1)S(1)}, bf16[4,144,512]{2,1,0:T(8,128)(2,1)S(1)}, u32[]{:S(2)}, u32[]{:S(2)}) collective-permute-start(bf16[4,144,512]{2,1,0:T(8,128)(2,1)S(1)} %pad_maximum_fusion.3), channel_id=1, source_target_pairs={{0,2},{1,5},{2,0},{3,7},{4,6},{5,1},{6,4},{7,3},{8,10},{9,13},{10,... | collective-permute-start | bytes 1769480 | tf_op jit(solution)/shard_map/ppermute | solution.py:458
  24.1 8.0 %collective-permute-done.8 = bf16[4,64,512]{2,1,0:T(8,128)(2,1)S(1)} collective-permute-done((bf16[4,64,512]{2,1,0:T(8,128)(2,1)S(1)}, bf16[4,64,512]{2,1,0:T(8,128)(2,1)S(1)}, u32[]{:S(2)}, u32[]{:S(2)}) %collective-permute-start.8) | collective-permute-done | bytes 262176 | tf_op jit(solution)/shard_map/ppermute | solution.py:458
  38.2 2.0 %collective-permute-start.9 = (bf16[8,64,512]{2,1,0:T(8,128)(2,1)S(1)}, bf16[8,64,512]{2,1,0:T(8,128)(2,1)S(1)}, u32[]{:S(2)}, u32[]{:S(2)}) collective-permute-start(bf16[8,64,512]{2,1,0:T(8,128)(2,1)S(1)} %constant_dynamic-update-slice_fusion.4.refs_0_), channel_id=1, source_target_pairs={{0,16},{1,9},{2,18},{3,11},{4,20},{5,13},{6,22},{7,15},{8,24},{9,1... | collective-permute-start | bytes 1572872 | tf_op jit(solution)/shard_map/ppermute | solution.py:458
  40.2 4.0 %collective-permute-done.10.refs_1_ = bf16[8,64,512]{2,1,0:T(8,128)(2,1)S(1)} collective-permute-done((bf16[8,64,512]{2,1,0:T(8,128)(2,1)S(1)}, bf16[8,64,512]{2,1,0:T(8,128)(2,1)S(1)}, u32[]{:S(2)}, u32[]{:S(2)}) %collective-permute-start.10) | collective-permute-done | bytes 524320 | tf_op jit(solution)/shard_map/ppermute | solution.py:458
  45.2 8.8 %collective-permute-done.9.refs_1_ = bf16[8,64,512]{2,1,0:T(8,128)(2,1)S(1)} collective-permute-done((bf16[8,64,512]{2,1,0:T(8,128)(2,1)S(1)}, bf16[8,64,512]{2,1,0:T(8,128)(2,1)S(1)}, u32[]{:S(2)}, u32[]{:S(2)}) %collective-permute-start.9) | collective-permute-done | bytes 524320 | tf_op jit(solution)/shard_map/ppermute | solution.py:458
  54.1 6.6 %shard_map.244 = (bf16[640,1536]{1,0:T(8,128)(2,1)S(1)}, f32[20,2,32,256]{3,2,1,0:T(8,128)S(1)}, bf16[640,512]{1,0:T(8,128)(2,1)S(1)}, bf16[640,512]{1,0:T(8,128...) custom-call(s32[32]{0:T(128)S(1)} %get-tuple-element.153.own_ref, ...), custom_call_target="tpu_custom_call" | custom-call | flops 6600000000 | bytes 1048576 | tf_op jit(solution)/shard_map/pallas_call | solution.py:444
  61.6 1.3 collective-permute-done.14.refs_3_
  62.9 7.1 %shard_map.245 = (bf16[16,64,512]{2,1,0:T(8,128)(2,1)S(1)}, bf16[16,64,512]{2,1,0:T(8,128)(2,1)S(1)}, f32[640,512]{1,0:T(8,128)S(1)}, bf16[640,2048]{1,0:T(8,128...) custom-call(s32[32]{0:T(128)S(1)} %get-tuple-element.153.own_ref, ...), custom_call_target="tpu_custom_call" | custom-call | flops 8800000000 | bytes 1048576 | tf_op jit(solution)/shard_map/pallas_call | solution.py:444
  70.2 6.1 %shard_map.246 = (bf16[16,64,512]{2,1,0:T(8,128)(2,1)S(1)}, bf16[16,64,512]{2,1,0:T(8,128)(2,1)S(1)}, f32[512,512]{1,0:T(8,128)S(1)}, f32[640,512]{1,0:T(8,128)S(1)}, f32[8,512]{1,0:T(8,128)S(1)}) custom-call(s32[32]{0:T(128)S(1)} %get-tuple-element.153.own_ref, s32[32]{0:T(128)S(1)} %add_xor_fusion.1.own_down_ref, ...), custom_call_target="tpu_custom_call" | custom-call | flops 8800000000 | bytes 1048576 | tf_op jit(solution)/shard_map/pallas_call | solution.py:444
  77.2 1.9 %collective-permute-done.17 = bf16[16,64,512]{2,1,0:T(8,128)(2,1)S(1)} collective-permute-done((bf16[16,64,512]{2,1,0:T(8,128)(2,1)S(1)}, bf16[16,64,512]{2,1,0:T(8,128)(2,1)S(1)}, u32[]{:S(2)}, u32[]{:S(2)}) %collective-permute-start.17) | collective-permute-done | bytes 1048608 | tf_op jit(solution)/shard_map/ppermute | solution.py:458
  79.4 4.1 %shard_map.247 = (bf16[512,512]{1,0:T(8,128)(2,1)}, f32[640,512]{1,0:T(8,128)S(1)}, bf16[16,16,512]{2,1,0:T(8,128)(2,1)S(1)}, bf16[16,16,512]{2,1,0:T(8,128)(2,1...) custom-call(s32[32]{0:T(128)S(1)} %get-tuple-element.153.own_ref, f32[640,128]{1,0:T(8,128)S(1)} %broadcast_in_dim.54.keep_ref, ...), custom_call_target="tpu_custom_call" | custom-call | flops 5500000256 | bytes 1048576 | tf_op jit(solution)/shard_map/pallas_call | solution.py:444
  85.2 1.2 collective-permute-start.22
  86.4 8.8 %shard_map.248 = (bf16[640,1536]{1,0:T(8,128)(2,1)S(1)}, bf16[16,64,512]{2,1,0:T(8,128)(2,1)S(1)}, bf16[16,64,512]{2,1,0:T(8,128)(2,1)S(1)}) custom-call(s32[32]{0:T(128)S(1)} %get-tuple-element.154.own_ref, bf16[640,512]{1,0:T(8,128)(2,1)S(1)} %get-tuple-element.104.gmix_ref, bf16[640,1536]{1,0:T(8,128)(2,1)S(1)} %get-tuple-element.79.proj_ref, ...), custom_call_target="tpu_custom_call" | custom-call | flops 22000001024 | bytes 1048576 | tf_op jit(solution)/shard_map/pallas_call | solution.py:444
  95.3 4.3 %collective-permute-done.19 = bf16[8,64,512]{2,1,0:T(8,128)(2,1)S(1)} collective-permute-done((bf16[8,64,512]{2,1,0:T(8,128)(2,1)S(1)}, bf16[8,64,512]{2,1,0:T(8,128)(2,1)S(1)}, u32[]{:S(2)}, u32[]{:S(2)}) %collective-permute-start.19) | collective-permute-done | bytes 524320 | tf_op jit(solution)/shard_map/ppermute | solution.py:458
  101.4 7.0 %collective-permute-done.34 = bf16[4,64,512]{2,1,0:T(8,128)(2,1)S(1)} collective-permute-done((bf16[4,64,512]{2,1,0:T(8,128)(2,1)S(1)}, bf16[4,64,512]{2,1,0:T(8,128)(2,1)S(1)}, u32[]{:S(2)}, u32[]{:S(2)}) %collective-permute-start.34) | collective-permute-done | bytes 262176 | tf_op jit(solution)/shard_map/ppermute | solution.py:458
  108.5 1.4 collective-permute-start.35
  110.1 2.0 %collective-permute-start.33 = (bf16[1,80,512]{2,1,0:T(8,128)(2,1)S(1)}, bf16[1,80,512]{2,1,0:T(8,128)(2,1)S(1)}, u32[]{:S(2)}, u32[]{:S(2)}) collective-permute-start(bf16[1,80,512]{2,1,0:T(8,128)(2,1)S(1)} %get-tuple-element.142), channel_id=1, source_target_pairs={{0,24},{1,25},{2,26},{3,27},{4,28},{5,29},{6,30},{7,31},{8,16},{9,... | collective-permute-start | bytes 245768 | tf_op jit(solution)/shard_map/ppermute | solution.py:458
  112.1 1.4 %collective-permute-start.32 = (bf16[1,80,512]{2,1,0:T(8,128)(2,1)S(1)}, bf16[1,80,512]{2,1,0:T(8,128)(2,1)S(1)}, u32[]{:S(2)}, u32[]{:S(2)}) collective-permute-start(bf16[1,80,512]{2,1,0:T(8,128)(2,1)S(1)} %get-tuple-element.143), channel_id=1, source_target_pairs={{0,16},{1,17},{2,18},{3,19},{4,20},{5,21},{6,22},{7,23},{8,24},{9,... | collective-permute-start | bytes 245768 | tf_op jit(solution)/shard_map/ppermute | solution.py:458
  113.5 2.9 %shard_map.249 = f32[512,512]{1,0:T(8,128)} custom-call(bf16[640,1536]{1,0:T(8,128)(2,1)S(1)} %get-tuple-element.115.gproj_ref, bf16[640,512]{1,0:T(8,128)(2,1)S(1)} %pad_maximum_fusion.2.x_ref, f32[640,512]{1,0:T(8,128)S(1)} %get-tuple-element.116.gres_ref, bf16[1536,512]{1,0:T(8,128)(2,1)S(1)} %get-tuple-element.107.wqkv_ref, ...), custom_call_target="tpu_custom_call" | custom-call | flops 5500000256 | bytes 1048576 | tf_op jit(solution)/shard_map/pallas_call | solution.py:444
  116.6 2.0 %collective-permute-done.32 = bf16[1,80,512]{2,1,0:T(8,128)(2,1)S(1)} collective-permute-done((bf16[1,80,512]{2,1,0:T(8,128)(2,1)S(1)}, bf16[1,80,512]{2,1,0:T(8,128)(2,1)S(1)}, u32[]{:S(2)}, u32[]{:S(2)}) %collective-permute-start.32) | collective-permute-done | bytes 81952 | tf_op jit(solution)/shard_map/ppermute | solution.py:458
  119.2 1.3 collective-permute-start.25
  120.4 1.2 collective-permute-start.27
  124.0 6.9 %collective-permute-done.25 = bf16[4,64,512]{2,1,0:T(8,128)(2,1)S(1)} collective-permute-done((bf16[4,64,512]{2,1,0:T(8,128)(2,1)S(1)}, bf16[4,64,512]{2,1,0:T(8,128)(2,1)S(1)}, u32[]{:S(2)}, u32[]{:S(2)}) %collective-permute-start.25) | collective-permute-done | bytes 262176 | tf_op jit(solution)/shard_map/ppermute | solution.py:458
  131.8 2.8 %collective-permute-start.30 = (bf16[1,64,512]{2,1,0:T(8,128)(2,1)S(1)}, bf16[1,64,512]{2,1,0:T(8,128)(2,1)S(1)}, u32[]{:S(2)}, u32[]{:S(2)}) collective-permute-start(bf16[1,64,512]{2,1,0:T(8,128)(2,1)S(1)} %get-tuple-element.145), channel_id=1, source_target_pairs={{0,24},{1,25},{2,26},{3,27},{4,28},{5,29},{6,30},{7,31},{8,16},{9,... | collective-permute-start | bytes 196616 | tf_op jit(solution)/shard_map/ppermute | solution.py:458
  136.5 1.5 %collective-permute-done.30 = bf16[1,64,512]{2,1,0:T(8,128)(2,1)S(1)} collective-permute-done((bf16[1,64,512]{2,1,0:T(8,128)(2,1)S(1)}, bf16[1,64,512]{2,1,0:T(8,128)(2,1)S(1)}, u32[]{:S(2)}, u32[]{:S(2)}) %collective-permute-start.30) | collective-permute-done | bytes 65568 | tf_op jit(solution)/shard_map/ppermute | solution.py:458
  138.0 2.4 %collective-permute-done.29 = bf16[1,64,512]{2,1,0:T(8,128)(2,1)S(1)} collective-permute-done((bf16[1,64,512]{2,1,0:T(8,128)(2,1)S(1)}, bf16[1,64,512]{2,1,0:T(8,128)(2,1)S(1)}, u32[]{:S(2)}, u32[]{:S(2)}) %collective-permute-start.29) | collective-permute-done | bytes 65568 | tf_op jit(solution)/shard_map/ppermute | solution.py:458
  (142 shorter events, 27.1 us)
Async XLA Ops:
  3.8 14.0 %collective-permute-start.2 = (bf16[1,144,512]{2,1,0:T(8,128)(2,1)S(1)}, bf16[1,144,512]{2,1,0:T(8,128)(2,1)S(1)}, u32[]{:S(2)}, u32[]{:S(2)}) collective-permute-start(bf16[1,144,512]{2,1,0:T(8,128)(2,1)S(1)} %bitcast.36), channel_id=1, source_target_pairs={{0,24},{1,25},{2,26},{3,27},{4,28},{5,29},{6,30},{7,31},{8,16},{9,... | collective-permute-start | bytes 442376 | tf_op jit(solution)/shard_map/ppermute | solution.py:458
  8.9 12.5 %collective-permute-start.1 = (bf16[1,144,512]{2,1,0:T(8,128)(2,1)S(1)}, bf16[1,144,512]{2,1,0:T(8,128)(2,1)S(1)}, u32[]{:S(2)}, u32[]{:S(2)}) collective-permute-start(bf16[1,144,512]{2,1,0:T(8,128)(2,1)S(1)} %bitcast.37), channel_id=1, source_target_pairs={{0,16},{1,17},{2,18},{3,19},{4,20},{5,21},{6,22},{7,23},{8,24},{9,... | collective-permute-start | bytes 442376 | tf_op jit(solution)/shard_map/ppermute | solution.py:458
  8.9 12.5 %collective-permute-start = (bf16[1,144,512]{2,1,0:T(8,128)(2,1)S(1)}, bf16[1,144,512]{2,1,0:T(8,128)(2,1)S(1)}, u32[]{:S(2)}, u32[]{:S(2)}) collective-permute-start(bf16[1,144,512]{2,1,0:T(8,128)(2,1)S(1)} %bitcast.38), channel_id=1, source_target_pairs={{0,8},{1,9},{2,10},{3,11},{4,12},{5,13},{6,14},{7,15},{8,0},{9,1},... | collective-permute-start | bytes 442376 | tf_op jit(solution)/shard_map/ppermute | solution.py:458
  11.3 4.5 %collective-permute-start.6 = (bf16[2,4,16,512]{3,2,1,0:T(8,128)(2,1)S(1)}, bf16[2,4,16,512]{3,2,1,0:T(8,128)(2,1)S(1)}, u32[]{:S(2)}, u32[]{:S(2)}) collective-permute-start(bf16[2,4,16,512]{3,2,1,0:T(8,128)(2,1)S(1)} %get-tuple-element.139), channel_id=1, source_target_pairs={{1,0},{2,1},{3,2},{5,4},{6,5},{7,6},{9,8},{10,9},{11,10},{13,12},{... | collective-permute-start | bytes 393224 | tf_op jit(solution)/shard_map/ppermute | solution.py:511
  15.7 5.7 %collective-permute-start.4 = (bf16[2,64,512]{2,1,0:T(8,128)(2,1)S(1)}, bf16[2,64,512]{2,1,0:T(8,128)(2,1)S(1)}, u32[]{:S(2)}, u32[]{:S(2)}) collective-permute-start(bf16[2,64,512]{2,1,0:T(8,128)(2,1)S(1)} %pad_maximum_fusion.6), channel_id=1, source_target_pairs={{0,4},{1,3},{2,6},{3,1},{4,0},{5,7},{6,2},{7,5},{8,12},{9,11},{10,... | collective-permute-start | bytes 393224 | tf_op jit(solution)/shard_map/ppermute | solution.py:458
  21.5 11.3 %collective-permute-start.7 = (bf16[4,144,512]{2,1,0:T(8,128)(2,1)S(1)}, bf16[4,144,512]{2,1,0:T(8,128)(2,1)S(1)}, u32[]{:S(2)}, u32[]{:S(2)}) collective-permute-start(bf16[4,144,512]{2,1,0:T(8,128)(2,1)S(1)} %pad_maximum_fusion.3), channel_id=1, source_target_pairs={{0,2},{1,5},{2,0},{3,7},{4,6},{5,1},{6,4},{7,3},{8,10},{9,13},{10,... | collective-permute-start | bytes 1769480 | tf_op jit(solution)/shard_map/ppermute | solution.py:458
  23.1 9.0 %collective-permute-start.8 = (bf16[4,64,512]{2,1,0:T(8,128)(2,1)S(1)}, bf16[4,64,512]{2,1,0:T(8,128)(2,1)S(1)}, u32[]{:S(2)}, u32[]{:S(2)}) collective-permute-start(bf16[4,64,512]{2,1,0:T(8,128)(2,1)S(1)} %constant_dynamic-update-slice_fusion.2), channel_id=1, source_target_pairs={{0,8},{1,17},{2,10},{3,19},{4,12},{5,21},{6,14},{7,23},{8,0},{9,25... | collective-permute-start | bytes 786440 | tf_op jit(solution)/shard_map/ppermute | solution.py:458
  32.9 21.1 %collective-permute-start.11 = (bf16[8,144,512]{2,1,0:T(8,128)(2,1)S(1)}, bf16[8,144,512]{2,1,0:T(8,128)(2,1)S(1)}, u32[]{:S(2)}, u32[]{:S(2)}) collective-permute-start(bf16[8,144,512]{2,1,0:T(8,128)(2,1)S(1)} %constant_dynamic-update-slice_fusion.6.refs_0_), channel_id=1, source_target_pairs={{0,1},{1,0},{2,3},{3,2},{4,5},{5,4},{6,7},{7,6},{8,9},{9,8},{10,11... | collective-permute-start | bytes 3538952 | tf_op jit(solution)/shard_map/ppermute | solution.py:458
  34.9 9.2 %collective-permute-start.10 = (bf16[8,64,512]{2,1,0:T(8,128)(2,1)S(1)}, bf16[8,64,512]{2,1,0:T(8,128)(2,1)S(1)}, u32[]{:S(2)}, u32[]{:S(2)}) collective-permute-start(bf16[8,64,512]{2,1,0:T(8,128)(2,1)S(1)} %slice.176), channel_id=1, source_target_pairs={{0,4},{1,3},{2,6},{3,1},{4,0},{5,7},{6,2},{7,5},{8,12},{9,11},{10,... | collective-permute-start | bytes 1572872 | tf_op jit(solution)/shard_map/ppermute | solution.py:458
  38.2 15.8 %collective-permute-start.9 = (bf16[8,64,512]{2,1,0:T(8,128)(2,1)S(1)}, bf16[8,64,512]{2,1,0:T(8,128)(2,1)S(1)}, u32[]{:S(2)}, u32[]{:S(2)}) collective-permute-start(bf16[8,64,512]{2,1,0:T(8,128)(2,1)S(1)} %constant_dynamic-update-slice_fusion.4.refs_0_), channel_id=1, source_target_pairs={{0,16},{1,9},{2,18},{3,11},{4,20},{5,13},{6,22},{7,15},{8,24},{9,1... | collective-permute-start | bytes 1572872 | tf_op jit(solution)/shard_map/ppermute | solution.py:458
  44.2 9.8 %collective-permute-start.12 = (bf16[8,64,512]{2,1,0:T(8,128)(2,1)S(1)}, bf16[8,64,512]{2,1,0:T(8,128)(2,1)S(1)}, u32[]{:S(2)}, u32[]{:S(2)}) collective-permute-start(bf16[8,64,512]{2,1,0:T(8,128)(2,1)S(1)} %collective-permute-done.10.refs_1_), channel_id=1, source_target_pairs={{0,1},{1,0},{2,3},{3,2},{4,5},{5,4},{6,7},{7,6},{8,9},{9,8},{10,11... | collective-permute-start | bytes 1572872 | tf_op jit(solution)/shard_map/ppermute | solution.py:458
  44.3 16.5 %collective-permute-start.13 = (bf16[8,80,512]{2,1,0:T(8,128)(2,1)S(1)}, bf16[8,80,512]{2,1,0:T(8,128)(2,1)S(1)}, u32[]{:S(2)}, u32[]{:S(2)}) collective-permute-start(bf16[8,80,512]{2,1,0:T(8,128)(2,1)S(1)} %slice.177), channel_id=1, source_target_pairs={{0,4},{1,3},{2,6},{3,1},{4,0},{5,7},{6,2},{7,5},{8,12},{9,11},{10,... | collective-permute-start | bytes 1966088 | tf_op jit(solution)/shard_map/ppermute | solution.py:458
  61.0 9.2 %collective-permute-start.15 = (bf16[8,64,512]{2,1,0:T(8,128)(2,1)S(1)}, bf16[8,64,512]{2,1,0:T(8,128)(2,1)S(1)}, u32[]{:S(2)}, u32[]{:S(2)}) collective-permute-start(bf16[8,64,512]{2,1,0:T(8,128)(2,1)S(1)} %constant_dynamic-update-slice_fusion.4.refs_0_), channel_id=1, source_target_pairs={{0,1},{1,0},{2,3},{3,2},{4,5},{5,4},{6,7},{7,6},{8,9},{9,8},{10,11... | collective-permute-start | bytes 1572872 | tf_op jit(solution)/shard_map/ppermute | solution.py:458
  61.5 8.7 %collective-permute-start.16 = (bf16[8,64,512]{2,1,0:T(8,128)(2,1)S(1)}, bf16[8,64,512]{2,1,0:T(8,128)(2,1)S(1)}, u32[]{:S(2)}, u32[]{:S(2)}) collective-permute-start(bf16[8,64,512]{2,1,0:T(8,128)(2,1)S(1)} %collective-permute-done.9.refs_1_), channel_id=1, source_target_pairs={{0,1},{1,0},{2,3},{3,2},{4,5},{5,4},{6,7},{7,6},{8,9},{9,8},{10,11... | collective-permute-start | bytes 1572872 | tf_op jit(solution)/shard_map/ppermute | solution.py:458
  70.0 6.7 %collective-permute-start.18 = (bf16[16,64,512]{2,1,0:T(8,128)(2,1)S(1)}, bf16[16,64,512]{2,1,0:T(8,128)(2,1)S(1)}, u32[]{:S(2)}, u32[]{:S(2)}) collective-permute-start(bf16[16,64,512]{2,1,0:T(8,128)(2,1)S(1)} %get-tuple-element.94), channel_id=1, source_target_pairs={{0,1},{1,0},{2,3},{3,2},{4,5},{5,4},{6,7},{7,6},{8,9},{9,8},{10,11... | collective-permute-start | bytes 3145736 | tf_op jit(solution)/shard_map/ppermute | solution.py:458
  83.9 15.7 %collective-permute-start.19 = (bf16[8,64,512]{2,1,0:T(8,128)(2,1)S(1)}, bf16[8,64,512]{2,1,0:T(8,128)(2,1)S(1)}, u32[]{:S(2)}, u32[]{:S(2)}) collective-permute-start(bf16[8,64,512]{2,1,0:T(8,128)(2,1)S(1)} %slice.249), channel_id=1, source_target_pairs={{0,16},{1,9},{2,18},{3,11},{4,20},{5,13},{6,22},{7,15},{8,24},{9,1... | collective-permute-start | bytes 1572872 | tf_op jit(solution)/shard_map/ppermute | solution.py:458
  84.1 15.5 %collective-permute-start.20 = (bf16[8,64,512]{2,1,0:T(8,128)(2,1)S(1)}, bf16[8,64,512]{2,1,0:T(8,128)(2,1)S(1)}, u32[]{:S(2)}, u32[]{:S(2)}) collective-permute-start(bf16[8,64,512]{2,1,0:T(8,128)(2,1)S(1)} %slice.250), channel_id=1, source_target_pairs={{0,4},{1,3},{2,6},{3,1},{4,0},{5,7},{6,2},{7,5},{8,12},{9,11},{10,... | collective-permute-start | bytes 1572872 | tf_op jit(solution)/shard_map/ppermute | solution.py:458
  85.2 10.0 %collective-permute-start.22 = (bf16[8,16,512]{2,1,0:T(8,128)(2,1)S(1)}, bf16[8,16,512]{2,1,0:T(8,128)(2,1)S(1)}, u32[]{:S(2)}, u32[]{:S(2)}) collective-permute-start(bf16[8,16,512]{2,1,0:T(8,128)(2,1)S(1)} %slice.253), channel_id=1, source_target_pairs={{0,4},{1,3},{2,6},{3,1},{4,0},{5,7},{6,2},{7,5},{8,12},{9,11},{10,... | collective-permute-start | bytes 393224 | tf_op jit(solution)/shard_map/ppermute | solution.py:458
  100.0 8.4 %collective-permute-start.34 = (bf16[4,64,512]{2,1,0:T(8,128)(2,1)S(1)}, bf16[4,64,512]{2,1,0:T(8,128)(2,1)S(1)}, u32[]{:S(2)}, u32[]{:S(2)}) collective-permute-start(bf16[4,64,512]{2,1,0:T(8,128)(2,1)S(1)} %slice.251), channel_id=1, source_target_pairs={{0,8},{1,17},{2,10},{3,19},{4,12},{5,21},{6,14},{7,23},{8,0},{9,25... | collective-permute-start | bytes 786440 | tf_op jit(solution)/shard_map/ppermute | solution.py:458
  100.6 9.2 %collective-permute-start.23 = (bf16[4,80,512]{2,1,0:T(8,128)(2,1)S(1)}, bf16[4,80,512]{2,1,0:T(8,128)(2,1)S(1)}, u32[]{:S(2)}, u32[]{:S(2)}) collective-permute-start(bf16[4,80,512]{2,1,0:T(8,128)(2,1)S(1)} %fusion.1), channel_id=1, source_target_pairs={{0,2},{1,5},{2,0},{3,7},{4,6},{5,1},{6,4},{7,3},{8,10},{9,13},{10,... | collective-permute-start | bytes 983048 | tf_op jit(solution)/shard_map/ppermute | solution.py:458
  101.4 17.3 %collective-permute-start.24 = (bf16[16,64,512]{2,1,0:T(8,128)(2,1)S(1)}, bf16[16,64,512]{2,1,0:T(8,128)(2,1)S(1)}, u32[]{:S(2)}, u32[]{:S(2)}) collective-permute-start(bf16[16,64,512]{2,1,0:T(8,128)(2,1)S(1)} %get-tuple-element.118), channel_id=1, source_target_pairs={{0,1},{1,0},{2,3},{3,2},{4,5},{5,4},{6,7},{7,6},{8,9},{9,8},{10,11... | collective-permute-start | bytes 3145736 | tf_op jit(solution)/shard_map/ppermute | solution.py:458
  108.5 8.0 %collective-permute-start.35 = (bf16[2,64,512]{2,1,0:T(8,128)(2,1)S(1)}, bf16[2,64,512]{2,1,0:T(8,128)(2,1)S(1)}, u32[]{:S(2)}, u32[]{:S(2)}) collective-permute-start(bf16[2,64,512]{2,1,0:T(8,128)(2,1)S(1)} %slice.252), channel_id=1, source_target_pairs={{0,4},{1,3},{2,6},{3,1},{4,0},{5,7},{6,2},{7,5},{8,12},{9,11},{10,... | collective-permute-start | bytes 393224 | tf_op jit(solution)/shard_map/ppermute | solution.py:458
  110.0 6.7 %collective-permute-start.31 = (bf16[1,80,512]{2,1,0:T(8,128)(2,1)S(1)}, bf16[1,80,512]{2,1,0:T(8,128)(2,1)S(1)}, u32[]{:S(2)}, u32[]{:S(2)}) collective-permute-start(bf16[1,80,512]{2,1,0:T(8,128)(2,1)S(1)} %get-tuple-element.141), channel_id=1, source_target_pairs={{0,8},{1,9},{2,10},{3,11},{4,12},{5,13},{6,14},{7,15},{8,0},{9,1},... | collective-permute-start | bytes 245768 | tf_op jit(solution)/shard_map/ppermute | solution.py:458
  110.1 6.6 %collective-permute-start.33 = (bf16[1,80,512]{2,1,0:T(8,128)(2,1)S(1)}, bf16[1,80,512]{2,1,0:T(8,128)(2,1)S(1)}, u32[]{:S(2)}, u32[]{:S(2)}) collective-permute-start(bf16[1,80,512]{2,1,0:T(8,128)(2,1)S(1)} %get-tuple-element.142), channel_id=1, source_target_pairs={{0,24},{1,25},{2,26},{3,27},{4,28},{5,29},{6,30},{7,31},{8,16},{9,... | collective-permute-start | bytes 245768 | tf_op jit(solution)/shard_map/ppermute | solution.py:458
  112.1 6.5 %collective-permute-start.32 = (bf16[1,80,512]{2,1,0:T(8,128)(2,1)S(1)}, bf16[1,80,512]{2,1,0:T(8,128)(2,1)S(1)}, u32[]{:S(2)}, u32[]{:S(2)}) collective-permute-start(bf16[1,80,512]{2,1,0:T(8,128)(2,1)S(1)} %get-tuple-element.143), channel_id=1, source_target_pairs={{0,16},{1,17},{2,18},{3,19},{4,20},{5,21},{6,22},{7,23},{8,24},{9,... | collective-permute-start | bytes 245768 | tf_op jit(solution)/shard_map/ppermute | solution.py:458
  116.5 18.8 %collective-permute-start.36 = (bf16[1,64,512]{2,1,0:T(8,128)(2,1)S(1)}, bf16[1,64,512]{2,1,0:T(8,128)(2,1)S(1)}, u32[]{:S(2)}, u32[]{:S(2)}) collective-permute-start(bf16[1,64,512]{2,1,0:T(8,128)(2,1)S(1)} %slice.254), channel_id=1, source_target_pairs={{0,2},{1,5},{2,0},{3,7},{4,6},{5,1},{6,4},{7,3},{8,10},{9,13},{10,... | collective-permute-start | bytes 196616 | tf_op jit(solution)/shard_map/ppermute | solution.py:458
  119.2 11.7 %collective-permute-start.25 = (bf16[4,64,512]{2,1,0:T(8,128)(2,1)S(1)}, bf16[4,64,512]{2,1,0:T(8,128)(2,1)S(1)}, u32[]{:S(2)}, u32[]{:S(2)}) collective-permute-start(bf16[4,64,512]{2,1,0:T(8,128)(2,1)S(1)} %get-tuple-element.136), channel_id=1, source_target_pairs={{0,2},{1,3},{2,0},{3,1},{4,6},{5,7},{6,4},{7,5},{8,10},{9,11},{10,... | collective-permute-start | bytes 786440 | tf_op jit(solution)/shard_map/ppermute | solution.py:458
  120.4 10.5 %collective-permute-start.27 = (bf16[4,64,512]{2,1,0:T(8,128)(2,1)S(1)}, bf16[4,64,512]{2,1,0:T(8,128)(2,1)S(1)}, u32[]{:S(2)}, u32[]{:S(2)}) collective-permute-start(bf16[4,64,512]{2,1,0:T(8,128)(2,1)S(1)} %get-tuple-element.137), channel_id=1, source_target_pairs={{0,6},{1,7},{2,4},{3,5},{4,2},{5,3},{6,0},{7,1},{8,14},{9,15},{10,... | collective-permute-start | bytes 786440 | tf_op jit(solution)/shard_map/ppermute | solution.py:458
  121.6 9.9 %collective-permute-start.26 = (bf16[4,64,512]{2,1,0:T(8,128)(2,1)S(1)}, bf16[4,64,512]{2,1,0:T(8,128)(2,1)S(1)}, u32[]{:S(2)}, u32[]{:S(2)}) collective-permute-start(bf16[4,64,512]{2,1,0:T(8,128)(2,1)S(1)} %get-tuple-element.138), channel_id=1, source_target_pairs={{0,4},{1,5},{2,6},{3,7},{4,0},{5,1},{6,2},{7,3},{8,12},{9,13},{10,... | collective-permute-start | bytes 786440 | tf_op jit(solution)/shard_map/ppermute | solution.py:458
  131.7 4.8 %collective-permute-start.28 = (bf16[1,64,512]{2,1,0:T(8,128)(2,1)S(1)}, bf16[1,64,512]{2,1,0:T(8,128)(2,1)S(1)}, u32[]{:S(2)}, u32[]{:S(2)}) collective-permute-start(bf16[1,64,512]{2,1,0:T(8,128)(2,1)S(1)} %get-tuple-element.144), channel_id=1, source_target_pairs={{0,8},{1,9},{2,10},{3,11},{4,12},{5,13},{6,14},{7,15},{8,0},{9,1},... | collective-permute-start | bytes 196616 | tf_op jit(solution)/shard_map/ppermute | solution.py:458
  131.8 6.2 %collective-permute-start.30 = (bf16[1,64,512]{2,1,0:T(8,128)(2,1)S(1)}, bf16[1,64,512]{2,1,0:T(8,128)(2,1)S(1)}, u32[]{:S(2)}, u32[]{:S(2)}) collective-permute-start(bf16[1,64,512]{2,1,0:T(8,128)(2,1)S(1)} %get-tuple-element.145), channel_id=1, source_target_pairs={{0,24},{1,25},{2,26},{3,27},{4,28},{5,29},{6,30},{7,31},{8,16},{9,... | collective-permute-start | bytes 196616 | tf_op jit(solution)/shard_map/ppermute | solution.py:458
  134.6 5.9 %collective-permute-start.29 = (bf16[1,64,512]{2,1,0:T(8,128)(2,1)S(1)}, bf16[1,64,512]{2,1,0:T(8,128)(2,1)S(1)}, u32[]{:S(2)}, u32[]{:S(2)}) collective-permute-start(bf16[1,64,512]{2,1,0:T(8,128)(2,1)S(1)} %get-tuple-element.146), channel_id=1, source_target_pairs={{0,16},{1,17},{2,18},{3,19},{4,20},{5,21},{6,22},{7,23},{8,24},{9,... | collective-permute-start | bytes 196616 | tf_op jit(solution)/shard_map/ppermute | solution.py:458
  (20 other events, 109.0 us)

commit v2 on v1

--- a/solution.py
+++ b/solution.py
@@ -32,6 +32,8 @@
 CHUNKS = FF // D
 UP_ROWS = D * CHUNKS // SLOTS
 B_ROWS = OUT_ROWS + UP_ROWS
+G_ROWS = QKV_ROWS + OUT_ROWS
+V_ROWS = 16
 
 CLIPS = 4
 OWN = 128
@@ -195,7 +197,8 @@
 def write_grads(own_ref, pieces, block_ref):
     for slot in range(SLOTS):
         grads_ref, held = find(pieces, slot)
-        grads_ref[held] = block_ref[weight_block(own_ref[slot])]
+        owner = own_ref[slot]
+        grads_ref[held] = block_ref[owner % CHUNKS, rows_at(owner // CHUNKS * UP_ROWS, UP_ROWS), :]
 
 
 def up_kernel(
@@ -231,9 +234,10 @@
     branch_t[...] = branch_low[:OWN_ALL, :].T
 
     def products(chunk):
-        for quarter in range(4):
-            columns = slice(chunk * D + quarter * 128, chunk * D + (quarter + 1) * 128)
+        for half in range(2):
+            columns = slice(chunk * D + half * HALF, chunk * D + (half + 1) * HALF)
             pre_ref[:, columns] = nn(normed_ref[...], up_ref[:, columns])
+            yield
             yield
 
     def slopes(chunk):
@@ -250,7 +254,8 @@
     def weights(chunk):
         for half in range(2):
             columns = slice(chunk * D + half * HALF, chunk * D + (half + 1) * HALF)
-            gdown_ref[:, columns] = nn(branch_t[...], hid_ref[:OWN_ALL, columns]).astype(bf16)
+            gdown = nn(branch_t[...], hid_ref[:OWN_ALL, columns])
+            gdown_ref[chunk, :, half * HALF : (half + 1) * HALF] = gdown.astype(bf16)
             yield
             yield
 
@@ -296,7 +301,7 @@
         for half in range(2):
             columns = slice(chunk * D + half * HALF, chunk * D + (half + 1) * HALF)
             gup = nn(second_t[...], gpre_ref[:OWN_ALL, columns])
-            gup_ref[:, columns] = gup[:D].astype(bf16)
+            gup_ref[chunk, :, half * HALF : (half + 1) * HALF] = gup[:D].astype(bf16)
             colsum_ref[chunk : chunk + 1, half * HALF : (half + 1) * HALF] = gup[D : D + 1]
             yield
             yield
@@ -313,9 +318,9 @@
 
 
 def finish_kernel(
-    own_ref, keep_ref, cot_ref, mixed_ref, resid_ref, branch_ref, gsec_ref, wout_ref, vec_ref,
-    out_ref, gres_ref, kept_ref, sent_ref, gmix_ref, sums_ref,
-    gatt_ref, gout_ref,
+    keep_ref, cot_ref, mixed_ref, resid_ref, branch_ref, gsec_ref, wout_ref, vec_ref,
+    out_ref, gres_ref, gout_ref, gmix_ref, sums_ref,
+    gatt_ref,
 ):
     def rows(step, totals):
         here = rows_at(step * SUB, SUB)
@@ -336,9 +341,6 @@
         sums_ref[place : place + 1, :] = jnp.sum(total, axis=0, keepdims=True)
     gmix_ref[...] = nn(gatt_ref[...], wout_ref[...]).astype(bf16)
     gout_ref[...] = nn(gatt_ref[:OWN_ALL, :].T, mixed_ref[:OWN_ALL, :]).astype(bf16)
-    for slot in range(SLOTS):
-        grads_ref, held = find((kept_ref, sent_ref), slot)
-        grads_ref[held] = gout_ref[rows_at(own_ref[slot] * OUT_ROWS, OUT_ROWS), :]
 
     def outputs(step, carry):
         here = rows_at(step * SUB, SUB)
@@ -349,11 +351,7 @@
     lax.fori_loop(0, OWN_ALL // SUB, outputs, 0, unroll=4)
 
 
-def back_kernel(
-    own_ref, gmix_ref, proj_ref, prob_ref, scaled_ref, wqkv_ref, vec_ref, sums_ref, colsum_ref,
-    gproj_ref, kept_ref, sent_ref,
-    lanes_ref, gscore_ref, gqkv_ref, gvec_ref, column_vec,
-):
+def back_kernel(gmix_ref, proj_ref, prob_ref, gproj_ref, lanes_ref, gscore_ref):
     lanes_ref[...] = head_lanes().astype(bf16)
 
     def score(band, carry):
@@ -389,6 +387,12 @@
 
     lax.fori_loop(0, CLIPS * BANDS, mix, 0, unroll=10)
 
+
+def project_kernel(
+    own_ref, gproj_ref, gout_ref, scaled_ref, wqkv_ref, vec_ref, sums_ref, colsum_ref,
+    kept_ref, sent_ref,
+    gqkv_ref, gvec_ref,
+):
     def add_rows(step, totals):
         here = rows_at(step * SUB, SUB)
         return totals + gproj_ref[here, :].astype(f32).reshape(SUB // 8, 8, 3 * D).sum(axis=0)
@@ -417,13 +421,30 @@
     gvec_ref[3:4, :] = totals[:, 2 * D :]
     gvec_ref[4:8, :] = sums_ref[0:4, :]
     gvec_ref[8:12, :] = colsum_ref[0:4, :]
-    column_vec[...] = gvec_ref[...].T.astype(bf16)
     for slot in range(SLOTS):
         owner = own_ref[slot]
-        grads_ref, held = find((kept_ref, sent_ref), slot)
-        grads_ref[held, :QKV_ROWS, :] = gqkv_ref[rows_at(owner * QKV_ROWS, QKV_ROWS), :]
-        grads_ref[held, QKV_ROWS:, :128] = column_vec[rows_at(owner * OUT_ROWS, OUT_ROWS), :]
-        grads_ref[held, QKV_ROWS:, 128:] = jnp.zeros((OUT_ROWS, D - 128), bf16)
+        grads_ref, held = (kept_ref, sent_ref)[slot // NEAR], slot % NEAR * G_ROWS
+        grads_ref[held : held + QKV_ROWS, :] = gqkv_ref[rows_at(owner * QKV_ROWS, QKV_ROWS), :]
+        grads_ref[held + QKV_ROWS : held + G_ROWS, :] = gout_ref[rows_at(owner * OUT_ROWS, OUT_ROWS), :]
+    for grads_ref in (kept_ref, sent_ref):
+        grads_ref[NEAR * G_ROWS :, :] = gvec_ref[:V_ROWS, :].astype(bf16)
+
+
+def share_kernel(*refs):
+    *pieces, kept_ref, first_ref, second_ref, third_ref = refs
+    size = kept_ref.shape[0] - V_ROWS
+
+    def total(rows):
+        result = pieces[0][rows, :].astype(f32)
+        for piece in pieces[1:]:
+            result = result + piece[rows, :].astype(f32)
+        return result
+
+    vectors = total(slice(4 * size, 4 * size + V_ROWS))
+    for part, out_ref in enumerate((kept_ref, first_ref, second_ref, third_ref)):
+        for low in range(0, size, 64):
+            out_ref[low : low + 64, :] = total(slice(part * size + low, part * size + low + 64)).astype(out_ref.dtype)
+        out_ref[size:, :] = vectors.astype(out_ref.dtype)
 
 
 def token_kernel( gproj_ref, x_ref, gres_ref, wqkv_ref, vec_ref, gtok_ref):
@@ -437,6 +458,17 @@
         return carry
 
     lax.fori_loop(0, OWN_ALL // STEP, rows, 0)
+
+
+def total_kernel(device_ref, *refs):
+    *pieces, gqkv_ref, gout_ref, gvec_ref = refs
+    total = pieces[0][...]
+    for piece in pieces[1:]:
+        total = total + piece[...].astype(f32)
+    gqkv_ref[...] = total[:QKV_ROWS]
+    gout_ref[...] = total[QKV_ROWS:G_ROWS]
+    own = pltpu.roll(total[G_ROWS:], lax.rem(D - device_ref[0] * OUT_ROWS, D), 1)
+    gvec_ref[...] = own[: gvec_ref.shape[0], : gvec_ref.shape[1]]
 
 
 def call(kernel, args, outs, scratch, micros, mib):
@@ -462,14 +494,14 @@
 ALONG_XY = (ALONG_Y, ALONG_X, ALONG_Y ^ ALONG_X)
 
 
-def owners(device, swapped, line_first=True):
+def owners(device, swapped, line_first=True, turn=None):
     def one(second_core):
         first = ALONG_X if second_core and swapped else ALONG_Y
         plane = [0, first, first ^ ALONG_XY[2], ALONG_XY[2]]
-        if line_first:
-            return [m ^ o for o in plane for m in (0, *ALONG_Z)]
-        line = [0, ALONG_Z[second_core], ALONG_Z[1 - second_core], ALONG_Z[2]]
-        return [m ^ o for o in line for m in plane]
+        line = [0, *ALONG_Z]
+        if turn is not None and second_core != turn:
+            line = [line[0], line[2], line[1], line[3]]
+        return [m ^ o for o in plane for m in line] if line_first else [m ^ o for o in line for m in plane]
 
     core = device % 2
     first = jnp.where(core == 0, jnp.array(one(0)), jnp.array(one(1)))
@@ -489,15 +521,10 @@
     return array.astype(f32)
 
 
-def scatter_sum(pieces, phase):
-    total = pieces[0]
-    for piece, mask in zip(pieces[1:], phase):
-        total = total + wide(swap(piece.astype(bf16), mask))
+def add_all(total, others):
+    for other in others:
+        total = total + wide(other)
     return total
-
-
-def singles(piece):
-    return [piece[i : i + 1] for i in range(PIECE)]
 
 
 def after(array, *others):
@@ -528,7 +555,8 @@
 
     if near:
         device = lax.axis_index("dp") * devices_t + rank
-        own_near, own_far, own_down = owners(device, False), owners(device, True), owners(device, True, False)
+        own_near, own_far = owners(device, False), owners(device, True)
+        own_down, own_up = owners(device, True, False, 0), owners(device, True, True, 1)
         (block,) = call(
             pack_kernel, [w_qkv.T, vectors.T, w_out.T, w_up], [((A_ROWS + B_ROWS, D), bf16)], [], 1, 4,
         )
@@ -537,7 +565,9 @@
         down = w_down.T[None]
         down = jnp.concatenate([down, swap(down, ALONG_Y, ALONG_X)], axis=0)
         down = [down, swap(down, ALONG_X, ALONG_Y)]
-        line, down, edges = lax.optimization_barrier((line, down, edges))
+        line, down, edges, keep, own_near, own_far, own_down, own_up = lax.optimization_barrier(
+            (line, down, edges, keep, own_near, own_far, own_down, own_up)
+        )
         line, down = jnp.concatenate(line, axis=0), jnp.concatenate(down, axis=0)
         near_pieces = swap(line, ALONG_Y, ALONG_X)
         down = [down, swap(down, ALONG_Z[0], ALONG_Z[1])]
@@ -550,7 +580,7 @@
         a_pieces = [pieces[0], a_far, pieces[1], swap(a_far, CORES)]
         c_pieces = [down, swap(down, ALONG_Z[1], ALONG_Z[0])]
     else:
-        own_near = own_far = own_down = jnp.arange(SLOTS, dtype=jnp.int32)
+        own_near = own_far = own_down = own_up = jnp.arange(SLOTS, dtype=jnp.int32)
         edges = neighbours(jnp.stack([tokens, cotangent]), "tensor", EDGE)
         qkv, out, vec = (lax.all_gather(a, BOTH, axis=1, tiled=True).T for a in (w_qkv, w_out, vectors))
         vec = jnp.pad(vec, ((0, 0), (0, D - vec.shape[1])))
@@ -569,8 +599,6 @@
     edges = jnp.concatenate(edges, axis=2).reshape(2, CLIPS * BAND, D)
     x = jnp.concatenate([tokens.reshape(OWN_ALL, D), edges[0]], axis=0)
     cot = jnp.concatenate([cotangent.reshape(OWN_ALL, D), edges[1]], axis=0)
-    if near:
-        x, *c_pieces = lax.optimization_barrier((x, *c_pieces))
     proj, probs, mixed, scaled, wqkv, vec = call(
         attend_kernel, [own_far, keep, x, *a_pieces],
         [
@@ -578,11 +606,12 @@
             ((3 * D, D), bf16), ((16, D), f32),
         ],
         [((D, 128), f32), ((HALF, HALF), bf16), ((BAND, HALF), f32), ((ROWS, D), bf16)],
-        6, 20,
+        0.1, 20,
     )
     if near:
-        b_far = after(b_far, proj)
+        b_far, c_pieces, proj = lax.optimization_barrier((b_far, c_pieces, proj))
         b_pieces = [pieces[0], b_far, pieces[1], swap(b_far, CORES)]
+        c_pieces = both_cores(c_pieces)
     dn_kept, dn_sent, resid, hid, slope, second, branch_low, up_all, wout = call(
         up_kernel, [own_far, own_down, keep, cot, x, mixed, vec, *b_pieces],
         [
@@ -590,20 +619,18 @@
             ((ROWS, FF), bf16), ((ROWS, D), bf16), ((ROWS, D), bf16), ((D, FF), bf16), ((D, D), bf16),
         ],
         [
-            ((D, FF), bf16), ((ROWS, FF), f32), ((D, OWN_ALL), bf16), ((ROWS, D), f32), ((ROWS, D), bf16),
+            ((CHUNKS, D, D), bf16), ((ROWS, FF), f32), ((D, OWN_ALL), bf16), ((ROWS, D), f32), ((ROWS, D), bf16),
         ],
         8, 30,
     )
-    if near:
-        c_pieces = both_cores(c_pieces)
     up_kept, up_sent, branch, gsec, colsum = call(
-        down_kernel, [own_far, own_down, hid, slope, second, branch_low, up_all, *c_pieces],
+        down_kernel, [own_up, own_down, hid, slope, second, branch_low, up_all, *c_pieces],
         [
             ((NEAR, UP_ROWS, D), bf16), ((NEAR, UP_ROWS, D), bf16), ((OWN_ALL, D), f32), ((ROWS, D), f32),
             ((8, D), f32),
         ],
         [
-            ((D, FF), bf16), ((D, FF), bf16), ((ROWS, FF), f32), ((ROWS, FF), bf16), ((D + 16, OWN_ALL), bf16),
+            ((D, FF), bf16), ((CHUNKS, D, D), bf16), ((ROWS, FF), f32), ((ROWS, FF), bf16), ((D + 16, OWN_ALL), bf16),
         ],
         8, 30,
     )
@@ -613,60 +640,71 @@
         up_sum = wide(up_kept) + wide(swap(up_sent, CORES))
         up_far = up_sum[NEAR // 2 :].astype(bf16)
         gsec, up_far, dn_far = lax.optimization_barrier((gsec, up_far, dn_far))
-    out, gres, go_kept, go_sent, gmix, sums = call(
-        finish_kernel, [own_far, keep, cot, mixed, resid, branch, gsec, wout, vec],
+    out, gres, gout, gmix, sums = call(
+        finish_kernel, [keep, cot, mixed, resid, branch, gsec, wout, vec],
         [
-            ((OWN_ALL, D), bf16), ((ROWS, D), f32), ((NEAR, OUT_ROWS, D), bf16), ((NEAR, OUT_ROWS, D), bf16),
-            ((ROWS, D), bf16), ((8, D), f32),
+            ((OWN_ALL, D), bf16), ((ROWS, D), f32), ((D, D), bf16), ((ROWS, D), bf16), ((8, D), f32),
         ],
-        [((ROWS, D), bf16), ((D, D), bf16)],
-        5, 16,
+        [((ROWS, D), bf16)],
+        0.1, 16,
+    )
+    (gproj,) = call(
+        back_kernel, [gmix, proj, probs], [((ROWS, 3 * D), bf16)],
+        [((HALF, HALF), bf16), ((CLIPS * BANDS, 2, BAND, HALF), bf16)],
+        0.1, 16,
     )
     if near:
-        go_sum = wide(go_kept) + wide(swap(go_sent, CORES))
-        go_far = go_sum[NEAR // 2 :].astype(bf16)
-        gmix = after(gmix, go_far)
-    gproj, at_kept, at_sent = call(
-        back_kernel, [own_near, gmix, proj, probs, scaled, wqkv, vec, sums, colsum],
-        [((ROWS, 3 * D), bf16), ((NEAR, A_ROWS, D), bf16), ((NEAR, A_ROWS, D), bf16)],
-        [
-            ((HALF, HALF), bf16), ((CLIPS * BANDS, 2, BAND, HALF), bf16), ((3 * D, D), bf16),
-            ((128, D), f32), ((D, 128), bf16),
-        ],
-        20, 20,
+        up_arrived, gproj = lax.optimization_barrier((swap(up_far, ALONG_X, ALONG_Y), gproj))
+        up_sum = up_sum[: NEAR // 2] + wide(up_arrived)
+        up_near, gproj = lax.optimization_barrier((up_sum[PIECE:].astype(bf16), gproj))
+    at_kept, at_sent = call(
+        project_kernel, [own_near, gproj, gout, scaled, wqkv, vec, sums, colsum],
+        [((NEAR * G_ROWS + V_ROWS, D), bf16)] * 2,
+        [((3 * D, D), bf16), ((128, D), f32)],
+        0.1, 16,
     )
     if near:
-        dn_arrived = swap(dn_far, ALONG_Z[1], ALONG_Z[0])
-        ff_arrived = [swap(far, ALONG_X, ALONG_Y) for far in (up_far, go_far)]
-        dn_arrived, ff_arrived, gproj, at_sent = lax.optimization_barrier((dn_arrived, ff_arrived, gproj, at_sent))
+        dn_arrived, at_sent = lax.optimization_barrier((swap(dn_far, ALONG_Z[1], ALONG_Z[0]), at_sent))
+        up_arrived, at_arrived, gproj = lax.optimization_barrier(
+            (swap(up_near, ALONG_Y, ALONG_X), swap(at_sent, CORES), gproj)
+        )
+    (gtok,) = call(
+        token_kernel, [gproj, x, gres, wqkv, vec], [((OWN_ALL, D), f32)], [], 0.1, 12,
+    )
+    if near:
+        at_sum, *at_rest = call(
+            share_kernel, [at_kept, at_arrived],
+            [((PIECE * G_ROWS + V_ROWS, D), t) for t in (f32, bf16, bf16, bf16)], [], 0.1, 8,
+        )
         dn_sum = dn_sum[: NEAR // 2] + wide(dn_arrived)
-        dn_sum = dn_sum[:PIECE] + wide(swap(dn_sum[PIECE:].astype(bf16), ALONG_Z[0], ALONG_Z[1]))
-        dn_sum = dn_sum[:2] + wide(swap(dn_sum[2:].astype(bf16), ALONG_X, ALONG_Y))
-        dn_sum = dn_sum[0] + wide(swap(dn_sum[1:].astype(bf16), ALONG_Y, ALONG_X))[0]
-        up_sum = up_sum[: NEAR // 2] + wide(ff_arrived[0])
-        go_sum = go_sum[: NEAR // 2] + wide(ff_arrived[1])
-        ff_sum = jnp.concatenate([up_sum, go_sum], axis=1)
-        ff_arrived = swap(ff_sum[PIECE:].astype(bf16), ALONG_Y, ALONG_X)
-        at_sum = wide(at_kept) + wide(swap(at_sent, CORES))
-        at_rest = [at_sum[i : i + PIECE].astype(bf16) for i in range(PIECE, NEAR, PIECE)]
-        gproj = after(gproj, ff_arrived)
-    (gtok,) = call(
-        token_kernel, [gproj, x, gres, wqkv, vec], [((OWN_ALL, D), f32)], [], 5, 12,
-    )
+        up_sum = up_sum[:PIECE] + wide(up_arrived)
+        at_arrived = [swap(piece, mask) for piece, mask in zip(at_rest, ALONG_XY)]
+        ff_arrived = jnp.concatenate([dn_sum[PIECE:], up_sum[2:]], axis=0).astype(bf16)
+        ff_arrived = swap(ff_arrived, ALONG_Z[0], ALONG_Z[1])
+        ff_arrived, gtok = lax.optimization_barrier((ff_arrived, gtok))
+        dn_sum, up_sum = dn_sum[:PIECE] + wide(ff_arrived[:PIECE]), up_sum[:2] + wide(ff_arrived[PIECE:])
+        up_arrived = swap(up_sum[1:].astype(bf16), ALONG_Z[1], ALONG_Z[0])
+        dn_rest = dn_sum.astype(bf16)
+        dn_arrived = [
+            swap(dn_rest[1:2], ALONG_Y, ALONG_X), swap(dn_rest[2:3], ALONG_X, ALONG_Y), swap(dn_rest[3:], ALONG_XY[2]),
+        ]
+        at_arrived, up_arrived = lax.optimization_barrier((at_arrived, up_arrived))
+        at_sum, *at_rest = call(
+            share_kernel, [at_sum, *at_arrived],
+            [((G_ROWS + V_ROWS, D), t) for t in (f32, bf16, bf16, bf16)], [], 0.1, 8,
+        )
+        up_sum = up_sum[0] + wide(up_arrived)[0]
+        dn_sum = add_all(dn_sum[:1], dn_arrived)[0]
+        at_arrived = [swap(piece, mask) for piece, mask in zip(at_rest, ALONG_Z)]
+        g_qkv, g_out, g_vec = call(
+            total_kernel, [device.astype(jnp.int32)[None], at_sum, *at_arrived],
+            [((QKV_ROWS, D), f32), ((OUT_ROWS, D), f32), (vectors.shape, f32)], [], 0.1, 4,
+        )
     if near:
-        ff_sum = ff_sum[:PIECE] + wide(ff_arrived)
-        at_sum = at_sum[:PIECE]
-        for piece, mask in zip(at_rest, ALONG_XY):
-            at_sum = at_sum + wide(after(swap(piece, mask), gtok))
-        ff_sum = scatter_sum(singles(ff_sum), ALONG_Z)[0]
-        at_sum = scatter_sum(singles(at_sum), ALONG_Z)[0]
-    if near:
-        g_up, g_down = ff_sum[:UP_ROWS], dn_sum.T
-        g_out = ff_sum[UP_ROWS:].T
-        g_qkv = at_sum[:QKV_ROWS].T
-        g_vec = at_sum[QKV_ROWS:, : vectors.shape[0]].T
+        g_up, g_down = up_sum, dn_sum.T
+        g_qkv, g_out = g_qkv.T, g_out.T
     else:
-        at_grads = jnp.concatenate([at_kept, at_sent], axis=0)
+        at_grads = jnp.concatenate([a[: NEAR * G_ROWS].reshape(NEAR, G_ROWS, D) for a in (at_kept, at_sent)], axis=0)
 
         def whole(array):
             blocks = array.reshape(SLOTS // CHUNKS, CHUNKS, UP_ROWS, D).transpose(0, 2, 1, 3)
@@ -677,13 +715,12 @@
         g_down = lax.psum_scatter(whole(jnp.concatenate([dn_kept, dn_sent], axis=0)).T, "dp", scatter_dimension=1, tiled=True)
         g_down = lax.psum_scatter(g_down, "tensor", scatter_dimension=0, tiled=True).astype(f32)
 
-        def owned(array, columns):
-            array = array.astype(f32).reshape(-1, D)[:, :columns].T
-            return lax.psum_scatter(array, BOTH, scatter_dimension=1, tiled=True)
-
-        g_qkv = owned(at_grads[:, :QKV_ROWS], D)
-        g_out = owned(jnp.concatenate([go_kept, go_sent], axis=0), D)
-        g_vec = owned(at_grads[:, QKV_ROWS:], vectors.shape[0])
+        def owned(array):
+            return lax.psum_scatter(array.astype(f32), BOTH, scatter_dimension=1, tiled=True)
+
+        g_qkv = owned(at_grads[:, :QKV_ROWS].reshape(-1, D).T)
+        g_out = owned(at_grads[:, QKV_ROWS:].reshape(-1, D).T)
+        g_vec = owned(at_kept[NEAR * G_ROWS :][: vectors.shape[0]])
     shape = tokens.shape
     return (out.reshape(shape), gtok.reshape(shape), g_qkv, g_out, g_vec, g_up, g_down)
 

time: 142 us -> 121 us (0.85)
  waiting for transfers between devices: 54 us -> 35.5 us
  local copies, waits for them, and re-layouts: 9.65 us -> 4.15 us
  starting transfers between devices: 36 us -> 41.3 us
  other arithmetic: 5.43 us -> 2.96 us
    ppermute x35 -> x32, waiting for transfers between devices: 54 us -> 35.5 us  [swap(): lax.ppermute(array, BOTH, [(device, device ^ masks[device % 2]) for devic...]
    ppermute x35 -> x32, starting transfers between devices: 32.8 us -> 38 us  [swap(): lax.ppermute(array, BOTH, [(device, device ^ masks[device % 2]) for devic...]
    unnamed x39 -> x32, local copies, waits for them, and re-layouts: 5.6 us -> 3.26 us
    pallas_call x7 -> x11, Pallas kernels: 35.6 us -> 35.4 us  [call(): pl.pallas_call(kernel, out_shape=[jax.ShapeDtypeStruct(s, t) for s, t in...]
  transfers between devices with their start and end apart: 37 -> 34, of which waited for: 15 -> 12; matrix products, arithmetic and copies ran while one was open for 6% -> 3% of each run, Pallas kernels for 22% -> 29%
where the time goes in v2:
time: 121 us; the launch traced here: 120 us
  starting transfers between devices  41.3 us (34%)
  waiting for transfers between devices  35.5 us (29%)
  Pallas kernels  35.4 us (29%)
  local copies, waits for them, and re-layouts  4.15 us (3%)
  other arithmetic  2.96 us (2%)
    ppermute x32, starting transfers between devices, swap(): lax.ppermute(array, BOTH, [(device, device ^ masks[device % 2]) for devic...  38 us
    ppermute x32, waiting for transfers between devices, swap(): lax.ppermute(array, BOTH, [(device, device ^ masks[device % 2]) for devic...  35.5 us
    pallas_call x11, Pallas kernels, call(): pl.pallas_call(kernel, out_shape=[jax.ShapeDtypeStruct(s, t) for s, t in...  35.4 us
    unnamed x32, local copies, waits for them, and re-layouts  3.26 us
  transfers between devices with their start and end apart: 34, of which 12 were waited for; matrix products, arithmetic and copies ran while one was open for 3% of the time, Pallas kernels for 29%

profile of v2, /device:TPU:0, one launch (start us, length us, event | category | flops | bytes accessed | tf_op | source)
XLA Modules:
  0.0 120.4 jit_solution(7048447942901139604)
XLA Ops:
  3.9 5.1 %collective-permute-start.2 = (bf16[1,144,512]{2,1,0:T(8,128)(2,1)S(1)}, bf16[1,144,512]{2,1,0:T(8,128)(2,1)S(1)}, u32[]{:S(2)}, u32[]{:S(2)}) collective-permute-start(bf16[1,144,512]{2,1,0:T(8,128)(2,1)S(1)} %bitcast.28), channel_id=1, source_target_pairs={{0,24},{1,25},{2,26},{3,27},{4,28},{5,29},{6,30},{7,31},{8,16},{9,... | collective-permute-start | bytes 442376 | tf_op jit(solution)/shard_map/ppermute | solution.py:490
  9.6 1.7 %collective-permute-start.3 = (bf16[1,64,512]{2,1,0:T(8,128)(2,1)S(1)}, bf16[1,64,512]{2,1,0:T(8,128)(2,1)S(1)}, u32[]{:S(2)}, u32[]{:S(2)}) collective-permute-start(bf16[1,64,512]{2,1,0:T(8,128)(2,1)S(1)} %bitcast.43), channel_id=1, source_target_pairs={{0,2},{1,5},{2,0},{3,7},{4,6},{5,1},{6,4},{7,3},{8,10},{9,13},{10,... | collective-permute-start | bytes 196616 | tf_op jit(solution)/shard_map/ppermute | solution.py:490
  11.3 1.3 %collective-permute-start.6 = (bf16[2,4,16,512]{3,2,1,0:T(8,128)(2,1)S(1)}, bf16[2,4,16,512]{3,2,1,0:T(8,128)(2,1)S(1)}, u32[]{:S(2)}, u32[]{:S(2)}) collective-permute-start(bf16[2,4,16,512]{3,2,1,0:T(8,128)(2,1)S(1)} %get-tuple-element.163), channel_id=1, source_target_pairs={{1,0},{2,1},{3,2},{5,4},{6,5},{7,6},{9,8},{10,9},{11,10},{13,12},{... | collective-permute-start | bytes 393224 | tf_op jit(solution)/shard_map/ppermute | solution.py:538
  13.9 2.1 %collective-permute-start.5 = (bf16[2,4,16,512]{3,2,1,0:T(8,128)(2,1)S(1)}, bf16[2,4,16,512]{3,2,1,0:T(8,128)(2,1)S(1)}, u32[]{:S(2)}, u32[]{:S(2)}) collective-permute-start(bf16[2,4,16,512]{3,2,1,0:T(8,128)(2,1)S(1)} %get-tuple-element.164), channel_id=1, source_target_pairs={{0,1},{1,2},{2,3},{4,5},{5,6},{6,7},{8,9},{9,10},{10,11},{12,13},{... | collective-permute-start | bytes 393224 | tf_op jit(solution)/shard_map/ppermute | solution.py:537
  16.0 1.6 %collective-permute-start.4 = (bf16[2,64,512]{2,1,0:T(8,128)(2,1)S(1)}, bf16[2,64,512]{2,1,0:T(8,128)(2,1)S(1)}, u32[]{:S(2)}, u32[]{:S(2)}) collective-permute-start(bf16[2,64,512]{2,1,0:T(8,128)(2,1)S(1)} %pad_maximum_fusion.6), channel_id=1, source_target_pairs={{0,4},{1,3},{2,6},{3,1},{4,0},{5,7},{6,2},{7,5},{8,12},{9,11},{10,... | collective-permute-start | bytes 393224 | tf_op jit(solution)/shard_map/ppermute | solution.py:490
  17.9 3.6 %collective-permute-done.1 = bf16[1,144,512]{2,1,0:T(8,128)(2,1)S(1)} collective-permute-done((bf16[1,144,512]{2,1,0:T(8,128)(2,1)S(1)}, bf16[1,144,512]{2,1,0:T(8,128)(2,1)S(1)}, u32[]{:S(2)}, u32[]{:S(2)}) %collective-permute-start.1) | collective-permute-done | bytes 147488 | tf_op jit(solution)/shard_map/ppermute | solution.py:490
  21.7 1.6 %collective-permute-start.7 = (bf16[4,144,512]{2,1,0:T(8,128)(2,1)S(1)}, bf16[4,144,512]{2,1,0:T(8,128)(2,1)S(1)}, u32[]{:S(2)}, u32[]{:S(2)}) collective-permute-start(bf16[4,144,512]{2,1,0:T(8,128)(2,1)S(1)} %pad_maximum_fusion.2), channel_id=1, source_target_pairs={{0,2},{1,5},{2,0},{3,7},{4,6},{5,1},{6,4},{7,3},{8,10},{9,13},{10,... | collective-permute-start | bytes 1769480 | tf_op jit(solution)/shard_map/ppermute | solution.py:490
  24.2 8.0 %collective-permute-done.8 = bf16[4,64,512]{2,1,0:T(8,128)(2,1)S(1)} collective-permute-done((bf16[4,64,512]{2,1,0:T(8,128)(2,1)S(1)}, bf16[4,64,512]{2,1,0:T(8,128)(2,1)S(1)}, u32[]{:S(2)}, u32[]{:S(2)}) %collective-permute-start.8) | collective-permute-done | bytes 262176 | tf_op jit(solution)/shard_map/ppermute | solution.py:490
  33.4 1.2 %collective-permute-start.12 = (bf16[8,80,512]{2,1,0:T(8,128)(2,1)S(1)}, bf16[8,80,512]{2,1,0:T(8,128)(2,1)S(1)}, u32[]{:S(2)}, u32[]{:S(2)}) collective-permute-start(bf16[8,80,512]{2,1,0:T(8,128)(2,1)S(1)} %slice.107), channel_id=1, source_target_pairs={{0,4},{1,3},{2,6},{3,1},{4,0},{5,7},{6,2},{7,5},{8,12},{9,11},{10,... | collective-permute-start | bytes 1966088 | tf_op jit(solution)/shard_map/ppermute | solution.py:490
  34.7 1.9 %collective-permute-start.13 = (bf16[8,64,512]{2,1,0:T(8,128)(2,1)S(1)}, bf16[8,64,512]{2,1,0:T(8,128)(2,1)S(1)}, u32[]{:S(2)}, u32[]{:S(2)}) collective-permute-start(bf16[8,64,512]{2,1,0:T(8,128)(2,1)S(1)} %constant_dynamic-update-slice_fusion.9.refs_0_), channel_id=1, source_target_pairs={{0,16},{1,9},{2,18},{3,11},{4,20},{5,13},{6,22},{7,15},{8,24},{9,1... | collective-permute-start | bytes 1572872 | tf_op jit(solution)/shard_map/ppermute | solution.py:490
  36.6 5.1 %collective-permute-done.9.refs_1_ = bf16[8,64,512]{2,1,0:T(8,128)(2,1)S(1)} collective-permute-done((bf16[8,64,512]{2,1,0:T(8,128)(2,1)S(1)}, bf16[8,64,512]{2,1,0:T(8,128)(2,1)S(1)}, u32[]{:S(2)}, u32[]{:S(2)}) %collective-permute-start.9) | collective-permute-done | bytes 524320 | tf_op jit(solution)/shard_map/ppermute | solution.py:490
  41.8 1.8 %collective-permute-done.11.refs_3_ = bf16[8,64,512]{2,1,0:T(8,128)(2,1)S(1)} collective-permute-done((bf16[8,64,512]{2,1,0:T(8,128)(2,1)S(1)}, bf16[8,64,512]{2,1,0:T(8,128)(2,1)S(1)}, u32[]{:S(2)}, u32[]{:S(2)}) %collective-permute-start.11) | collective-permute-done | bytes 524320 | tf_op jit(solution)/shard_map/ppermute | solution.py:490
  43.6 6.6 %shard_map.280 = (bf16[640,1536]{1,0:T(8,128)(2,1)S(1)}, f32[20,2,32,256]{3,2,1,0:T(8,128)S(1)}, bf16[640,512]{1,0:T(8,128)(2,1)S(1)}, bf16[640,512]{1,0:T(8,128...) custom-call(s32[32]{0:T(128)S(1)} %get-tuple-element.87.own_ref, ...), custom_call_target="tpu_custom_call" | custom-call | flops 110000000 | bytes 1048576 | tf_op jit(solution)/shard_map/pallas_call | solution.py:476
  51.2 1.4 %collective-permute-done.14.refs_3_ = bf16[8,80,512]{2,1,0:T(8,128)(2,1)S(1)} collective-permute-done((bf16[8,80,512]{2,1,0:T(8,128)(2,1)S(1)}, bf16[8,80,512]{2,1,0:T(8,128)(2,1)S(1)}, u32[]{:S(2)}, u32[]{:S(2)}) %collective-permute-start.14) | collective-permute-done | bytes 655392 | tf_op jit(solution)/shard_map/ppermute | solution.py:490
  52.6 6.6 %shard_map.281 = (bf16[16,64,512]{2,1,0:T(8,128)(2,1)S(1)}, bf16[16,64,512]{2,1,0:T(8,128)(2,1)S(1)}, f32[640,512]{1,0:T(8,128)S(1)}, bf16[640,2048]{1,0:T(8,128...) custom-call(s32[32]{0:T(128)S(1)} %get-tuple-element.87.own_ref, ...), custom_call_target="tpu_custom_call" | custom-call | flops 8800000000 | bytes 1048576 | tf_op jit(solution)/shard_map/pallas_call | solution.py:476
  59.4 6.0 %shard_map.282 = (bf16[16,64,512]{2,1,0:T(8,128)(2,1)S(1)}, bf16[16,64,512]{2,1,0:T(8,128)(2,1)S(1)}, f32[512,512]{1,0:T(8,128)S(1)}, f32[640,512]{1,0:T(8,128)S(1)}, f32[8,512]{1,0:T(8,128)S(1)}) custom-call(s32[32]{0:T(128)S(1)} %get-tuple-element.103.own_ref, s32[32]{0:T(128)S(1)} %get-tuple-element.96.own_down_ref, ...), custom_call_target="tpu_custom_call" | custom-call | flops 8800000000 | bytes 1048576 | tf_op jit(solution)/shard_map/pallas_call | solution.py:476
  66.2 1.9 %collective-permute-done.17 = bf16[16,64,512]{2,1,0:T(8,128)(2,1)S(1)} collective-permute-done((bf16[16,64,512]{2,1,0:T(8,128)(2,1)S(1)}, bf16[16,64,512]{2,1,0:T(8,128)(2,1)S(1)}, u32[]{:S(2)}, u32[]{:S(2)}) %collective-permute-start.17) | collective-permute-done | bytes 1048608 | tf_op jit(solution)/shard_map/ppermute | solution.py:490
  69.3 1.9 %collective-permute-start.19 = (bf16[8,64,512]{2,1,0:T(8,128)(2,1)S(1)}, bf16[8,64,512]{2,1,0:T(8,128)(2,1)S(1)}, u32[]{:S(2)}, u32[]{:S(2)}) collective-permute-start(bf16[8,64,512]{2,1,0:T(8,128)(2,1)S(1)} %slice.147), channel_id=1, source_target_pairs={{0,16},{1,9},{2,18},{3,11},{4,20},{5,13},{6,22},{7,15},{8,24},{9,1... | collective-permute-start | bytes 1572872 | tf_op jit(solution)/shard_map/ppermute | solution.py:490
  71.1 3.5 %shard_map.283 = (bf16[512,512]{1,0:T(8,128)(2,1)}, f32[640,512]{1,0:T(8,128)S(1)}, bf16[512,512]{1,0:T(8,128)(2,1)S(1)}, bf16[640,512]{1,0:T(8,128)(2,1)S(1)}, f32[8,512]{1,0:T(8,128)S(1)}) custom-call(f32[640,128]{1,0:T(8,128)S(1)} %broadcast_in_dim.59.keep_ref, bf16[640,512]{1,0:T(8,128)(2,1)S(1)} %pad_maximum_fusion.cot_ref, ...), custom_call_target="tpu_custom_call" | custom-call | flops 110000000 | bytes 1048576 | tf_op jit(solution)/shard_map/pallas_call | solution.py:476
  74.6 6.0 %shard_map.284.gproj_ref = bf16[640,1536]{1,0:T(8,128)(2,1)S(1)} custom-call(bf16[640,512]{1,0:T(8,128)(2,1)S(1)} %get-tuple-element.124.gmix_ref, bf16[640,1536]{1,0:T(8,128)(2,1)S(1)} %get-tuple-element.125.proj_ref, f32[20,2,32,256]{3,2,1,0:T(8,128)S(1)} %get-tuple-element.126.prob_ref), custom_call_target="tpu_custom_call" | custom-call | flops 110000000 | bytes 1048576 | tf_op jit(solution)/shard_map/pallas_call | solution.py:476
  80.8 2.8 %shard_map.285 = (bf16[1040,512]{1,0:T(8,128)(2,1)S(1)}, bf16[1040,512]{1,0:T(8,128)(2,1)S(1)}) custom-call(s32[32]{0:T(128)S(1)} %get-tuple-element.122.own_ref, bf16[640,1536]{1,0:T(8,128)(2,1)S(1)} %shard_map.284.gproj_ref, bf16[512,512]{1,0:T(8,128)(2,1)S(1)} %get-tuple-element.130.gout_ref, bf16[640,512]{1,0:T(8,128)(2,1)S(1)} %get-tuple-element.131.scaled_ref, ...), custom_call_target="tpu_custom_call" | custom-call | flops 110000000 | bytes 1048576 | tf_op jit(solution)/shard_map/pallas_call | solution.py:476
  84.2 2.5 %collective-permute-start.21 = (bf16[4,64,512]{2,1,0:T(8,128)(2,1)S(1)}, bf16[4,64,512]{2,1,0:T(8,128)(2,1)S(1)}, u32[]{:S(2)}, u32[]{:S(2)}) collective-permute-start(bf16[4,64,512]{2,1,0:T(8,128)(2,1)S(1)} %slice.150), channel_id=1, source_target_pairs={{0,2},{1,5},{2,0},{3,7},{4,6},{5,1},{6,4},{7,3},{8,10},{9,13},{10,... | collective-permute-start | bytes 786440 | tf_op jit(solution)/shard_map/ppermute | solution.py:490
  86.8 4.1 %collective-permute-done.21 = bf16[4,64,512]{2,1,0:T(8,128)(2,1)S(1)} collective-permute-done((bf16[4,64,512]{2,1,0:T(8,128)(2,1)S(1)}, bf16[4,64,512]{2,1,0:T(8,128)(2,1)S(1)}, u32[]{:S(2)}, u32[]{:S(2)}) %collective-permute-start.21) | collective-permute-done | bytes 262176 | tf_op jit(solution)/shard_map/ppermute | solution.py:490
  91.2 1.7 %collective-permute-start.23 = (bf16[6,64,512]{2,1,0:T(8,128)(2,1)S(1)}, bf16[6,64,512]{2,1,0:T(8,128)(2,1)S(1)}, u32[]{:S(2)}, u32[]{:S(2)}) collective-permute-start(bf16[6,64,512]{2,1,0:T(8,128)(2,1)S(1)} %pad_maximum_fusion.3), channel_id=1, source_target_pairs={{0,8},{1,17},{2,10},{3,19},{4,12},{5,21},{6,14},{7,23},{8,0},{9,25... | collective-permute-start | bytes 1179656 | tf_op jit(solution)/shard_map/ppermute | solution.py:490
  95.1 1.5 %collective-permute-start.26 = (bf16[272,512]{1,0:T(8,128)(2,1)S(1)}, bf16[272,512]{1,0:T(8,128)(2,1)S(1)}, u32[]{:S(2)}, u32[]{:S(2)}) collective-permute-start(bf16[272,512]{1,0:T(8,128)(2,1)S(1)} %get-tuple-element.148), channel_id=1, source_target_pairs={{0,6},{1,7},{2,4},{3,5},{4,2},{5,3},{6,0},{7,1},{8,14},{9,15},{10,... | collective-permute-start | bytes 835592 | tf_op jit(solution)/shard_map/ppermute | solution.py:490
  96.6 2.9 %shard_map.286 = f32[512,512]{1,0:T(8,128)} custom-call(bf16[640,1536]{1,0:T(8,128)(2,1)S(1)} %shard_map.284.gproj_ref, bf16[640,512]{1,0:T(8,128)(2,1)S(1)} %pad_maximum_fusion.1.x_ref, f32[640,512]{1,0:T(8,128)S(1)} %get-tuple-element.141.gres_ref, bf16[1536,512]{1,0:T(8,128)(2,1)S(1)} %get-tuple-element.132.wqkv_ref, f32[16,512]{1,0:T(8,128)S(1)} %get-tuple-element.97.vec_ref), custom_call_target="tpu_custom_call" | custom-call | flops 110000000 | bytes 1048576 | tf_op jit(solution)/shard_map/pallas_call | solution.py:476
  99.5 3.2 %collective-permute-done.23 = bf16[6,64,512]{2,1,0:T(8,128)(2,1)S(1)} collective-permute-done((bf16[6,64,512]{2,1,0:T(8,128)(2,1)S(1)}, bf16[6,64,512]{2,1,0:T(8,128)(2,1)S(1)}, u32[]{:S(2)}, u32[]{:S(2)}) %collective-permute-start.23) | collective-permute-done | bytes 393248 | tf_op jit(solution)/shard_map/ppermute | solution.py:490
  102.9 2.2 %collective-permute-start.27 = (bf16[1,64,512]{2,1,0:T(8,128)(2,1)S(1)}, bf16[1,64,512]{2,1,0:T(8,128)(2,1)S(1)}, u32[]{:S(2)}, u32[]{:S(2)}) collective-permute-start(bf16[1,64,512]{2,1,0:T(8,128)(2,1)S(1)} %slice.152), channel_id=1, source_target_pairs={{0,16},{1,9},{2,18},{3,11},{4,20},{5,13},{6,22},{7,15},{8,24},{9,1... | collective-permute-start | bytes 196616 | tf_op jit(solution)/shard_map/ppermute | solution.py:490
  106.2 1.4 %collective-permute-start.33 = (bf16[1,64,512]{2,1,0:T(8,128)(2,1)S(1)}, bf16[1,64,512]{2,1,0:T(8,128)(2,1)S(1)}, u32[]{:S(2)}, u32[]{:S(2)}) collective-permute-start(bf16[1,64,512]{2,1,0:T(8,128)(2,1)S(1)} %get-tuple-element.166), channel_id=1, source_target_pairs={{0,6},{1,7},{2,4},{3,5},{4,2},{5,3},{6,0},{7,1},{8,14},{9,15},{10,... | collective-permute-start | bytes 196616 | tf_op jit(solution)/shard_map/ppermute | solution.py:490
  108.8 2.5 %collective-permute-start.28 = (bf16[80,512]{1,0:T(8,128)(2,1)S(1)}, bf16[80,512]{1,0:T(8,128)(2,1)S(1)}, u32[]{:S(2)}, u32[]{:S(2)}) collective-permute-start(bf16[80,512]{1,0:T(8,128)(2,1)S(1)} %get-tuple-element.154), channel_id=1, source_target_pairs={{0,8},{1,9},{2,10},{3,11},{4,12},{5,13},{6,14},{7,15},{8,0},{9,1},... | collective-permute-start | bytes 245768 | tf_op jit(solution)/shard_map/ppermute | solution.py:490
  111.3 1.6 %collective-permute-start.29 = (bf16[80,512]{1,0:T(8,128)(2,1)S(1)}, bf16[80,512]{1,0:T(8,128)(2,1)S(1)}, u32[]{:S(2)}, u32[]{:S(2)}) collective-permute-start(bf16[80,512]{1,0:T(8,128)(2,1)S(1)} %get-tuple-element.155), channel_id=1, source_target_pairs={{0,16},{1,17},{2,18},{3,19},{4,20},{5,21},{6,22},{7,23},{8,24},{9,... | collective-permute-start | bytes 245768 | tf_op jit(solution)/shard_map/ppermute | solution.py:490
  115.2 4.6 %collective-permute-done.29.refs_2_ = bf16[80,512]{1,0:T(8,128)(2,1)S(1)} collective-permute-done((bf16[80,512]{1,0:T(8,128)(2,1)S(1)}, bf16[80,512]{1,0:T(8,128)(2,1)S(1)}, u32[]{:S(2)}, u32[]{:S(2)}) %collective-permute-start.29) | collective-permute-done | bytes 81952 | tf_op jit(solution)/shard_map/ppermute | solution.py:490
  (122 shorter events, 19.6 us)
Async XLA Ops:
  3.9 14.0 %collective-permute-start.2 = (bf16[1,144,512]{2,1,0:T(8,128)(2,1)S(1)}, bf16[1,144,512]{2,1,0:T(8,128)(2,1)S(1)}, u32[]{:S(2)}, u32[]{:S(2)}) collective-permute-start(bf16[1,144,512]{2,1,0:T(8,128)(2,1)S(1)} %bitcast.28), channel_id=1, source_target_pairs={{0,24},{1,25},{2,26},{3,27},{4,28},{5,29},{6,30},{7,31},{8,16},{9,... | collective-permute-start | bytes 442376 | tf_op jit(solution)/shard_map/ppermute | solution.py:490
  9.0 12.5 %collective-permute-start.1 = (bf16[1,144,512]{2,1,0:T(8,128)(2,1)S(1)}, bf16[1,144,512]{2,1,0:T(8,128)(2,1)S(1)}, u32[]{:S(2)}, u32[]{:S(2)}) collective-permute-start(bf16[1,144,512]{2,1,0:T(8,128)(2,1)S(1)} %bitcast.29), channel_id=1, source_target_pairs={{0,16},{1,17},{2,18},{3,19},{4,20},{5,21},{6,22},{7,23},{8,24},{9,... | collective-permute-start | bytes 442376 | tf_op jit(solution)/shard_map/ppermute | solution.py:490
  9.0 12.5 %collective-permute-start = (bf16[1,144,512]{2,1,0:T(8,128)(2,1)S(1)}, bf16[1,144,512]{2,1,0:T(8,128)(2,1)S(1)}, u32[]{:S(2)}, u32[]{:S(2)}) collective-permute-start(bf16[1,144,512]{2,1,0:T(8,128)(2,1)S(1)} %bitcast.30), channel_id=1, source_target_pairs={{0,8},{1,9},{2,10},{3,11},{4,12},{5,13},{6,14},{7,15},{8,0},{9,1},... | collective-permute-start | bytes 442376 | tf_op jit(solution)/shard_map/ppermute | solution.py:490
  9.6 4.3 %collective-permute-start.3 = (bf16[1,64,512]{2,1,0:T(8,128)(2,1)S(1)}, bf16[1,64,512]{2,1,0:T(8,128)(2,1)S(1)}, u32[]{:S(2)}, u32[]{:S(2)}) collective-permute-start(bf16[1,64,512]{2,1,0:T(8,128)(2,1)S(1)} %bitcast.43), channel_id=1, source_target_pairs={{0,2},{1,5},{2,0},{3,7},{4,6},{5,1},{6,4},{7,3},{8,10},{9,13},{10,... | collective-permute-start | bytes 196616 | tf_op jit(solution)/shard_map/ppermute | solution.py:490
  11.3 4.7 %collective-permute-start.6 = (bf16[2,4,16,512]{3,2,1,0:T(8,128)(2,1)S(1)}, bf16[2,4,16,512]{3,2,1,0:T(8,128)(2,1)S(1)}, u32[]{:S(2)}, u32[]{:S(2)}) collective-permute-start(bf16[2,4,16,512]{3,2,1,0:T(8,128)(2,1)S(1)} %get-tuple-element.163), channel_id=1, source_target_pairs={{1,0},{2,1},{3,2},{5,4},{6,5},{7,6},{9,8},{10,9},{11,10},{13,12},{... | collective-permute-start | bytes 393224 | tf_op jit(solution)/shard_map/ppermute | solution.py:538
  13.9 4.0 %collective-permute-start.5 = (bf16[2,4,16,512]{3,2,1,0:T(8,128)(2,1)S(1)}, bf16[2,4,16,512]{3,2,1,0:T(8,128)(2,1)S(1)}, u32[]{:S(2)}, u32[]{:S(2)}) collective-permute-start(bf16[2,4,16,512]{3,2,1,0:T(8,128)(2,1)S(1)} %get-tuple-element.164), channel_id=1, source_target_pairs={{0,1},{1,2},{2,3},{4,5},{5,6},{6,7},{8,9},{9,10},{10,11},{12,13},{... | collective-permute-start | bytes 393224 | tf_op jit(solution)/shard_map/ppermute | solution.py:537
  16.0 5.4 %collective-permute-start.4 = (bf16[2,64,512]{2,1,0:T(8,128)(2,1)S(1)}, bf16[2,64,512]{2,1,0:T(8,128)(2,1)S(1)}, u32[]{:S(2)}, u32[]{:S(2)}) collective-permute-start(bf16[2,64,512]{2,1,0:T(8,128)(2,1)S(1)} %pad_maximum_fusion.6), channel_id=1, source_target_pairs={{0,4},{1,3},{2,6},{3,1},{4,0},{5,7},{6,2},{7,5},{8,12},{9,11},{10,... | collective-permute-start | bytes 393224 | tf_op jit(solution)/shard_map/ppermute | solution.py:490
  21.7 10.6 %collective-permute-start.7 = (bf16[4,144,512]{2,1,0:T(8,128)(2,1)S(1)}, bf16[4,144,512]{2,1,0:T(8,128)(2,1)S(1)}, u32[]{:S(2)}, u32[]{:S(2)}) collective-permute-start(bf16[4,144,512]{2,1,0:T(8,128)(2,1)S(1)} %pad_maximum_fusion.2), channel_id=1, source_target_pairs={{0,2},{1,5},{2,0},{3,7},{4,6},{5,1},{6,4},{7,3},{8,10},{9,13},{10,... | collective-permute-start | bytes 1769480 | tf_op jit(solution)/shard_map/ppermute | solution.py:490
  23.3 9.0 %collective-permute-start.8 = (bf16[4,64,512]{2,1,0:T(8,128)(2,1)S(1)}, bf16[4,64,512]{2,1,0:T(8,128)(2,1)S(1)}, u32[]{:S(2)}, u32[]{:S(2)}) collective-permute-start(bf16[4,64,512]{2,1,0:T(8,128)(2,1)S(1)} %constant_dynamic-update-slice_fusion.2), channel_id=1, source_target_pairs={{0,8},{1,17},{2,10},{3,19},{4,12},{5,21},{6,14},{7,23},{8,0},{9,25... | collective-permute-start | bytes 786440 | tf_op jit(solution)/shard_map/ppermute | solution.py:490
  32.3 11.3 %collective-permute-start.10 = (bf16[8,144,512]{2,1,0:T(8,128)(2,1)S(1)}, bf16[8,144,512]{2,1,0:T(8,128)(2,1)S(1)}, u32[]{:S(2)}, u32[]{:S(2)}) collective-permute-start(bf16[8,144,512]{2,1,0:T(8,128)(2,1)S(1)} %constant_dynamic-update-slice_fusion.4.refs_0_), channel_id=1, source_target_pairs={{0,1},{1,0},{2,3},{3,2},{4,5},{5,4},{6,7},{7,6},{8,9},{9,8},{10,11... | collective-permute-start | bytes 3538952 | tf_op jit(solution)/shard_map/ppermute | solution.py:490
  32.5 9.2 %collective-permute-start.9 = (bf16[8,64,512]{2,1,0:T(8,128)(2,1)S(1)}, bf16[8,64,512]{2,1,0:T(8,128)(2,1)S(1)}, u32[]{:S(2)}, u32[]{:S(2)}) collective-permute-start(bf16[8,64,512]{2,1,0:T(8,128)(2,1)S(1)} %slice.106), channel_id=1, source_target_pairs={{0,4},{1,3},{2,6},{3,1},{4,0},{5,7},{6,2},{7,5},{8,12},{9,11},{10,... | collective-permute-start | bytes 1572872 | tf_op jit(solution)/shard_map/ppermute | solution.py:490
  33.4 17.1 %collective-permute-start.12 = (bf16[8,80,512]{2,1,0:T(8,128)(2,1)S(1)}, bf16[8,80,512]{2,1,0:T(8,128)(2,1)S(1)}, u32[]{:S(2)}, u32[]{:S(2)}) collective-permute-start(bf16[8,80,512]{2,1,0:T(8,128)(2,1)S(1)} %slice.107), channel_id=1, source_target_pairs={{0,4},{1,3},{2,6},{3,1},{4,0},{5,7},{6,2},{7,5},{8,12},{9,11},{10,... | collective-permute-start | bytes 1966088 | tf_op jit(solution)/shard_map/ppermute | solution.py:490
  34.7 15.8 %collective-permute-start.13 = (bf16[8,64,512]{2,1,0:T(8,128)(2,1)S(1)}, bf16[8,64,512]{2,1,0:T(8,128)(2,1)S(1)}, u32[]{:S(2)}, u32[]{:S(2)}) collective-permute-start(bf16[8,64,512]{2,1,0:T(8,128)(2,1)S(1)} %constant_dynamic-update-slice_fusion.9.refs_0_), channel_id=1, source_target_pairs={{0,16},{1,9},{2,18},{3,11},{4,20},{5,13},{6,22},{7,15},{8,24},{9,1... | collective-permute-start | bytes 1572872 | tf_op jit(solution)/shard_map/ppermute | solution.py:490
  50.5 8.8 %collective-permute-start.15 = (bf16[8,64,512]{2,1,0:T(8,128)(2,1)S(1)}, bf16[8,64,512]{2,1,0:T(8,128)(2,1)S(1)}, u32[]{:S(2)}, u32[]{:S(2)}) collective-permute-start(bf16[8,64,512]{2,1,0:T(8,128)(2,1)S(1)} %constant_dynamic-update-slice_fusion.9.refs_0_), channel_id=1, source_target_pairs={{0,1},{1,0},{2,3},{3,2},{4,5},{5,4},{6,7},{7,6},{8,9},{9,8},{10,11... | collective-permute-start | bytes 1572872 | tf_op jit(solution)/shard_map/ppermute | solution.py:490
  51.1 8.3 %collective-permute-start.16 = (bf16[8,64,512]{2,1,0:T(8,128)(2,1)S(1)}, bf16[8,64,512]{2,1,0:T(8,128)(2,1)S(1)}, u32[]{:S(2)}, u32[]{:S(2)}) collective-permute-start(bf16[8,64,512]{2,1,0:T(8,128)(2,1)S(1)} %collective-permute-done.13.refs_1_), channel_id=1, source_target_pairs={{0,1},{1,0},{2,3},{3,2},{4,5},{5,4},{6,7},{7,6},{8,9},{9,8},{10,11... | collective-permute-start | bytes 1572872 | tf_op jit(solution)/shard_map/ppermute | solution.py:490
  59.1 6.7 %collective-permute-start.18 = (bf16[16,64,512]{2,1,0:T(8,128)(2,1)S(1)}, bf16[16,64,512]{2,1,0:T(8,128)(2,1)S(1)}, u32[]{:S(2)}, u32[]{:S(2)}) collective-permute-start(bf16[16,64,512]{2,1,0:T(8,128)(2,1)S(1)} %get-tuple-element.116), channel_id=1, source_target_pairs={{0,1},{1,0},{2,3},{3,2},{4,5},{5,4},{6,7},{7,6},{8,9},{9,8},{10,11... | collective-permute-start | bytes 3145736 | tf_op jit(solution)/shard_map/ppermute | solution.py:490
  65.4 2.7 %collective-permute-start.17 = (bf16[16,64,512]{2,1,0:T(8,128)(2,1)S(1)}, bf16[16,64,512]{2,1,0:T(8,128)(2,1)S(1)}, u32[]{:S(2)}, u32[]{:S(2)}) collective-permute-start(bf16[16,64,512]{2,1,0:T(8,128)(2,1)S(1)} %get-tuple-element.114), channel_id=1, source_target_pairs={{0,1},{1,0},{2,3},{3,2},{4,5},{5,4},{6,7},{7,6},{8,9},{9,8},{10,11... | collective-permute-start | bytes 3145736 | tf_op jit(solution)/shard_map/ppermute | solution.py:490
  68.5 12.1 %collective-permute-start.20 = (bf16[8,64,512]{2,1,0:T(8,128)(2,1)S(1)}, bf16[8,64,512]{2,1,0:T(8,128)(2,1)S(1)}, u32[]{:S(2)}, u32[]{:S(2)}) collective-permute-start(bf16[8,64,512]{2,1,0:T(8,128)(2,1)S(1)} %slice.148), channel_id=1, source_target_pairs={{0,4},{1,3},{2,6},{3,1},{4,0},{5,7},{6,2},{7,5},{8,12},{9,11},{10,... | collective-permute-start | bytes 1572872 | tf_op jit(solution)/shard_map/ppermute | solution.py:490
  69.3 14.9 %collective-permute-start.19 = (bf16[8,64,512]{2,1,0:T(8,128)(2,1)S(1)}, bf16[8,64,512]{2,1,0:T(8,128)(2,1)S(1)}, u32[]{:S(2)}, u32[]{:S(2)}) collective-permute-start(bf16[8,64,512]{2,1,0:T(8,128)(2,1)S(1)} %slice.147), channel_id=1, source_target_pairs={{0,16},{1,9},{2,18},{3,11},{4,20},{5,13},{6,22},{7,15},{8,24},{9,1... | collective-permute-start | bytes 1572872 | tf_op jit(solution)/shard_map/ppermute | solution.py:490
  84.2 6.8 %collective-permute-start.22 = (bf16[1040,512]{1,0:T(8,128)(2,1)S(1)}, bf16[1040,512]{1,0:T(8,128)(2,1)S(1)}, u32[]{:S(2)}, u32[]{:S(2)}) collective-permute-start(bf16[1040,512]{1,0:T(8,128)(2,1)S(1)} %get-tuple-element.138), channel_id=1, source_target_pairs={{0,1},{1,0},{2,3},{3,2},{4,5},{5,4},{6,7},{7,6},{8,9},{9,8},{10,11... | collective-permute-start | bytes 3194888 | tf_op jit(solution)/shard_map/ppermute | solution.py:490
  84.2 6.8 %collective-permute-start.21 = (bf16[4,64,512]{2,1,0:T(8,128)(2,1)S(1)}, bf16[4,64,512]{2,1,0:T(8,128)(2,1)S(1)}, u32[]{:S(2)}, u32[]{:S(2)}) collective-permute-start(bf16[4,64,512]{2,1,0:T(8,128)(2,1)S(1)} %slice.150), channel_id=1, source_target_pairs={{0,2},{1,5},{2,0},{3,7},{4,6},{5,1},{6,4},{7,3},{8,10},{9,13},{10,... | collective-permute-start | bytes 786440 | tf_op jit(solution)/shard_map/ppermute | solution.py:490
  91.2 11.6 %collective-permute-start.23 = (bf16[6,64,512]{2,1,0:T(8,128)(2,1)S(1)}, bf16[6,64,512]{2,1,0:T(8,128)(2,1)S(1)}, u32[]{:S(2)}, u32[]{:S(2)}) collective-permute-start(bf16[6,64,512]{2,1,0:T(8,128)(2,1)S(1)} %pad_maximum_fusion.3), channel_id=1, source_target_pairs={{0,8},{1,17},{2,10},{3,19},{4,12},{5,21},{6,14},{7,23},{8,0},{9,25... | collective-permute-start | bytes 1179656 | tf_op jit(solution)/shard_map/ppermute | solution.py:490
  93.1 13.1 %collective-permute-start.24 = (bf16[272,512]{1,0:T(8,128)(2,1)S(1)}, bf16[272,512]{1,0:T(8,128)(2,1)S(1)}, u32[]{:S(2)}, u32[]{:S(2)}) collective-permute-start(bf16[272,512]{1,0:T(8,128)(2,1)S(1)} %get-tuple-element.146), channel_id=1, source_target_pairs={{0,2},{1,3},{2,0},{3,1},{4,6},{5,7},{6,4},{7,5},{8,10},{9,11},{10,... | collective-permute-start | bytes 835592 | tf_op jit(solution)/shard_map/ppermute | solution.py:490
  94.0 13.5 %collective-permute-start.25 = (bf16[272,512]{1,0:T(8,128)(2,1)S(1)}, bf16[272,512]{1,0:T(8,128)(2,1)S(1)}, u32[]{:S(2)}, u32[]{:S(2)}) collective-permute-start(bf16[272,512]{1,0:T(8,128)(2,1)S(1)} %get-tuple-element.147), channel_id=1, source_target_pairs={{0,4},{1,5},{2,6},{3,7},{4,0},{5,1},{6,2},{7,3},{8,12},{9,13},{10,... | collective-permute-start | bytes 835592 | tf_op jit(solution)/shard_map/ppermute | solution.py:490
  95.1 13.5 %collective-permute-start.26 = (bf16[272,512]{1,0:T(8,128)(2,1)S(1)}, bf16[272,512]{1,0:T(8,128)(2,1)S(1)}, u32[]{:S(2)}, u32[]{:S(2)}) collective-permute-start(bf16[272,512]{1,0:T(8,128)(2,1)S(1)} %get-tuple-element.148), channel_id=1, source_target_pairs={{0,6},{1,7},{2,4},{3,5},{4,2},{5,3},{6,0},{7,1},{8,14},{9,15},{10,... | collective-permute-start | bytes 835592 | tf_op jit(solution)/shard_map/ppermute | solution.py:490
  102.9 5.8 %collective-permute-start.27 = (bf16[1,64,512]{2,1,0:T(8,128)(2,1)S(1)}, bf16[1,64,512]{2,1,0:T(8,128)(2,1)S(1)}, u32[]{:S(2)}, u32[]{:S(2)}) collective-permute-start(bf16[1,64,512]{2,1,0:T(8,128)(2,1)S(1)} %slice.152), channel_id=1, source_target_pairs={{0,16},{1,9},{2,18},{3,11},{4,20},{5,13},{6,22},{7,15},{8,24},{9,1... | collective-permute-start | bytes 196616 | tf_op jit(solution)/shard_map/ppermute | solution.py:490
  105.1 7.9 %collective-permute-start.31 = (bf16[1,64,512]{2,1,0:T(8,128)(2,1)S(1)}, bf16[1,64,512]{2,1,0:T(8,128)(2,1)S(1)}, u32[]{:S(2)}, u32[]{:S(2)}) collective-permute-start(bf16[1,64,512]{2,1,0:T(8,128)(2,1)S(1)} %get-tuple-element.165), channel_id=1, source_target_pairs={{0,2},{1,5},{2,0},{3,7},{4,6},{5,1},{6,4},{7,3},{8,10},{9,13},{10,... | collective-permute-start | bytes 196616 | tf_op jit(solution)/shard_map/ppermute | solution.py:490
  106.2 7.6 %collective-permute-start.33 = (bf16[1,64,512]{2,1,0:T(8,128)(2,1)S(1)}, bf16[1,64,512]{2,1,0:T(8,128)(2,1)S(1)}, u32[]{:S(2)}, u32[]{:S(2)}) collective-permute-start(bf16[1,64,512]{2,1,0:T(8,128)(2,1)S(1)} %get-tuple-element.166), channel_id=1, source_target_pairs={{0,6},{1,7},{2,4},{3,5},{4,2},{5,3},{6,0},{7,1},{8,14},{9,15},{10,... | collective-permute-start | bytes 196616 | tf_op jit(solution)/shard_map/ppermute | solution.py:490
  107.5 6.3 %collective-permute-start.32 = (bf16[1,64,512]{2,1,0:T(8,128)(2,1)S(1)}, bf16[1,64,512]{2,1,0:T(8,128)(2,1)S(1)}, u32[]{:S(2)}, u32[]{:S(2)}) collective-permute-start(bf16[1,64,512]{2,1,0:T(8,128)(2,1)S(1)} %get-tuple-element.167), channel_id=1, source_target_pairs={{0,4},{1,3},{2,6},{3,1},{4,0},{5,7},{6,2},{7,5},{8,12},{9,11},{10,... | collective-permute-start | bytes 196616 | tf_op jit(solution)/shard_map/ppermute | solution.py:490
  108.8 6.4 %collective-permute-start.28 = (bf16[80,512]{1,0:T(8,128)(2,1)S(1)}, bf16[80,512]{1,0:T(8,128)(2,1)S(1)}, u32[]{:S(2)}, u32[]{:S(2)}) collective-permute-start(bf16[80,512]{1,0:T(8,128)(2,1)S(1)} %get-tuple-element.154), channel_id=1, source_target_pairs={{0,8},{1,9},{2,10},{3,11},{4,12},{5,13},{6,14},{7,15},{8,0},{9,1},... | collective-permute-start | bytes 245768 | tf_op jit(solution)/shard_map/ppermute | solution.py:490
  111.3 8.4 %collective-permute-start.29 = (bf16[80,512]{1,0:T(8,128)(2,1)S(1)}, bf16[80,512]{1,0:T(8,128)(2,1)S(1)}, u32[]{:S(2)}, u32[]{:S(2)}) collective-permute-start(bf16[80,512]{1,0:T(8,128)(2,1)S(1)} %get-tuple-element.155), channel_id=1, source_target_pairs={{0,16},{1,17},{2,18},{3,19},{4,20},{5,21},{6,22},{7,23},{8,24},{9,... | collective-permute-start | bytes 245768 | tf_op jit(solution)/shard_map/ppermute | solution.py:490
  113.0 6.8 %collective-permute-start.30 = (bf16[80,512]{1,0:T(8,128)(2,1)S(1)}, bf16[80,512]{1,0:T(8,128)(2,1)S(1)}, u32[]{:S(2)}, u32[]{:S(2)}) collective-permute-start(bf16[80,512]{1,0:T(8,128)(2,1)S(1)} %get-tuple-element.156), channel_id=1, source_target_pairs={{0,24},{1,25},{2,26},{3,27},{4,28},{5,29},{6,30},{7,31},{8,16},{9,... | collective-permute-start | bytes 245768 | tf_op jit(solution)/shard_map/ppermute | solution.py:490
  (14 other events, 80.8 us)

commit v3 on v2

--- a/solution.py
+++ b/solution.py
@@ -34,6 +34,8 @@
 B_ROWS = OUT_ROWS + UP_ROWS
 G_ROWS = QKV_ROWS + OUT_ROWS
 V_ROWS = 16
+AT_ROWS = SLOTS // 2 * G_ROWS + V_ROWS
+PARTS = 5
 
 CLIPS = 4
 OWN = 128
@@ -82,12 +84,11 @@
     return inverse * (grad_hat - centre - scaled * slope)
 
 
-def band_rows(band):
-    clip = band // BANDS
-    place = band % BANDS
-    first = jnp.where(place == 0, OWN_ALL + clip * BAND, clip * OWN + place * BAND - EDGE)
-    last = jnp.where(place == BANDS - 1, OWN_ALL + clip * BAND + EDGE, clip * OWN + place * BAND)
-    return rows_at(first, EDGE), rows_at(last, EDGE)
+def band_places(band):
+    clip, place = divmod(band, BANDS)
+    first = OWN_ALL + clip * BAND if place == 0 else clip * OWN + place * BAND - EDGE
+    last = OWN_ALL + clip * BAND + EDGE if place == BANDS - 1 else clip * OWN + place * BAND
+    return slice(first, first + EDGE), slice(last, last + EDGE)
 
 
 def load_band(ref, places, columns):
@@ -103,12 +104,24 @@
     return rows_at(owner // CHUNKS * UP_ROWS, UP_ROWS), rows_at(owner % CHUNKS * D, D)
 
 
-def pack_kernel(qkv_ref, vec_ref, out_ref, up_ref, block_ref):
-    block_ref[:QKV_ROWS, :] = qkv_ref[...]
+def pack_kernel(qkv_ref, vec_ref, out_ref, up_ref, block_ref, rows_ref, sems):
+    here = (
+        rows_ref, block_ref.at[:QKV_ROWS], block_ref.at[A_ROWS : A_ROWS + OUT_ROWS], block_ref.at[A_ROWS + OUT_ROWS :],
+    )
+    copies = [
+        pltpu.make_async_copy(there, place, sems.at[i])
+        for i, (there, place) in enumerate(zip((vec_ref, qkv_ref, out_ref, up_ref), here))
+    ]
+    for copy in copies:
+        copy.start()
     block_ref[QKV_ROWS:A_ROWS, :] = jnp.zeros((OUT_ROWS, D), bf16)
-    block_ref[QKV_ROWS:A_ROWS, : vec_ref.shape[1]] = vec_ref[...]
-    block_ref[A_ROWS : A_ROWS + OUT_ROWS, :] = out_ref[...]
-    block_ref[A_ROWS + OUT_ROWS :, :] = up_ref[...]
+    row = lax.broadcasted_iota(jnp.int32, (OUT_ROWS, OUT_ROWS), 0)
+    lane = lax.broadcasted_iota(jnp.int32, (OUT_ROWS, OUT_ROWS), 1)
+    copies[0].wait()
+    turned = nt(jnp.where(row == lane, 1.0, 0.0).astype(bf16), rows_ref[...])
+    block_ref[QKV_ROWS:A_ROWS, : vec_ref.shape[0]] = turned.astype(bf16)
+    for copy in copies[1:]:
+        copy.wait()
 
 
 def head_lanes():
@@ -142,14 +155,11 @@
     query_group = (lax.broadcasted_iota(jnp.int32, (BAND, HALF), 1) % FREQ + SHIFT) // WINDOW
     pair_ref[...] = jnp.where(key_group == query_group, 1.0, 0.0)
 
-    def scale(step, carry):
-        here = rows_at(step * SUB, SUB)
+    for step in range(ROWS // SUB):
+        here = slice(step * SUB, (step + 1) * SUB)
         scaled, _ = norm_parts(x_ref[here, :].astype(f32))
         scaled_ref[here, :] = scaled.astype(bf16)
         normed_ref[here, :] = (scaled * vec_ref[0:1, :] + vec_ref[1:2, :]).astype(bf16)
-        return carry
-
-    lax.fori_loop(0, ROWS // SUB, scale, 0, unroll=4)
     for part in range(3):
         columns = slice(part * D, (part + 1) * D)
         part_out = nt(normed_ref[...], wqkv_ref[columns, :])
@@ -158,8 +168,8 @@
             part_out = part_out + vec_ref[bias : bias + 1, :]
         proj_ref[:, columns] = part_out.astype(bf16)
 
-    def score(band, carry):
-        places = band_rows(band)
+    for band in range(CLIPS * BANDS):
+        places = band_places(band)
         key_ok = load_band(keep_ref, places, slice(None))
         key_ok = jnp.concatenate([key_ok, key_ok], axis=1) * pair_ref[...] > 0.5
         for half in range(2):
@@ -170,12 +180,8 @@
             scores = jnp.where(key_ok, scores, MASKED)
             exponent = jnp.exp(scores - jnp.max(scores, axis=0, keepdims=True))
             prob_ref[band, half] = exponent / jnp.sum(exponent, axis=0, keepdims=True)
-        return carry
-
-    lax.fori_loop(0, CLIPS * BANDS, score, 0, unroll=10)
-
-    def mix(band, carry):
-        places = band_rows(band)
+    for band in range(CLIPS * BANDS):
+        places = band_places(band)
         for half in range(2):
             low = half * HALF
             value = load_band(proj_ref, places, slice(2 * D + low, 2 * D + low + HALF))
@@ -183,9 +189,6 @@
             mixed = nn(probs, by_head(value, lanes_ref[...])).astype(bf16)
             mixed_ref[places[0], low : low + HALF] = mixed[:EDGE]
             mixed_ref[places[1], low : low + HALF] = mixed[EDGE:]
-        return carry
-
-    lax.fori_loop(0, CLIPS * BANDS, mix, 0, unroll=10)
 
 
 def together(*works):
@@ -218,8 +221,8 @@
 
     attended_ref[...] = nt(mixed_ref[...], wout_ref[...])
 
-    def begin(step, carry):
-        here = rows_at(step * SUB, SUB)
+    for step in range(ROWS // SUB):
+        here = slice(step * SUB, (step + 1) * SUB)
         residual = x_ref[here, :].astype(f32) + (attended_ref[here, :] + vec_ref[4:5, :])
         resid_ref[here, :] = residual
         scaled, _ = norm_parts(residual)
@@ -228,23 +231,22 @@
         normed_ref[here, :] = second
         wide = jnp.concatenate([keep_ref[here, :]] * (D // 128), axis=1)
         branch_low[here, :] = (cot_ref[here, :].astype(f32) * wide).astype(bf16)
-        return carry
-
-    lax.fori_loop(0, ROWS // SUB, begin, 0, unroll=4)
     branch_t[...] = branch_low[:OWN_ALL, :].T
 
     def products(chunk):
         for half in range(2):
             columns = slice(chunk * D + half * HALF, chunk * D + (half + 1) * HALF)
-            pre_ref[:, columns] = nn(normed_ref[...], up_ref[:, columns])
+            ring = slice(chunk % 2 * D + half * HALF, chunk % 2 * D + (half + 1) * HALF)
+            pre_ref[:, ring] = nn(normed_ref[...], up_ref[:, columns])
             yield
             yield
 
     def slopes(chunk):
         columns = slice(chunk * D, (chunk + 1) * D)
+        ring = slice(chunk % 2 * D, chunk % 2 * D + D)
         for step in range(ROWS // 16):
             here = slice(step * 16, step * 16 + 16)
-            pre = pre_ref[here, columns] + vec_ref[8 + chunk : 9 + chunk, :]
+            pre = pre_ref[here, ring] + vec_ref[8 + chunk : 9 + chunk, :]
             phi = 0.5 + 0.5 * lax.erf(pre * INV_ROOT_TWO)
             slope_ref[here, columns] = (phi + pre * (jnp.exp(-0.5 * pre * pre) * INV_ROOT_TAU)).astype(bf16)
             hid_ref[here, columns] = (pre * phi).astype(bf16)
@@ -269,12 +271,12 @@
 
 
 def down_kernel(
-    own_ref, own_down_ref, hid_ref, slope_ref, second_ref, branch_low, up_ref, *refs,
+    own_ref, own_down_ref, slope_ref, second_ref, branch_low, *refs,
 ):
-    c_refs, refs = refs[:-10], refs[-10:]
+    c_refs, refs = refs[:-8], refs[-8:]
     (
-        kept_ref, sent_ref, branch_ref, gsec_ref, colsum_ref,
-        down_ref, gup_ref, ghid_ref, gpre_ref, second_t,
+        kept_ref, sent_ref, gpre_ref, down_ref, colsum_ref,
+        gup_ref, ghid_ref, second_t,
     ) = refs
     for slot in range(SLOTS):
         c_ref, held = find(c_refs, slot)
@@ -285,15 +287,17 @@
     def products(chunk):
         for half in range(2):
             columns = slice(chunk * D + half * HALF, chunk * D + (half + 1) * HALF)
-            ghid_ref[:, columns] = nn(branch_low[...], down_ref[:, columns])
+            ring = slice(chunk % 2 * D + half * HALF, chunk % 2 * D + (half + 1) * HALF)
+            ghid_ref[:, ring] = nn(branch_low[...], down_ref[:, columns])
             yield
             yield
 
     def slopes(chunk):
         columns = slice(chunk * D, (chunk + 1) * D)
+        ring = slice(chunk % 2 * D, chunk % 2 * D + D)
         for step in range(ROWS // 16):
             here = slice(step * 16, step * 16 + 16)
-            gpre_ref[here, columns] = (ghid_ref[here, columns] * slope_ref[here, columns].astype(f32)).astype(bf16)
+            gpre_ref[here, columns] = (ghid_ref[here, ring] * slope_ref[here, columns].astype(f32)).astype(bf16)
             if step % 10 == 9:
                 yield
 
@@ -312,9 +316,12 @@
         together(products(chunk), slopes(chunk - 1), weights(chunk - 2))
     together(slopes(CHUNKS - 1), weights(CHUNKS - 2))
     together(weights(CHUNKS - 1))
+    write_grads(own_ref, (kept_ref, sent_ref), gup_ref)
+
+
+def sum_kernel(hid_ref, gpre_ref, up_ref, down_ref, branch_ref, gsec_ref):
     branch_ref[...] = nt(hid_ref[:OWN_ALL, :], down_ref[...])
     gsec_ref[...] = nt(gpre_ref[...], up_ref[...])
-    write_grads(own_ref, (kept_ref, sent_ref), gup_ref)
 
 
 def finish_kernel(
@@ -322,9 +329,9 @@
     out_ref, gres_ref, gout_ref, gmix_ref, sums_ref,
     gatt_ref,
 ):
-    def rows(step, totals):
-        here = rows_at(step * SUB, SUB)
-        own = jnp.where(step < OWN_ALL // SUB, 1.0, 0.0)
+    totals = [jnp.zeros((8, D), f32)] * 4
+    for step in range(ROWS // SUB):
+        here = slice(step * SUB, (step + 1) * SUB)
         wide = jnp.concatenate([keep_ref[here, :]] * (D // 128), axis=1)
         scaled, inverse = norm_parts(resid_ref[here, :])
         grad_out = cot_ref[here, :].astype(f32) * wide
@@ -333,29 +340,22 @@
         gres_ref[here, :] = gres
         gatt = gres.astype(bf16)
         gatt_ref[here, :] = gatt
-        parts = (gatt.astype(f32), gsec * scaled, gsec, grad_out.astype(bf16).astype(f32))
-        return tuple(t + own * p.reshape(SUB // 8, 8, D).sum(axis=0) for t, p in zip(totals, parts))
-
-    totals = lax.fori_loop(0, ROWS // SUB, rows, (jnp.zeros((8, D), f32),) * 4, unroll=4)
+        if step < OWN_ALL // SUB:
+            parts = (gatt.astype(f32), gsec * scaled, gsec, grad_out.astype(bf16).astype(f32))
+            totals = [t + p.reshape(SUB // 8, 8, D).sum(axis=0) for t, p in zip(totals, parts)]
+            branch = branch_ref[here, :] + vec_ref[7:8, :]
+            out_ref[here, :] = (wide * (resid_ref[here, :] + branch)).astype(bf16)
     for place, total in enumerate(totals):
         sums_ref[place : place + 1, :] = jnp.sum(total, axis=0, keepdims=True)
     gmix_ref[...] = nn(gatt_ref[...], wout_ref[...]).astype(bf16)
     gout_ref[...] = nn(gatt_ref[:OWN_ALL, :].T, mixed_ref[:OWN_ALL, :]).astype(bf16)
 
-    def outputs(step, carry):
-        here = rows_at(step * SUB, SUB)
-        wide = jnp.concatenate([keep_ref[here, :]] * (D // 128), axis=1)
-        out_ref[here, :] = (wide * (resid_ref[here, :] + (branch_ref[here, :] + vec_ref[7:8, :]))).astype(bf16)
-        return carry
-
-    lax.fori_loop(0, OWN_ALL // SUB, outputs, 0, unroll=4)
-
-
-def back_kernel(gmix_ref, proj_ref, prob_ref, gproj_ref, lanes_ref, gscore_ref):
+
+def back_kernel(clips, gmix_ref, proj_ref, prob_ref, gproj_ref, lanes_ref, gscore_ref):
     lanes_ref[...] = head_lanes().astype(bf16)
-
-    def score(band, carry):
-        places = band_rows(band)
+    bands = range(clips[0] * BANDS, (clips[-1] + 1) * BANDS)
+    for band in bands:
+        places = band_places(band)
         for half in range(2):
             low = half * HALF
             value = load_band(proj_ref, places, slice(2 * D + low, 2 * D + low + HALF))
@@ -363,47 +363,43 @@
             probs = prob_ref[band, half]
             grad_probs = nt(value, by_head(grad, lanes_ref[...]))
             row_dot = jnp.sum(probs * grad_probs, axis=0, keepdims=True)
-            gscore_ref[band, half] = (probs * (grad_probs - row_dot)).astype(bf16)
-        return carry
-
-    lax.fori_loop(0, CLIPS * BANDS, score, 0, unroll=10)
-
-    def mix(band, carry):
-        places = band_rows(band)
+            gscore_ref[band - bands[0], half] = (probs * (grad_probs - row_dot)).astype(bf16)
+    for band in bands:
+        places = band_places(band)
         for half in range(2):
             low = half * HALF
             query = load_band(proj_ref, places, slice(low, low + HALF))
             key = load_band(proj_ref, places, slice(D + low, D + low + HALF))
             grad = load_band(gmix_ref, places, slice(low, low + HALF))
-            grad_scores = gscore_ref[band, half]
+            grad_scores = gscore_ref[band - bands[0], half]
             grad_key = nn(grad_scores, by_head(query, lanes_ref[...])) * SCALE
             grad_value = nn(prob_ref[band, half].astype(bf16), by_head(grad, lanes_ref[...]))
             grad_query = nn(flip_heads(grad_scores), by_head(key, lanes_ref[...])) * SCALE
             for part, values in enumerate((grad_query, grad_key, grad_value)):
                 values = values.astype(bf16)
-                gproj_ref[places[0], part * D + low : part * D + low + HALF] = values[:EDGE]
-                gproj_ref[places[1], part * D + low : part * D + low + HALF] = values[EDGE:]
-        return carry
-
-    lax.fori_loop(0, CLIPS * BANDS, mix, 0, unroll=10)
+                for rows, place in ((values[:EDGE], places[0]), (values[EDGE:], places[1])):
+                    if place.start < OWN_ALL:
+                        start = place.start - clips[0] * OWN
+                        gproj_ref[start : start + EDGE, part * D + low : part * D + low + HALF] = rows
 
 
 def project_kernel(
-    own_ref, gproj_ref, gout_ref, scaled_ref, wqkv_ref, vec_ref, sums_ref, colsum_ref,
-    kept_ref, sent_ref,
-    gqkv_ref, gvec_ref,
+    own_ref, gproj_a, gproj_b, gout_ref, scaled_ref, wqkv_ref, vec_ref, sums_ref, colsum_ref,
+    kept_ref, *refs,
 ):
-    def add_rows(step, totals):
-        here = rows_at(step * SUB, SUB)
-        return totals + gproj_ref[here, :].astype(f32).reshape(SUB // 8, 8, 3 * D).sum(axis=0)
-
-    totals = lax.fori_loop(0, OWN_ALL // SUB, add_rows, jnp.zeros((8, 3 * D), f32))
+    *sent_refs, gqkv_ref, gvec_ref = refs
+    totals = jnp.zeros((8, 3 * D), f32)
+    for step in range(OWN_ALL // 2 // SUB):
+        here = slice(step * SUB, (step + 1) * SUB)
+        for gproj_ref in (gproj_a, gproj_b):
+            totals = totals + gproj_ref[here, :].astype(f32).reshape(SUB // 8, 8, 3 * D).sum(axis=0)
     totals = jnp.sum(totals, axis=0, keepdims=True)
     gvec_ref[...] = jnp.zeros_like(gvec_ref)
     gain_grad = jnp.zeros((8, D), f32)
     shift_grad = jnp.zeros((1, D), f32)
     for part in range(3):
-        gproj_t = gproj_ref[:OWN_ALL, part * D : (part + 1) * D].T
+        columns = slice(part * D, (part + 1) * D)
+        gproj_t = jnp.concatenate([gproj_a[:, columns].T, gproj_b[:, columns].T], axis=1)
         product = nn(gproj_t, scaled_ref[:OWN_ALL, :])
         total = totals[:, part * D : (part + 1) * D]
         weight = wqkv_ref[part * D : (part + 1) * D, :]
@@ -423,41 +419,51 @@
     gvec_ref[8:12, :] = colsum_ref[0:4, :]
     for slot in range(SLOTS):
         owner = own_ref[slot]
-        grads_ref, held = (kept_ref, sent_ref)[slot // NEAR], slot % NEAR * G_ROWS
-        grads_ref[held : held + QKV_ROWS, :] = gqkv_ref[rows_at(owner * QKV_ROWS, QKV_ROWS), :]
-        grads_ref[held + QKV_ROWS : held + G_ROWS, :] = gout_ref[rows_at(owner * OUT_ROWS, OUT_ROWS), :]
-    for grads_ref in (kept_ref, sent_ref):
-        grads_ref[NEAR * G_ROWS :, :] = gvec_ref[:V_ROWS, :].astype(bf16)
-
-
-def share_kernel(*refs):
-    *pieces, kept_ref, first_ref, second_ref, third_ref = refs
-    size = kept_ref.shape[0] - V_ROWS
-
-    def total(rows):
-        result = pieces[0][rows, :].astype(f32)
-        for piece in pieces[1:]:
-            result = result + piece[rows, :].astype(f32)
+        held = slot % NEAR * G_ROWS
+        for low in range(0, G_ROWS, 16):
+            if low < QKV_ROWS:
+                rows = gqkv_ref[rows_at(owner * QKV_ROWS + low, 16), :]
+            else:
+                rows = gout_ref[rows_at(owner * OUT_ROWS + low - QKV_ROWS, 16), :]
+            grads_ref, place = find_row([kept_ref] if slot < NEAR else sent_refs, held + low)
+            grads_ref[place : place + 16, :] = rows
+    for refs in ([kept_ref], sent_refs):
+        grads_ref, place = find_row(refs, NEAR * G_ROWS)
+        grads_ref[place : place + V_ROWS, :] = gvec_ref[:V_ROWS, :].astype(bf16)
+
+
+def find_row(pieces, row):
+    for piece in pieces:
+        if row < piece.shape[0]:
+            return piece, row
+        row -= piece.shape[0]
+
+
+def share_kernel(first_ref, *refs, end_to_end=False):
+    pieces, outs = refs[:-4], refs[-4:]
+    size = outs[0].shape[0] - V_ROWS
+
+    def total(start):
+        result = first_ref[start : start + 16, :].astype(f32)
+        for found, row in [find_row(pieces, start)] if end_to_end else [(piece, start) for piece in pieces]:
+            result = result + found[row : row + 16, :].astype(f32)
         return result
 
-    vectors = total(slice(4 * size, 4 * size + V_ROWS))
-    for part, out_ref in enumerate((kept_ref, first_ref, second_ref, third_ref)):
-        for low in range(0, size, 64):
-            out_ref[low : low + 64, :] = total(slice(part * size + low, part * size + low + 64)).astype(out_ref.dtype)
+    vectors = total(4 * size)
+    for part, out_ref in enumerate(outs):
+        for low in range(0, size, 16):
+            out_ref[low : low + 16, :] = total(part * size + low).astype(out_ref.dtype)
         out_ref[size:, :] = vectors.astype(out_ref.dtype)
 
 
-def token_kernel( gproj_ref, x_ref, gres_ref, wqkv_ref, vec_ref, gtok_ref):
-    def rows(step, carry):
-        here = rows_at(step * STEP, STEP)
-        gnormed = nn(gproj_ref[here, :D], wqkv_ref[:D, :])
-        for part in range(1, 3):
-            gnormed += nn(gproj_ref[here, part * D : (part + 1) * D], wqkv_ref[part * D : (part + 1) * D, :])
+def token_kernel(gproj_a, gproj_b, x_ref, gres_ref, wqkv_ref, vec_ref, gtok_ref):
+    for step in range(OWN_ALL // STEP):
+        here = slice(step * STEP, (step + 1) * STEP)
+        gproj_ref, steps = (gproj_a, gproj_b)[step * STEP * 2 // OWN_ALL], OWN_ALL // 2 // STEP
+        rows = slice(step % steps * STEP, (step % steps + 1) * STEP)
+        gnormed = nn(gproj_ref[rows, :], wqkv_ref[...])
         scaled, inverse = norm_parts(x_ref[here, :].astype(f32))
         gtok_ref[here, :] = gres_ref[here, :] + norm_back(gnormed, scaled, inverse, vec_ref[0:1, :])
-        return carry
-
-    lax.fori_loop(0, OWN_ALL // STEP, rows, 0)
 
 
 def total_kernel(device_ref, *refs):
@@ -557,21 +563,26 @@
         device = lax.axis_index("dp") * devices_t + rank
         own_near, own_far = owners(device, False), owners(device, True)
         own_down, own_up = owners(device, True, False, 0), owners(device, True, True, 1)
-        (block,) = call(
-            pack_kernel, [w_qkv.T, vectors.T, w_out.T, w_up], [((A_ROWS + B_ROWS, D), bf16)], [], 1, 4,
-        )
+        block = pl.pallas_call(
+            pack_kernel,
+            out_shape=jax.ShapeDtypeStruct((A_ROWS + B_ROWS, D), bf16),
+            in_specs=[pl.BlockSpec(memory_space=pl.ANY)] * 4,
+            out_specs=pl.BlockSpec(memory_space=pltpu.VMEM),
+            scratch_shapes=[pltpu.VMEM(vectors.shape, bf16), pltpu.SemaphoreType.DMA((4,))],
+            compiler_params=pltpu.CompilerParams(vmem_limit_bytes=60 * 1024 * 1024),
+        )(w_qkv.T, vectors, w_out.T, w_up)
         edges = neighbours(jnp.stack([tokens, cotangent]), "tensor", EDGE)
         line = gather(block[None], ALONG_Z)
         down = w_down.T[None]
         down = jnp.concatenate([down, swap(down, ALONG_Y, ALONG_X)], axis=0)
         down = [down, swap(down, ALONG_X, ALONG_Y)]
-        line, down, edges, keep, own_near, own_far, own_down, own_up = lax.optimization_barrier(
-            (line, down, edges, keep, own_near, own_far, own_down, own_up)
+        line, down, keep, own_near, own_far, own_down, own_up = lax.optimization_barrier(
+            (line, down, keep, own_near, own_far, own_down, own_up)
         )
         line, down = jnp.concatenate(line, axis=0), jnp.concatenate(down, axis=0)
         near_pieces = swap(line, ALONG_Y, ALONG_X)
         down = [down, swap(down, ALONG_Z[0], ALONG_Z[1])]
-        near_pieces, down = lax.optimization_barrier((near_pieces, down))
+        near_pieces, down, edges = lax.optimization_barrier((near_pieces, down, edges))
         down = jnp.concatenate(down, axis=0)
         near_pieces = jnp.concatenate([line, near_pieces], axis=0)
         a_far = swap(near_pieces[:, :A_ROWS], ALONG_X, ALONG_Y)
@@ -606,7 +617,7 @@
             ((3 * D, D), bf16), ((16, D), f32),
         ],
         [((D, 128), f32), ((HALF, HALF), bf16), ((BAND, HALF), f32), ((ROWS, D), bf16)],
-        0.1, 20,
+        0.1, 16,
     )
     if near:
         b_far, c_pieces, proj = lax.optimization_barrier((b_far, c_pieces, proj))
@@ -619,25 +630,26 @@
             ((ROWS, FF), bf16), ((ROWS, D), bf16), ((ROWS, D), bf16), ((D, FF), bf16), ((D, D), bf16),
         ],
         [
-            ((CHUNKS, D, D), bf16), ((ROWS, FF), f32), ((D, OWN_ALL), bf16), ((ROWS, D), f32), ((ROWS, D), bf16),
+            ((CHUNKS, D, D), bf16), ((ROWS, 2 * D), f32), ((D, OWN_ALL), bf16), ((ROWS, D), f32), ((ROWS, D), bf16),
         ],
-        8, 30,
-    )
-    up_kept, up_sent, branch, gsec, colsum = call(
-        down_kernel, [own_up, own_down, hid, slope, second, branch_low, up_all, *c_pieces],
+        8, 25,
+    )
+    up_kept, up_sent, gpre, down_all, colsum = call(
+        down_kernel, [own_up, own_down, slope, second, branch_low, *c_pieces],
         [
-            ((NEAR, UP_ROWS, D), bf16), ((NEAR, UP_ROWS, D), bf16), ((OWN_ALL, D), f32), ((ROWS, D), f32),
-            ((8, D), f32),
+            ((NEAR, UP_ROWS, D), bf16), ((NEAR, UP_ROWS, D), bf16), ((ROWS, FF), bf16), ((D, FF), bf16), ((8, D), f32),
         ],
-        [
-            ((D, FF), bf16), ((CHUNKS, D, D), bf16), ((ROWS, FF), f32), ((ROWS, FF), bf16), ((D + 16, OWN_ALL), bf16),
-        ],
-        8, 30,
+        [((CHUNKS, D, D), bf16), ((ROWS, 2 * D), f32), ((D + 16, OWN_ALL), bf16)],
+        8, 20,
     )
     if near:
-        dn_sum = wide(dn_kept) + wide(after(swap(dn_sent, CORES), gsec))
-        dn_far = dn_sum[NEAR // 2 :].astype(bf16)
-        up_sum = wide(up_kept) + wide(swap(up_sent, CORES))
+        dn_sum = wide(dn_kept) + wide(after(swap(dn_sent, CORES), gpre))
+        gpre, dn_far = lax.optimization_barrier((gpre, dn_sum[NEAR // 2 :].astype(bf16)))
+    branch, gsec = call(
+        sum_kernel, [hid, gpre, up_all, down_all], [((OWN_ALL, D), f32), ((ROWS, D), f32)], [], 0.1, 13,
+    )
+    if near:
+        up_sum = wide(up_kept) + wide(after(swap(up_sent, CORES), gsec))
         up_far = up_sum[NEAR // 2 :].astype(bf16)
         gsec, up_far, dn_far = lax.optimization_barrier((gsec, up_far, dn_far))
     out, gres, gout, gmix, sums = call(
@@ -648,32 +660,36 @@
         [((ROWS, D), bf16)],
         0.1, 16,
     )
-    (gproj,) = call(
-        back_kernel, [gmix, proj, probs], [((ROWS, 3 * D), bf16)],
-        [((HALF, HALF), bf16), ((CLIPS * BANDS, 2, BAND, HALF), bf16)],
-        0.1, 16,
-    )
+    def attend_back(*clips):
+        rows = len(clips) * OWN
+        return call(
+            functools.partial(back_kernel, clips), [gmix, proj, probs], [((rows, 3 * D), bf16)],
+            [((HALF, HALF), bf16), ((len(clips) * BANDS, 2, BAND, HALF), bf16)], 0.1, 12,
+        )[0]
+
+    gproj_a, gproj_b = attend_back(0, 1), attend_back(2, 3)
     if near:
-        up_arrived, gproj = lax.optimization_barrier((swap(up_far, ALONG_X, ALONG_Y), gproj))
+        up_arrived, gproj_a, gproj_b = lax.optimization_barrier((swap(up_far, ALONG_X, ALONG_Y), gproj_a, gproj_b))
         up_sum = up_sum[: NEAR // 2] + wide(up_arrived)
-        up_near, gproj = lax.optimization_barrier((up_sum[PIECE:].astype(bf16), gproj))
-    at_kept, at_sent = call(
-        project_kernel, [own_near, gproj, gout, scaled, wqkv, vec, sums, colsum],
-        [((NEAR * G_ROWS + V_ROWS, D), bf16)] * 2,
+        up_near, gproj_a, gproj_b = lax.optimization_barrier((up_sum[PIECE:].astype(bf16), gproj_a, gproj_b))
+    at_kept, *at_sent = call(
+        project_kernel, [own_near, gproj_a, gproj_b, gout, scaled, wqkv, vec, sums, colsum],
+        [((NEAR * G_ROWS + V_ROWS, D), bf16)] + [((AT_ROWS // PARTS, D), bf16)] * PARTS,
         [((3 * D, D), bf16), ((128, D), f32)],
         0.1, 16,
     )
     if near:
-        dn_arrived, at_sent = lax.optimization_barrier((swap(dn_far, ALONG_Z[1], ALONG_Z[0]), at_sent))
-        up_arrived, at_arrived, gproj = lax.optimization_barrier(
-            (swap(up_near, ALONG_Y, ALONG_X), swap(at_sent, CORES), gproj)
+        up_arrived, at_sent[-1] = lax.optimization_barrier((swap(up_near, ALONG_Y, ALONG_X), at_sent[-1]))
+        at_arrived = [swap(piece, CORES) for piece in at_sent]
+        up_arrived, dn_arrived, at_arrived, gproj_a = lax.optimization_barrier(
+            (up_arrived, swap(dn_far, ALONG_Z[1], ALONG_Z[0]), at_arrived, gproj_a)
         )
     (gtok,) = call(
-        token_kernel, [gproj, x, gres, wqkv, vec], [((OWN_ALL, D), f32)], [], 0.1, 12,
+        token_kernel, [gproj_a, gproj_b, x, gres, wqkv, vec], [((OWN_ALL, D), f32)], [], 0.1, 12,
     )
     if near:
         at_sum, *at_rest = call(
-            share_kernel, [at_kept, at_arrived],
+            functools.partial(share_kernel, end_to_end=True), [at_kept, *at_arrived],
             [((PIECE * G_ROWS + V_ROWS, D), t) for t in (f32, bf16, bf16, bf16)], [], 0.1, 8,
         )
         dn_sum = dn_sum[: NEAR // 2] + wide(dn_arrived)
@@ -704,7 +720,8 @@
         g_up, g_down = up_sum, dn_sum.T
         g_qkv, g_out = g_qkv.T, g_out.T
     else:
-        at_grads = jnp.concatenate([a[: NEAR * G_ROWS].reshape(NEAR, G_ROWS, D) for a in (at_kept, at_sent)], axis=0)
+        at_grads = jnp.concatenate([at_kept[: NEAR * G_ROWS], *at_sent], axis=0)
+        at_grads = at_grads[: SLOTS * G_ROWS].reshape(SLOTS, G_ROWS, D)
 
         def whole(array):
             blocks = array.reshape(SLOTS // CHUNKS, CHUNKS, UP_ROWS, D).transpose(0, 2, 1, 3)

time: 121 us -> 112 us (0.926)
  starting transfers between devices: 41.3 us -> 35.4 us
  Pallas kernels: 35.4 us -> 31.3 us
  local copies, waits for them, and re-layouts: 4.15 us -> 1.03 us
  waiting for transfers between devices: 35.5 us -> 38.5 us
    pallas_call x11 -> x12, Pallas kernels: 35.4 us -> 29.6 us  [call(): pl.pallas_call(kernel, out_shape=[jax.ShapeDtypeStruct(s, t) for s, t in...]
    ppermute x32 -> x36, starting transfers between devices: 38 us -> 32.8 us  [swap(): lax.ppermute(array, BOTH, [(device, device ^ masks[device % 2]) for devic...]
    unnamed x32 -> x27, local copies, waits for them, and re-layouts: 3.26 us -> 0.15 us
    ppermute x32 -> x36, waiting for transfers between devices: 35.5 us -> 38.5 us  [swap(): lax.ppermute(array, BOTH, [(device, device ^ masks[device % 2]) for devic...]
    pallas_call x0 -> x1, Pallas kernels: none -> 1.63 us  [shards(): pl.pallas_call(pack_kernel, out_shape=jax.ShapeDtypeStruct((A_ROWS + B_RO...]
  transfers between devices with their start and end apart: 34 -> 38, of which waited for: 12 -> 16; matrix products, arithmetic and copies ran while one was open for 3% -> 4% of each run, Pallas kernels for 29% -> 26%
where the time goes in v3:
time: 112 us; the launch traced here: 111 us
  waiting for transfers between devices  38.5 us (34%)
  starting transfers between devices  35.4 us (32%)
  Pallas kernels  31.3 us (28%)
  other arithmetic  3.88 us (3%)
  between operations  1.21 us (1%)
    ppermute x36, waiting for transfers between devices, swap(): lax.ppermute(array, BOTH, [(device, device ^ masks[device % 2]) for devic...  38.5 us
    ppermute x36, starting transfers between devices, swap(): lax.ppermute(array, BOTH, [(device, device ^ masks[device % 2]) for devic...  32.8 us
    pallas_call x12, Pallas kernels, call(): pl.pallas_call(kernel, out_shape=[jax.ShapeDtypeStruct(s, t) for s, t in...  29.6 us
  transfers between devices with their start and end apart: 38, of which 16 were waited for; matrix products, arithmetic and copies ran while one was open for 4% of the time, Pallas kernels for 26%

profile of v3, /device:TPU:0, one launch (start us, length us, event | category | flops | bytes accessed | tf_op | source)
XLA Modules:
  0.0 111.3 jit_solution(488235404919194709)
XLA Ops:
  0.7 1.6 %shard_map.279 = bf16[144,512]{1,0:T(8,128)(2,1)} custom-call(bf16[48,512]{1,0:T(8,128)(2,1)} %bitcast.41, bf16[12,16]{1,0:T(8,128)(2,1)} %vec_ref.1, bf16[16,512]{1,0:T(8,128)(2,1)} %bitcast.42, bf16[64,512]{1,0:T(8,128)(2,1)} %up_ref.1), custom_call_target="tpu_custom_call" | custom-call | tf_op jit(solution)/shard_map/pallas_call | solution.py:566
  2.4 5.1 %collective-permute-start.2 = (bf16[1,144,512]{2,1,0:T(8,128)(2,1)}, bf16[1,144,512]{2,1,0:T(8,128)(2,1)S(1)}, u32[]{:S(2)}, u32[]{:S(2)}) collective-permute-start(bf16[1,144,512]{2,1,0:T(8,128)(2,1)} %bitcast.31), channel_id=1, source_target_pairs={{0,24},{1,25},{2,26},{3,27},{4,28},{5,29},{6,30},{7,31},{8,16},{9,... | collective-permute-start | bytes 442376 | tf_op jit(solution)/shard_map/ppermute | solution.py:496
  8.1 1.7 %collective-permute-start.3 = (bf16[1,64,512]{2,1,0:T(8,128)(2,1)}, bf16[1,64,512]{2,1,0:T(8,128)(2,1)S(1)}, u32[]{:S(2)}, u32[]{:S(2)}) collective-permute-start(bf16[1,64,512]{2,1,0:T(8,128)(2,1)} %bitcast.39), channel_id=1, source_target_pairs={{0,2},{1,5},{2,0},{3,7},{4,6},{5,1},{6,4},{7,3},{8,10},{9,13},{10,... | collective-permute-start | bytes 196616 | tf_op jit(solution)/shard_map/ppermute | solution.py:496
  12.6 1.7 %collective-permute-start.4 = (bf16[2,64,512]{2,1,0:T(8,128)(2,1)S(1)}, bf16[2,64,512]{2,1,0:T(8,128)(2,1)S(1)}, u32[]{:S(2)}, u32[]{:S(2)}) collective-permute-start(bf16[2,64,512]{2,1,0:T(8,128)(2,1)S(1)} %pad_maximum_fusion.6), channel_id=1, source_target_pairs={{0,4},{1,3},{2,6},{3,1},{4,0},{5,7},{6,2},{7,5},{8,12},{9,11},{10,... | collective-permute-start | bytes 393224 | tf_op jit(solution)/shard_map/ppermute | solution.py:496
  15.9 4.3 %collective-permute-done.1 = bf16[1,144,512]{2,1,0:T(8,128)(2,1)S(1)} collective-permute-done((bf16[1,144,512]{2,1,0:T(8,128)(2,1)}, bf16[1,144,512]{2,1,0:T(8,128)(2,1)S(1)}, u32[]{:S(2)}, u32[]{:S(2)}) %collective-permute-start.1) | collective-permute-done | bytes 147488 | tf_op jit(solution)/shard_map/ppermute | solution.py:496
  20.4 1.6 %collective-permute-start.5 = (bf16[4,144,512]{2,1,0:T(8,128)(2,1)S(1)}, bf16[4,144,512]{2,1,0:T(8,128)(2,1)S(1)}, u32[]{:S(2)}, u32[]{:S(2)}) collective-permute-start(bf16[4,144,512]{2,1,0:T(8,128)(2,1)S(1)} %pad_maximum_fusion.2), channel_id=1, source_target_pairs={{0,2},{1,5},{2,0},{3,7},{4,6},{5,1},{6,4},{7,3},{8,10},{9,13},{10,... | collective-permute-start | bytes 1769480 | tf_op jit(solution)/shard_map/ppermute | solution.py:496
  22.5 8.8 %collective-permute-done.6 = bf16[4,64,512]{2,1,0:T(8,128)(2,1)S(1)} collective-permute-done((bf16[4,64,512]{2,1,0:T(8,128)(2,1)S(1)}, bf16[4,64,512]{2,1,0:T(8,128)(2,1)S(1)}, u32[]{:S(2)}, u32[]{:S(2)}) %collective-permute-start.6) | collective-permute-done | bytes 262176 | tf_op jit(solution)/shard_map/ppermute | solution.py:496
  32.2 1.5 %collective-permute-start.12 = (bf16[8,80,512]{2,1,0:T(8,128)(2,1)S(1)}, bf16[8,80,512]{2,1,0:T(8,128)(2,1)S(1)}, u32[]{:S(2)}, u32[]{:S(2)}) collective-permute-start(bf16[8,80,512]{2,1,0:T(8,128)(2,1)S(1)} %slice.107), channel_id=1, source_target_pairs={{0,4},{1,3},{2,6},{3,1},{4,0},{5,7},{6,2},{7,5},{8,12},{9,11},{10,... | collective-permute-start | bytes 1966088 | tf_op jit(solution)/shard_map/ppermute | solution.py:496
  33.7 1.6 %collective-permute-start.13 = (bf16[8,64,512]{2,1,0:T(8,128)(2,1)S(1)}, bf16[8,64,512]{2,1,0:T(8,128)(2,1)S(1)}, u32[]{:S(2)}, u32[]{:S(2)}) collective-permute-start(bf16[8,64,512]{2,1,0:T(8,128)(2,1)S(1)} %constant_dynamic-update-slice_fusion.9.refs_0_), channel_id=1, source_target_pairs={{0,16},{1,9},{2,18},{3,11},{4,20},{5,13},{6,22},{7,15},{8,24},{9,1... | collective-permute-start | bytes 1572872 | tf_op jit(solution)/shard_map/ppermute | solution.py:496
  35.3 5.4 %collective-permute-done.9.refs_1_ = bf16[8,64,512]{2,1,0:T(8,128)(2,1)S(1)} collective-permute-done((bf16[8,64,512]{2,1,0:T(8,128)(2,1)S(1)}, bf16[8,64,512]{2,1,0:T(8,128)(2,1)S(1)}, u32[]{:S(2)}, u32[]{:S(2)}) %collective-permute-start.9) | collective-permute-done | bytes 524320 | tf_op jit(solution)/shard_map/ppermute | solution.py:496
  40.8 1.8 %collective-permute-done.11.refs_3_ = bf16[8,64,512]{2,1,0:T(8,128)(2,1)S(1)} collective-permute-done((bf16[8,64,512]{2,1,0:T(8,128)(2,1)S(1)}, bf16[8,64,512]{2,1,0:T(8,128)(2,1)S(1)}, u32[]{:S(2)}, u32[]{:S(2)}) %collective-permute-start.11) | collective-permute-done | bytes 524320 | tf_op jit(solution)/shard_map/ppermute | solution.py:496
  42.6 5.1 %shard_map.280 = (bf16[640,1536]{1,0:T(8,128)(2,1)S(1)}, f32[20,2,32,256]{3,2,1,0:T(8,128)S(1)}, bf16[640,512]{1,0:T(8,128)(2,1)S(1)}, bf16[640,512]{1,0:T(8,128...) custom-call(s32[32]{0:T(128)S(1)} %get-tuple-element.109.own_ref, ...), custom_call_target="tpu_custom_call" | custom-call | flops 110000000 | bytes 1048576 | tf_op jit(solution)/shard_map/pallas_call | solution.py:482
  47.7 1.7 %collective-permute-done.13.refs_1_ = bf16[8,64,512]{2,1,0:T(8,128)(2,1)S(1)} collective-permute-done((bf16[8,64,512]{2,1,0:T(8,128)(2,1)S(1)}, bf16[8,64,512]{2,1,0:T(8,128)(2,1)S(1)}, u32[]{:S(2)}, u32[]{:S(2)}) %collective-permute-start.13) | collective-permute-done | bytes 524320 | tf_op jit(solution)/shard_map/ppermute | solution.py:496
  50.2 1.4 %collective-permute-done.14.refs_3_ = bf16[8,80,512]{2,1,0:T(8,128)(2,1)S(1)} collective-permute-done((bf16[8,80,512]{2,1,0:T(8,128)(2,1)S(1)}, bf16[8,80,512]{2,1,0:T(8,128)(2,1)S(1)}, u32[]{:S(2)}, u32[]{:S(2)}) %collective-permute-start.14) | collective-permute-done | bytes 655392 | tf_op jit(solution)/shard_map/ppermute | solution.py:496
  51.6 5.5 %shard_map.281 = (bf16[16,64,512]{2,1,0:T(8,128)(2,1)S(1)}, bf16[16,64,512]{2,1,0:T(8,128)(2,1)S(1)}, f32[640,512]{1,0:T(8,128)S(1)}, bf16[640,2048]{1,0:T(8,128...) custom-call(s32[32]{0:T(128)S(1)} %get-tuple-element.109.own_ref, ...), custom_call_target="tpu_custom_call" | custom-call | flops 8800000000 | bytes 1048576 | tf_op jit(solution)/shard_map/pallas_call | solution.py:482
  57.2 3.8 %shard_map.282 = (bf16[16,64,512]{2,1,0:T(8,128)(2,1)S(1)}, bf16[16,64,512]{2,1,0:T(8,128)(2,1)S(1)}, bf16[640,2048]{1,0:T(8,128)(2,1)S(1)}, bf16[512,2048]{1,0:T(8,128)(2,1)S(1)}, f32[8,512]{1,0:T(8,128)S(1)}) custom-call(s32[32]{0:T(128)S(1)} %get-tuple-element.120.own_ref, s32[32]{0:T(128)S(1)} %get-tuple-element.112.own_down_ref, ...), custom_call_target="tpu_custom_call" | custom-call | flops 8800000000 | bytes 1048576 | tf_op jit(solution)/shard_map/pallas_call | solution.py:482
  62.0 2.6 %shard_map.283 = (f32[512,512]{1,0:T(8,128)S(1)}, f32[640,512]{1,0:T(8,128)S(1)}) custom-call(bf16[640,2048]{1,0:T(8,128)(2,1)S(1)} %get-tuple-element.119.hid_ref, bf16[640,2048]{1,0:T(8,128)(2,1)S(1)} %get-tuple-element.130.gpre_ref, bf16[512,2048]{1,0:T(8,128)(2,1)S(1)} %get-tuple-element.131.up_ref, bf16[512,2048]{1,0:T(8,128)(2,1)S(1)} %get-tuple-element.132.down_ref), custom_call_target="tpu_custom_call" | custom-call | flops 110000000 | bytes 1048576 | tf_op jit(solution)/shard_map/pallas_call | solution.py:482
  66.0 1.9 %shard_map.284 = (bf16[512,512]{1,0:T(8,128)(2,1)}, f32[640,512]{1,0:T(8,128)S(1)}, bf16[512,512]{1,0:T(8,128)(2,1)S(1)}, bf16[640,512]{1,0:T(8,128)(2,1)S(1)}, f32[8,512]{1,0:T(8,128)S(1)}) custom-call(f32[640,128]{1,0:T(8,128)S(1)} %broadcast_in_dim.59.keep_ref, bf16[640,512]{1,0:T(8,128)(2,1)S(1)} %pad_maximum_fusion.cot_ref, ...), custom_call_target="tpu_custom_call" | custom-call | flops 110000000 | bytes 1048576 | tf_op jit(solution)/shard_map/pallas_call | solution.py:482
  67.9 2.5 %shard_map.286.gproj_b = bf16[256,1536]{1,0:T(8,128)(2,1)S(1)} custom-call(bf16[640,512]{1,0:T(8,128)(2,1)S(1)} %get-tuple-element.143.gmix_ref, bf16[640,1536]{1,0:T(8,128)(2,1)S(1)} %get-tuple-element.144.proj_ref, f32[20,2,32,256]{3,2,1,0:T(8,128)S(1)} %get-tuple-element.145.prob_ref), custom_call_target="tpu_custom_call" | custom-call | flops 110000000 | bytes 1048576 | tf_op jit(solution)/shard_map/pallas_call | solution.py:482
  70.3 2.5 %shard_map.285.gproj_a = bf16[256,1536]{1,0:T(8,128)(2,1)S(1)} custom-call(bf16[640,512]{1,0:T(8,128)(2,1)S(1)} %get-tuple-element.143.gmix_ref, bf16[640,1536]{1,0:T(8,128)(2,1)S(1)} %get-tuple-element.144.proj_ref, f32[20,2,32,256]{3,2,1,0:T(8,128)S(1)} %get-tuple-element.145.prob_ref), custom_call_target="tpu_custom_call" | custom-call | flops 110000000 | bytes 1048576 | tf_op jit(solution)/shard_map/pallas_call | solution.py:482
  72.9 1.4 %collective-permute-done.19 = bf16[8,64,512]{2,1,0:T(8,128)(2,1)S(1)} collective-permute-done((bf16[8,64,512]{2,1,0:T(8,128)(2,1)S(1)}, bf16[8,64,512]{2,1,0:T(8,128)(2,1)S(1)}, u32[]{:S(2)}, u32[]{:S(2)}) %collective-permute-start.19) | collective-permute-done | bytes 524320 | tf_op jit(solution)/shard_map/ppermute | solution.py:496
  75.1 2.5 %shard_map.287 = (bf16[1040,512]{1,0:T(8,128)(2,1)S(1)}, bf16[208,512]{1,0:T(8,128)(2,1)S(1)}, bf16[208,512]{1,0:T(8,128)(2,1)S(1)}, bf16[208,512]{1,0:T(8,128)(...) custom-call(s32[32]{0:T(128)S(1)} %get-tuple-element.150.own_ref, ...), custom_call_target="tpu_custom_call" | custom-call | flops 110000000 | bytes 1048576 | tf_op jit(solution)/shard_map/pallas_call | solution.py:482
  78.2 2.6 %collective-permute-done.20 = bf16[4,64,512]{2,1,0:T(8,128)(2,1)S(1)} collective-permute-done((bf16[4,64,512]{2,1,0:T(8,128)(2,1)S(1)}, bf16[4,64,512]{2,1,0:T(8,128)(2,1)S(1)}, u32[]{:S(2)}, u32[]{:S(2)}) %collective-permute-start.20) | collective-permute-done | bytes 262176 | tf_op jit(solution)/shard_map/ppermute | solution.py:496
  83.0 1.5 %collective-permute-start.27 = (bf16[6,64,512]{2,1,0:T(8,128)(2,1)S(1)}, bf16[6,64,512]{2,1,0:T(8,128)(2,1)S(1)}, u32[]{:S(2)}, u32[]{:S(2)}) collective-permute-start(bf16[6,64,512]{2,1,0:T(8,128)(2,1)S(1)} %pad_maximum_fusion.3), channel_id=1, source_target_pairs={{0,8},{1,17},{2,10},{3,19},{4,12},{5,21},{6,14},{7,23},{8,0},{9,25... | collective-permute-start | bytes 1179656 | tf_op jit(solution)/shard_map/ppermute | solution.py:496
  84.7 1.6 %collective-permute-start.28 = (bf16[272,512]{1,0:T(8,128)(2,1)S(1)}, bf16[272,512]{1,0:T(8,128)(2,1)S(1)}, u32[]{:S(2)}, u32[]{:S(2)}) collective-permute-start(bf16[272,512]{1,0:T(8,128)(2,1)S(1)} %get-tuple-element.178), channel_id=1, source_target_pairs={{0,2},{1,3},{2,0},{3,1},{4,6},{5,7},{6,4},{7,5},{8,10},{9,11},{10,... | collective-permute-start | bytes 835592 | tf_op jit(solution)/shard_map/ppermute | solution.py:496
  86.8 1.4 %collective-permute-start.30 = (bf16[272,512]{1,0:T(8,128)(2,1)S(1)}, bf16[272,512]{1,0:T(8,128)(2,1)S(1)}, u32[]{:S(2)}, u32[]{:S(2)}) collective-permute-start(bf16[272,512]{1,0:T(8,128)(2,1)S(1)} %get-tuple-element.180), channel_id=1, source_target_pairs={{0,6},{1,7},{2,4},{3,5},{4,2},{5,3},{6,0},{7,1},{8,14},{9,15},{10,... | collective-permute-start | bytes 835592 | tf_op jit(solution)/shard_map/ppermute | solution.py:496
  88.3 2.2 %shard_map.288 = f32[512,512]{1,0:T(8,128)} custom-call(bf16[256,1536]{1,0:T(8,128)(2,1)S(1)} %shard_map.285.gproj_a, bf16[256,1536]{1,0:T(8,128)(2,1)S(1)} %shard_map.286.gproj_b, bf16[640,512]{1,0:T(8,128)(2,1)S(1)} %pad_maximum_fusion.1.x_ref, f32[640,512]{1,0:T(8,128)S(1)} %get-tuple-element.169.gres_ref, ...), custom_call_target="tpu_custom_call" | custom-call | flops 110000000 | bytes 1048576 | tf_op jit(solution)/shard_map/pallas_call | solution.py:482
  90.5 4.6 %collective-permute-done.27 = bf16[6,64,512]{2,1,0:T(8,128)(2,1)S(1)} collective-permute-done((bf16[6,64,512]{2,1,0:T(8,128)(2,1)S(1)}, bf16[6,64,512]{2,1,0:T(8,128)(2,1)S(1)}, u32[]{:S(2)}, u32[]{:S(2)}) %collective-permute-start.27) | collective-permute-done | bytes 393248 | tf_op jit(solution)/shard_map/ppermute | solution.py:496
  96.3 1.5 %collective-permute-start.35 = (bf16[1,64,512]{2,1,0:T(8,128)(2,1)S(1)}, bf16[1,64,512]{2,1,0:T(8,128)(2,1)S(1)}, u32[]{:S(2)}, u32[]{:S(2)}) collective-permute-start(bf16[1,64,512]{2,1,0:T(8,128)(2,1)S(1)} %get-tuple-element.197), channel_id=1, source_target_pairs={{0,2},{1,5},{2,0},{3,7},{4,6},{5,1},{6,4},{7,3},{8,10},{9,13},{10,... | collective-permute-start | bytes 196616 | tf_op jit(solution)/shard_map/ppermute | solution.py:496
  101.3 1.4 %collective-permute-start.32 = (bf16[80,512]{1,0:T(8,128)(2,1)S(1)}, bf16[80,512]{1,0:T(8,128)(2,1)S(1)}, u32[]{:S(2)}, u32[]{:S(2)}) collective-permute-start(bf16[80,512]{1,0:T(8,128)(2,1)S(1)} %get-tuple-element.186), channel_id=1, source_target_pairs={{0,8},{1,9},{2,10},{3,11},{4,12},{5,13},{6,14},{7,15},{8,0},{9,1},... | collective-permute-start | bytes 245768 | tf_op jit(solution)/shard_map/ppermute | solution.py:496
  103.8 1.9 %collective-permute-start.34 = (bf16[80,512]{1,0:T(8,128)(2,1)S(1)}, bf16[80,512]{1,0:T(8,128)(2,1)S(1)}, u32[]{:S(2)}, u32[]{:S(2)}) collective-permute-start(bf16[80,512]{1,0:T(8,128)(2,1)S(1)} %get-tuple-element.188), channel_id=1, source_target_pairs={{0,24},{1,25},{2,26},{3,27},{4,28},{5,29},{6,30},{7,31},{8,16},{9,... | collective-permute-start | bytes 245768 | tf_op jit(solution)/shard_map/ppermute | solution.py:496
  107.1 3.6 %collective-permute-done.33.refs_2_ = bf16[80,512]{1,0:T(8,128)(2,1)S(1)} collective-permute-done((bf16[80,512]{1,0:T(8,128)(2,1)S(1)}, bf16[80,512]{1,0:T(8,128)(2,1)S(1)}, u32[]{:S(2)}, u32[]{:S(2)}) %collective-permute-start.33) | collective-permute-done | bytes 81952 | tf_op jit(solution)/shard_map/ppermute | solution.py:496
  (127 shorter events, 22.0 us)
Async XLA Ops:
  2.4 12.2 %collective-permute-start.2 = (bf16[1,144,512]{2,1,0:T(8,128)(2,1)}, bf16[1,144,512]{2,1,0:T(8,128)(2,1)S(1)}, u32[]{:S(2)}, u32[]{:S(2)}) collective-permute-start(bf16[1,144,512]{2,1,0:T(8,128)(2,1)} %bitcast.31), channel_id=1, source_target_pairs={{0,24},{1,25},{2,26},{3,27},{4,28},{5,29},{6,30},{7,31},{8,16},{9,... | collective-permute-start | bytes 442376 | tf_op jit(solution)/shard_map/ppermute | solution.py:496
  7.5 12.7 %collective-permute-start.1 = (bf16[1,144,512]{2,1,0:T(8,128)(2,1)}, bf16[1,144,512]{2,1,0:T(8,128)(2,1)S(1)}, u32[]{:S(2)}, u32[]{:S(2)}) collective-permute-start(bf16[1,144,512]{2,1,0:T(8,128)(2,1)} %bitcast.32), channel_id=1, source_target_pairs={{0,16},{1,17},{2,18},{3,19},{4,20},{5,21},{6,22},{7,23},{8,24},{9,... | collective-permute-start | bytes 442376 | tf_op jit(solution)/shard_map/ppermute | solution.py:496
  7.5 12.7 %collective-permute-start = (bf16[1,144,512]{2,1,0:T(8,128)(2,1)}, bf16[1,144,512]{2,1,0:T(8,128)(2,1)S(1)}, u32[]{:S(2)}, u32[]{:S(2)}) collective-permute-start(bf16[1,144,512]{2,1,0:T(8,128)(2,1)} %bitcast.33), channel_id=1, source_target_pairs={{0,8},{1,9},{2,10},{3,11},{4,12},{5,13},{6,14},{7,15},{8,0},{9,1},... | collective-permute-start | bytes 442376 | tf_op jit(solution)/shard_map/ppermute | solution.py:496
  8.1 4.5 %collective-permute-start.3 = (bf16[1,64,512]{2,1,0:T(8,128)(2,1)}, bf16[1,64,512]{2,1,0:T(8,128)(2,1)S(1)}, u32[]{:S(2)}, u32[]{:S(2)}) collective-permute-start(bf16[1,64,512]{2,1,0:T(8,128)(2,1)} %bitcast.39), channel_id=1, source_target_pairs={{0,2},{1,5},{2,0},{3,7},{4,6},{5,1},{6,4},{7,3},{8,10},{9,13},{10,... | collective-permute-start | bytes 196616 | tf_op jit(solution)/shard_map/ppermute | solution.py:496
  10.8 11.7 %collective-permute-start.8 = (bf16[2,4,16,512]{3,2,1,0:T(8,128)(2,1)S(1)}, bf16[2,4,16,512]{3,2,1,0:T(8,128)(2,1)S(1)}, u32[]{:S(2)}, u32[]{:S(2)}) collective-permute-start(bf16[2,4,16,512]{3,2,1,0:T(8,128)(2,1)S(1)} %get-tuple-element.195), channel_id=1, source_target_pairs={{1,0},{2,1},{3,2},{5,4},{6,5},{7,6},{9,8},{10,9},{11,10},{13,12},{... | collective-permute-start | bytes 393224 | tf_op jit(solution)/shard_map/ppermute | solution.py:544
  12.6 7.6 %collective-permute-start.4 = (bf16[2,64,512]{2,1,0:T(8,128)(2,1)S(1)}, bf16[2,64,512]{2,1,0:T(8,128)(2,1)S(1)}, u32[]{:S(2)}, u32[]{:S(2)}) collective-permute-start(bf16[2,64,512]{2,1,0:T(8,128)(2,1)S(1)} %pad_maximum_fusion.6), channel_id=1, source_target_pairs={{0,4},{1,3},{2,6},{3,1},{4,0},{5,7},{6,2},{7,5},{8,12},{9,11},{10,... | collective-permute-start | bytes 393224 | tf_op jit(solution)/shard_map/ppermute | solution.py:496
  14.6 7.9 %collective-permute-start.7 = (bf16[2,4,16,512]{3,2,1,0:T(8,128)(2,1)S(1)}, bf16[2,4,16,512]{3,2,1,0:T(8,128)(2,1)S(1)}, u32[]{:S(2)}, u32[]{:S(2)}) collective-permute-start(bf16[2,4,16,512]{3,2,1,0:T(8,128)(2,1)S(1)} %get-tuple-element.196), channel_id=1, source_target_pairs={{0,1},{1,2},{2,3},{4,5},{5,6},{6,7},{8,9},{9,10},{10,11},{12,13},{... | collective-permute-start | bytes 393224 | tf_op jit(solution)/shard_map/ppermute | solution.py:543
  20.4 10.9 %collective-permute-start.5 = (bf16[4,144,512]{2,1,0:T(8,128)(2,1)S(1)}, bf16[4,144,512]{2,1,0:T(8,128)(2,1)S(1)}, u32[]{:S(2)}, u32[]{:S(2)}) collective-permute-start(bf16[4,144,512]{2,1,0:T(8,128)(2,1)S(1)} %pad_maximum_fusion.2), channel_id=1, source_target_pairs={{0,2},{1,5},{2,0},{3,7},{4,6},{5,1},{6,4},{7,3},{8,10},{9,13},{10,... | collective-permute-start | bytes 1769480 | tf_op jit(solution)/shard_map/ppermute | solution.py:496
  22.0 9.2 %collective-permute-start.6 = (bf16[4,64,512]{2,1,0:T(8,128)(2,1)S(1)}, bf16[4,64,512]{2,1,0:T(8,128)(2,1)S(1)}, u32[]{:S(2)}, u32[]{:S(2)}) collective-permute-start(bf16[4,64,512]{2,1,0:T(8,128)(2,1)S(1)} %constant_dynamic-update-slice_fusion), channel_id=1, source_target_pairs={{0,8},{1,17},{2,10},{3,19},{4,12},{5,21},{6,14},{7,23},{8,0},{9,25... | collective-permute-start | bytes 786440 | tf_op jit(solution)/shard_map/ppermute | solution.py:496
  31.3 11.3 %collective-permute-start.10 = (bf16[8,144,512]{2,1,0:T(8,128)(2,1)S(1)}, bf16[8,144,512]{2,1,0:T(8,128)(2,1)S(1)}, u32[]{:S(2)}, u32[]{:S(2)}) collective-permute-start(bf16[8,144,512]{2,1,0:T(8,128)(2,1)S(1)} %constant_dynamic-update-slice_fusion.4.refs_0_), channel_id=1, source_target_pairs={{0,1},{1,0},{2,3},{3,2},{4,5},{5,4},{6,7},{7,6},{8,9},{9,8},{10,11... | collective-permute-start | bytes 3538952 | tf_op jit(solution)/shard_map/ppermute | solution.py:496
  31.5 9.2 %collective-permute-start.9 = (bf16[8,64,512]{2,1,0:T(8,128)(2,1)S(1)}, bf16[8,64,512]{2,1,0:T(8,128)(2,1)S(1)}, u32[]{:S(2)}, u32[]{:S(2)}) collective-permute-start(bf16[8,64,512]{2,1,0:T(8,128)(2,1)S(1)} %slice.106), channel_id=1, source_target_pairs={{0,4},{1,3},{2,6},{3,1},{4,0},{5,7},{6,2},{7,5},{8,12},{9,11},{10,... | collective-permute-start | bytes 1572872 | tf_op jit(solution)/shard_map/ppermute | solution.py:496
  32.2 17.3 %collective-permute-start.12 = (bf16[8,80,512]{2,1,0:T(8,128)(2,1)S(1)}, bf16[8,80,512]{2,1,0:T(8,128)(2,1)S(1)}, u32[]{:S(2)}, u32[]{:S(2)}) collective-permute-start(bf16[8,80,512]{2,1,0:T(8,128)(2,1)S(1)} %slice.107), channel_id=1, source_target_pairs={{0,4},{1,3},{2,6},{3,1},{4,0},{5,7},{6,2},{7,5},{8,12},{9,11},{10,... | collective-permute-start | bytes 1966088 | tf_op jit(solution)/shard_map/ppermute | solution.py:496
  33.7 15.8 %collective-permute-start.13 = (bf16[8,64,512]{2,1,0:T(8,128)(2,1)S(1)}, bf16[8,64,512]{2,1,0:T(8,128)(2,1)S(1)}, u32[]{:S(2)}, u32[]{:S(2)}) collective-permute-start(bf16[8,64,512]{2,1,0:T(8,128)(2,1)S(1)} %constant_dynamic-update-slice_fusion.9.refs_0_), channel_id=1, source_target_pairs={{0,16},{1,9},{2,18},{3,11},{4,20},{5,13},{6,22},{7,15},{8,24},{9,1... | collective-permute-start | bytes 1572872 | tf_op jit(solution)/shard_map/ppermute | solution.py:496
  49.6 7.7 %collective-permute-start.15 = (bf16[8,64,512]{2,1,0:T(8,128)(2,1)S(1)}, bf16[8,64,512]{2,1,0:T(8,128)(2,1)S(1)}, u32[]{:S(2)}, u32[]{:S(2)}) collective-permute-start(bf16[8,64,512]{2,1,0:T(8,128)(2,1)S(1)} %constant_dynamic-update-slice_fusion.9.refs_0_), channel_id=1, source_target_pairs={{0,1},{1,0},{2,3},{3,2},{4,5},{5,4},{6,7},{7,6},{8,9},{9,8},{10,11... | collective-permute-start | bytes 1572872 | tf_op jit(solution)/shard_map/ppermute | solution.py:496
  50.1 7.1 %collective-permute-start.16 = (bf16[8,64,512]{2,1,0:T(8,128)(2,1)S(1)}, bf16[8,64,512]{2,1,0:T(8,128)(2,1)S(1)}, u32[]{:S(2)}, u32[]{:S(2)}) collective-permute-start(bf16[8,64,512]{2,1,0:T(8,128)(2,1)S(1)} %collective-permute-done.13.refs_1_), channel_id=1, source_target_pairs={{0,1},{1,0},{2,3},{3,2},{4,5},{5,4},{6,7},{7,6},{8,9},{9,8},{10,11... | collective-permute-start | bytes 1572872 | tf_op jit(solution)/shard_map/ppermute | solution.py:496
  57.0 4.5 %collective-permute-start.17 = (bf16[16,64,512]{2,1,0:T(8,128)(2,1)S(1)}, bf16[16,64,512]{2,1,0:T(8,128)(2,1)S(1)}, u32[]{:S(2)}, u32[]{:S(2)}) collective-permute-start(bf16[16,64,512]{2,1,0:T(8,128)(2,1)S(1)} %get-tuple-element.128), channel_id=1, source_target_pairs={{0,1},{1,0},{2,3},{3,2},{4,5},{5,4},{6,7},{7,6},{8,9},{9,8},{10,11... | collective-permute-start | bytes 3145736 | tf_op jit(solution)/shard_map/ppermute | solution.py:496
  65.0 9.2 %collective-permute-start.19 = (bf16[8,64,512]{2,1,0:T(8,128)(2,1)S(1)}, bf16[8,64,512]{2,1,0:T(8,128)(2,1)S(1)}, u32[]{:S(2)}, u32[]{:S(2)}) collective-permute-start(bf16[8,64,512]{2,1,0:T(8,128)(2,1)S(1)} %slice.147), channel_id=1, source_target_pairs={{0,4},{1,3},{2,6},{3,1},{4,0},{5,7},{6,2},{7,5},{8,12},{9,11},{10,... | collective-permute-start | bytes 1572872 | tf_op jit(solution)/shard_map/ppermute | solution.py:496
  65.6 15.5 %collective-permute-start.21 = (bf16[8,64,512]{2,1,0:T(8,128)(2,1)S(1)}, bf16[8,64,512]{2,1,0:T(8,128)(2,1)S(1)}, u32[]{:S(2)}, u32[]{:S(2)}) collective-permute-start(bf16[8,64,512]{2,1,0:T(8,128)(2,1)S(1)} %slice.148), channel_id=1, source_target_pairs={{0,16},{1,9},{2,18},{3,11},{4,20},{5,13},{6,22},{7,15},{8,24},{9,1... | collective-permute-start | bytes 1572872 | tf_op jit(solution)/shard_map/ppermute | solution.py:496
  74.4 6.4 %collective-permute-start.20 = (bf16[4,64,512]{2,1,0:T(8,128)(2,1)S(1)}, bf16[4,64,512]{2,1,0:T(8,128)(2,1)S(1)}, u32[]{:S(2)}, u32[]{:S(2)}) collective-permute-start(bf16[4,64,512]{2,1,0:T(8,128)(2,1)S(1)} %slice.150), channel_id=1, source_target_pairs={{0,2},{1,5},{2,0},{3,7},{4,6},{5,1},{6,4},{7,3},{8,10},{9,13},{10,... | collective-permute-start | bytes 786440 | tf_op jit(solution)/shard_map/ppermute | solution.py:496
  77.6 3.8 %collective-permute-start.22 = (bf16[208,512]{1,0:T(8,128)(2,1)S(1)}, bf16[208,512]{1,0:T(8,128)(2,1)S(1)}, u32[]{:S(2)}, u32[]{:S(2)}) collective-permute-start(bf16[208,512]{1,0:T(8,128)(2,1)S(1)} %get-tuple-element.161), channel_id=1, source_target_pairs={{0,1},{1,0},{2,3},{3,2},{4,5},{5,4},{6,7},{7,6},{8,9},{9,8},{10,11... | collective-permute-start | bytes 638984 | tf_op jit(solution)/shard_map/ppermute | solution.py:496
  77.7 3.7 %collective-permute-start.23 = (bf16[208,512]{1,0:T(8,128)(2,1)S(1)}, bf16[208,512]{1,0:T(8,128)(2,1)S(1)}, u32[]{:S(2)}, u32[]{:S(2)}) collective-permute-start(bf16[208,512]{1,0:T(8,128)(2,1)S(1)} %get-tuple-element.162), channel_id=1, source_target_pairs={{0,1},{1,0},{2,3},{3,2},{4,5},{5,4},{6,7},{7,6},{8,9},{9,8},{10,11... | collective-permute-start | bytes 638984 | tf_op jit(solution)/shard_map/ppermute | solution.py:496
  83.0 12.1 %collective-permute-start.27 = (bf16[6,64,512]{2,1,0:T(8,128)(2,1)S(1)}, bf16[6,64,512]{2,1,0:T(8,128)(2,1)S(1)}, u32[]{:S(2)}, u32[]{:S(2)}) collective-permute-start(bf16[6,64,512]{2,1,0:T(8,128)(2,1)S(1)} %pad_maximum_fusion.3), channel_id=1, source_target_pairs={{0,8},{1,17},{2,10},{3,19},{4,12},{5,21},{6,14},{7,23},{8,0},{9,25... | collective-permute-start | bytes 1179656 | tf_op jit(solution)/shard_map/ppermute | solution.py:496
  84.7 13.1 %collective-permute-start.28 = (bf16[272,512]{1,0:T(8,128)(2,1)S(1)}, bf16[272,512]{1,0:T(8,128)(2,1)S(1)}, u32[]{:S(2)}, u32[]{:S(2)}) collective-permute-start(bf16[272,512]{1,0:T(8,128)(2,1)S(1)} %get-tuple-element.178), channel_id=1, source_target_pairs={{0,2},{1,3},{2,0},{3,1},{4,6},{5,7},{6,4},{7,5},{8,10},{9,11},{10,... | collective-permute-start | bytes 835592 | tf_op jit(solution)/shard_map/ppermute | solution.py:496
  86.3 12.6 %collective-permute-start.29 = (bf16[272,512]{1,0:T(8,128)(2,1)S(1)}, bf16[272,512]{1,0:T(8,128)(2,1)S(1)}, u32[]{:S(2)}, u32[]{:S(2)}) collective-permute-start(bf16[272,512]{1,0:T(8,128)(2,1)S(1)} %get-tuple-element.179), channel_id=1, source_target_pairs={{0,4},{1,5},{2,6},{3,7},{4,0},{5,1},{6,2},{7,3},{8,12},{9,13},{10,... | collective-permute-start | bytes 835592 | tf_op jit(solution)/shard_map/ppermute | solution.py:496
  86.8 13.9 %collective-permute-start.30 = (bf16[272,512]{1,0:T(8,128)(2,1)S(1)}, bf16[272,512]{1,0:T(8,128)(2,1)S(1)}, u32[]{:S(2)}, u32[]{:S(2)}) collective-permute-start(bf16[272,512]{1,0:T(8,128)(2,1)S(1)} %get-tuple-element.180), channel_id=1, source_target_pairs={{0,6},{1,7},{2,4},{3,5},{4,2},{5,3},{6,0},{7,1},{8,14},{9,15},{10,... | collective-permute-start | bytes 835592 | tf_op jit(solution)/shard_map/ppermute | solution.py:496
  95.2 5.9 %collective-permute-start.31 = (bf16[1,64,512]{2,1,0:T(8,128)(2,1)S(1)}, bf16[1,64,512]{2,1,0:T(8,128)(2,1)S(1)}, u32[]{:S(2)}, u32[]{:S(2)}) collective-permute-start(bf16[1,64,512]{2,1,0:T(8,128)(2,1)S(1)} %slice.152), channel_id=1, source_target_pairs={{0,16},{1,9},{2,18},{3,11},{4,20},{5,13},{6,22},{7,15},{8,24},{9,1... | collective-permute-start | bytes 196616 | tf_op jit(solution)/shard_map/ppermute | solution.py:496
  96.3 7.5 %collective-permute-start.35 = (bf16[1,64,512]{2,1,0:T(8,128)(2,1)S(1)}, bf16[1,64,512]{2,1,0:T(8,128)(2,1)S(1)}, u32[]{:S(2)}, u32[]{:S(2)}) collective-permute-start(bf16[1,64,512]{2,1,0:T(8,128)(2,1)S(1)} %get-tuple-element.197), channel_id=1, source_target_pairs={{0,2},{1,5},{2,0},{3,7},{4,6},{5,1},{6,4},{7,3},{8,10},{9,13},{10,... | collective-permute-start | bytes 196616 | tf_op jit(solution)/shard_map/ppermute | solution.py:496
  97.8 7.9 %collective-permute-start.37 = (bf16[1,64,512]{2,1,0:T(8,128)(2,1)S(1)}, bf16[1,64,512]{2,1,0:T(8,128)(2,1)S(1)}, u32[]{:S(2)}, u32[]{:S(2)}) collective-permute-start(bf16[1,64,512]{2,1,0:T(8,128)(2,1)S(1)} %get-tuple-element.198), channel_id=1, source_target_pairs={{0,6},{1,7},{2,4},{3,5},{4,2},{5,3},{6,0},{7,1},{8,14},{9,15},{10,... | collective-permute-start | bytes 196616 | tf_op jit(solution)/shard_map/ppermute | solution.py:496
  98.9 6.8 %collective-permute-start.36 = (bf16[1,64,512]{2,1,0:T(8,128)(2,1)S(1)}, bf16[1,64,512]{2,1,0:T(8,128)(2,1)S(1)}, u32[]{:S(2)}, u32[]{:S(2)}) collective-permute-start(bf16[1,64,512]{2,1,0:T(8,128)(2,1)S(1)} %get-tuple-element.199), channel_id=1, source_target_pairs={{0,4},{1,3},{2,6},{3,1},{4,0},{5,7},{6,2},{7,5},{8,12},{9,11},{10,... | collective-permute-start | bytes 196616 | tf_op jit(solution)/shard_map/ppermute | solution.py:496
  101.3 5.8 %collective-permute-start.32 = (bf16[80,512]{1,0:T(8,128)(2,1)S(1)}, bf16[80,512]{1,0:T(8,128)(2,1)S(1)}, u32[]{:S(2)}, u32[]{:S(2)}) collective-permute-start(bf16[80,512]{1,0:T(8,128)(2,1)S(1)} %get-tuple-element.186), channel_id=1, source_target_pairs={{0,8},{1,9},{2,10},{3,11},{4,12},{5,13},{6,14},{7,15},{8,0},{9,1},... | collective-permute-start | bytes 245768 | tf_op jit(solution)/shard_map/ppermute | solution.py:496
  102.7 8.0 %collective-permute-start.33 = (bf16[80,512]{1,0:T(8,128)(2,1)S(1)}, bf16[80,512]{1,0:T(8,128)(2,1)S(1)}, u32[]{:S(2)}, u32[]{:S(2)}) collective-permute-start(bf16[80,512]{1,0:T(8,128)(2,1)S(1)} %get-tuple-element.187), channel_id=1, source_target_pairs={{0,16},{1,17},{2,18},{3,19},{4,20},{5,21},{6,22},{7,23},{8,24},{9,... | collective-permute-start | bytes 245768 | tf_op jit(solution)/shard_map/ppermute | solution.py:496
  103.8 6.8 %collective-permute-start.34 = (bf16[80,512]{1,0:T(8,128)(2,1)S(1)}, bf16[80,512]{1,0:T(8,128)(2,1)S(1)}, u32[]{:S(2)}, u32[]{:S(2)}) collective-permute-start(bf16[80,512]{1,0:T(8,128)(2,1)S(1)} %get-tuple-element.188), channel_id=1, source_target_pairs={{0,24},{1,25},{2,26},{3,27},{4,28},{5,29},{6,30},{7,31},{8,16},{9,... | collective-permute-start | bytes 245768 | tf_op jit(solution)/shard_map/ppermute | solution.py:496
  (16 other events, 130.0 us)

commit v4 on v3

--- a/solution.py
+++ b/solution.py
@@ -496,13 +496,13 @@
     return lax.ppermute(array, BOTH, [(device, device ^ masks[device % 2]) for device in range(count)])
 
 
-ALONG_Z, ALONG_Y, ALONG_X, CORES = (8, 16, 24), 2, 4, 1
+ALONG_Z, ALONG_Y, ALONG_X, CORES = (16, 8, 24), 2, 4, 1
 ALONG_XY = (ALONG_Y, ALONG_X, ALONG_Y ^ ALONG_X)
 
 
-def owners(device, swapped, line_first=True, turn=None):
+def owners(device, swapped, line_first=True, turn=None, second_first=True):
     def one(second_core):
-        first = ALONG_X if second_core and swapped else ALONG_Y
+        first = ALONG_X if swapped and bool(second_core) == second_first else ALONG_Y
         plane = [0, first, first ^ ALONG_XY[2], ALONG_XY[2]]
         line = [0, *ALONG_Z]
         if turn is not None and second_core != turn:
@@ -561,7 +561,7 @@
 
     if near:
         device = lax.axis_index("dp") * devices_t + rank
-        own_near, own_far = owners(device, False), owners(device, True)
+        own_near, own_far = owners(device, False), owners(device, True, second_first=False)
         own_down, own_up = owners(device, True, False, 0), owners(device, True, True, 1)
         block = pl.pallas_call(
             pack_kernel,
@@ -580,13 +580,13 @@
             (line, down, keep, own_near, own_far, own_down, own_up)
         )
         line, down = jnp.concatenate(line, axis=0), jnp.concatenate(down, axis=0)
-        near_pieces = swap(line, ALONG_Y, ALONG_X)
+        near_pieces = swap(line, ALONG_X, ALONG_Y)
         down = [down, swap(down, ALONG_Z[0], ALONG_Z[1])]
         near_pieces, down, edges = lax.optimization_barrier((near_pieces, down, edges))
         down = jnp.concatenate(down, axis=0)
         near_pieces = jnp.concatenate([line, near_pieces], axis=0)
-        a_far = swap(near_pieces[:, :A_ROWS], ALONG_X, ALONG_Y)
-        b_far = swap(near_pieces[:, A_ROWS:], ALONG_X, ALONG_Y)
+        a_far = swap(near_pieces[:, :A_ROWS], ALONG_Y, ALONG_X)
+        b_far = swap(near_pieces[:, A_ROWS:], ALONG_Y, ALONG_X)
         pieces = both_cores([near_pieces])
         a_pieces = [pieces[0], a_far, pieces[1], swap(a_far, CORES)]
         c_pieces = [down, swap(down, ALONG_Z[1], ALONG_Z[0])]

time: 112 us -> 111 us (level)
  starting transfers between devices: 35.4 us -> 33.8 us
    ppermute x36, starting transfers between devices: 32.8 us -> 31.2 us  [swap(): lax.ppermute(array, BOTH, [(device, device ^ masks[device % 2]) for devic...]
where the time goes in v4:
time: 111 us
  waiting for transfers between devices  39.3 us (35%)
  starting transfers between devices  33.8 us (30%)
  Pallas kernels  31.2 us (28%)
  other arithmetic  3.89 us (4%)
  between operations  1.26 us (1%)
    ppermute x36, waiting for transfers between devices, swap(): lax.ppermute(array, BOTH, [(device, device ^ masks[device % 2]) for devic...  39.3 us
    ppermute x36, starting transfers between devices, swap(): lax.ppermute(array, BOTH, [(device, device ^ masks[device % 2]) for devic...  31.2 us
    pallas_call x12, Pallas kernels, call(): pl.pallas_call(kernel, out_shape=[jax.ShapeDtypeStruct(s, t) for s, t in...  29.6 us
  transfers between devices with their start and end apart: 38, of which 16 were waited for; matrix products, arithmetic and copies ran while one was open for 4% of the time, Pallas kernels for 26%

profile of v4, /device:TPU:0, one launch (start us, length us, event | category | flops | bytes accessed | tf_op | source)
XLA Modules:
  0.0 110.5 jit_solution(14662888659908296252)
XLA Ops:
  0.7 1.6 %shard_map.279 = bf16[144,512]{1,0:T(8,128)(2,1)} custom-call(bf16[48,512]{1,0:T(8,128)(2,1)} %bitcast.41, bf16[12,16]{1,0:T(8,128)(2,1)} %vec_ref.1, bf16[16,512]{1,0:T(8,128)(2,1)} %bitcast.42, bf16[64,512]{1,0:T(8,128)(2,1)} %up_ref.1), custom_call_target="tpu_custom_call" | custom-call | tf_op jit(solution)/shard_map/pallas_call | solution.py:566
  2.4 5.1 %collective-permute-start.2 = (bf16[1,144,512]{2,1,0:T(8,128)(2,1)}, bf16[1,144,512]{2,1,0:T(8,128)(2,1)S(1)}, u32[]{:S(2)}, u32[]{:S(2)}) collective-permute-start(bf16[1,144,512]{2,1,0:T(8,128)(2,1)} %bitcast.31), channel_id=1, source_target_pairs={{0,24},{1,25},{2,26},{3,27},{4,28},{5,29},{6,30},{7,31},{8,16},{9,... | collective-permute-start | bytes 442376 | tf_op jit(solution)/shard_map/ppermute | solution.py:496
  8.1 1.7 %collective-permute-start.3 = (bf16[1,64,512]{2,1,0:T(8,128)(2,1)}, bf16[1,64,512]{2,1,0:T(8,128)(2,1)S(1)}, u32[]{:S(2)}, u32[]{:S(2)}) collective-permute-start(bf16[1,64,512]{2,1,0:T(8,128)(2,1)} %bitcast.39), channel_id=1, source_target_pairs={{0,2},{1,5},{2,0},{3,7},{4,6},{5,1},{6,4},{7,3},{8,10},{9,13},{10,... | collective-permute-start | bytes 196616 | tf_op jit(solution)/shard_map/ppermute | solution.py:496
  10.8 1.3 %collective-permute-start.8 = (bf16[2,4,16,512]{3,2,1,0:T(8,128)(2,1)S(1)}, bf16[2,4,16,512]{3,2,1,0:T(8,128)(2,1)S(1)}, u32[]{:S(2)}, u32[]{:S(2)}) collective-permute-start(bf16[2,4,16,512]{3,2,1,0:T(8,128)(2,1)S(1)} %get-tuple-element.195), channel_id=1, source_target_pairs={{1,0},{2,1},{3,2},{5,4},{6,5},{7,6},{9,8},{10,9},{11,10},{13,12},{... | collective-permute-start | bytes 393224 | tf_op jit(solution)/shard_map/ppermute | solution.py:544
  12.6 1.7 %collective-permute-start.4 = (bf16[2,64,512]{2,1,0:T(8,128)(2,1)S(1)}, bf16[2,64,512]{2,1,0:T(8,128)(2,1)S(1)}, u32[]{:S(2)}, u32[]{:S(2)}) collective-permute-start(bf16[2,64,512]{2,1,0:T(8,128)(2,1)S(1)} %pad_maximum_fusion.6), channel_id=1, source_target_pairs={{0,4},{1,3},{2,6},{3,1},{4,0},{5,7},{6,2},{7,5},{8,12},{9,11},{10,... | collective-permute-start | bytes 393224 | tf_op jit(solution)/shard_map/ppermute | solution.py:496
  14.6 1.3 %collective-permute-start.7 = (bf16[2,4,16,512]{3,2,1,0:T(8,128)(2,1)S(1)}, bf16[2,4,16,512]{3,2,1,0:T(8,128)(2,1)S(1)}, u32[]{:S(2)}, u32[]{:S(2)}) collective-permute-start(bf16[2,4,16,512]{3,2,1,0:T(8,128)(2,1)S(1)} %get-tuple-element.196), channel_id=1, source_target_pairs={{0,1},{1,2},{2,3},{4,5},{5,6},{6,7},{8,9},{9,10},{10,11},{12,13},{... | collective-permute-start | bytes 393224 | tf_op jit(solution)/shard_map/ppermute | solution.py:543
  15.9 4.3 %collective-permute-done = bf16[1,144,512]{2,1,0:T(8,128)(2,1)S(1)} collective-permute-done((bf16[1,144,512]{2,1,0:T(8,128)(2,1)}, bf16[1,144,512]{2,1,0:T(8,128)(2,1)S(1)}, u32[]{:S(2)}, u32[]{:S(2)}) %collective-permute-start) | collective-permute-done | bytes 147488 | tf_op jit(solution)/shard_map/ppermute | solution.py:496
  20.4 1.6 %collective-permute-start.5 = (bf16[4,144,512]{2,1,0:T(8,128)(2,1)S(1)}, bf16[4,144,512]{2,1,0:T(8,128)(2,1)S(1)}, u32[]{:S(2)}, u32[]{:S(2)}) collective-permute-start(bf16[4,144,512]{2,1,0:T(8,128)(2,1)S(1)} %pad_maximum_fusion.2), channel_id=1, source_target_pairs={{0,4},{1,3},{2,6},{3,1},{4,0},{5,7},{6,2},{7,5},{8,12},{9,11},{10,... | collective-permute-start | bytes 1769480 | tf_op jit(solution)/shard_map/ppermute | solution.py:496
  22.7 9.1 %collective-permute-done.6 = bf16[4,64,512]{2,1,0:T(8,128)(2,1)S(1)} collective-permute-done((bf16[4,64,512]{2,1,0:T(8,128)(2,1)S(1)}, bf16[4,64,512]{2,1,0:T(8,128)(2,1)S(1)}, u32[]{:S(2)}, u32[]{:S(2)}) %collective-permute-start.6) | collective-permute-done | bytes 262176 | tf_op jit(solution)/shard_map/ppermute | solution.py:496
  31.9 1.6 %collective-permute-start.9 = (bf16[8,64,512]{2,1,0:T(8,128)(2,1)S(1)}, bf16[8,64,512]{2,1,0:T(8,128)(2,1)S(1)}, u32[]{:S(2)}, u32[]{:S(2)}) collective-permute-start(bf16[8,64,512]{2,1,0:T(8,128)(2,1)S(1)} %slice.106), channel_id=1, source_target_pairs={{0,2},{1,5},{2,0},{3,7},{4,6},{5,1},{6,4},{7,3},{8,10},{9,13},{10,... | collective-permute-start | bytes 1572872 | tf_op jit(solution)/shard_map/ppermute | solution.py:496
  34.2 6.9 %collective-permute-done.9.refs_1_ = bf16[8,64,512]{2,1,0:T(8,128)(2,1)S(1)} collective-permute-done((bf16[8,64,512]{2,1,0:T(8,128)(2,1)S(1)}, bf16[8,64,512]{2,1,0:T(8,128)(2,1)S(1)}, u32[]{:S(2)}, u32[]{:S(2)}) %collective-permute-start.9) | collective-permute-done | bytes 524320 | tf_op jit(solution)/shard_map/ppermute | solution.py:496
  41.3 1.8 %collective-permute-done.11.refs_3_ = bf16[8,64,512]{2,1,0:T(8,128)(2,1)S(1)} collective-permute-done((bf16[8,64,512]{2,1,0:T(8,128)(2,1)S(1)}, bf16[8,64,512]{2,1,0:T(8,128)(2,1)S(1)}, u32[]{:S(2)}, u32[]{:S(2)}) %collective-permute-start.11) | collective-permute-done | bytes 524320 | tf_op jit(solution)/shard_map/ppermute | solution.py:496
  43.1 5.1 %shard_map.280 = (bf16[640,1536]{1,0:T(8,128)(2,1)S(1)}, f32[20,2,32,256]{3,2,1,0:T(8,128)S(1)}, bf16[640,512]{1,0:T(8,128)(2,1)S(1)}, bf16[640,512]{1,0:T(8,128...) custom-call(s32[32]{0:T(128)S(1)} %get-tuple-element.109.own_ref, ...), custom_call_target="tpu_custom_call" | custom-call | flops 110000000 | bytes 1048576 | tf_op jit(solution)/shard_map/pallas_call | solution.py:482
  49.7 1.4 %collective-permute-done.14.refs_3_ = bf16[8,80,512]{2,1,0:T(8,128)(2,1)S(1)} collective-permute-done((bf16[8,80,512]{2,1,0:T(8,128)(2,1)S(1)}, bf16[8,80,512]{2,1,0:T(8,128)(2,1)S(1)}, u32[]{:S(2)}, u32[]{:S(2)}) %collective-permute-start.14) | collective-permute-done | bytes 655392 | tf_op jit(solution)/shard_map/ppermute | solution.py:496
  51.1 5.5 %shard_map.281 = (bf16[16,64,512]{2,1,0:T(8,128)(2,1)S(1)}, bf16[16,64,512]{2,1,0:T(8,128)(2,1)S(1)}, f32[640,512]{1,0:T(8,128)S(1)}, bf16[640,2048]{1,0:T(8,128...) custom-call(s32[32]{0:T(128)S(1)} %get-tuple-element.109.own_ref, ...), custom_call_target="tpu_custom_call" | custom-call | flops 8800000000 | bytes 1048576 | tf_op jit(solution)/shard_map/pallas_call | solution.py:482
  56.8 3.8 %shard_map.282 = (bf16[16,64,512]{2,1,0:T(8,128)(2,1)S(1)}, bf16[16,64,512]{2,1,0:T(8,128)(2,1)S(1)}, bf16[640,2048]{1,0:T(8,128)(2,1)S(1)}, bf16[512,2048]{1,0:T(8,128)(2,1)S(1)}, f32[8,512]{1,0:T(8,128)S(1)}) custom-call(s32[32]{0:T(128)S(1)} %get-tuple-element.120.own_ref, s32[32]{0:T(128)S(1)} %get-tuple-element.112.own_down_ref, ...), custom_call_target="tpu_custom_call" | custom-call | flops 8800000000 | bytes 1048576 | tf_op jit(solution)/shard_map/pallas_call | solution.py:482
  61.5 2.6 %shard_map.283 = (f32[512,512]{1,0:T(8,128)S(1)}, f32[640,512]{1,0:T(8,128)S(1)}) custom-call(bf16[640,2048]{1,0:T(8,128)(2,1)S(1)} %get-tuple-element.119.hid_ref, bf16[640,2048]{1,0:T(8,128)(2,1)S(1)} %get-tuple-element.130.gpre_ref, bf16[512,2048]{1,0:T(8,128)(2,1)S(1)} %get-tuple-element.131.up_ref, bf16[512,2048]{1,0:T(8,128)(2,1)S(1)} %get-tuple-element.132.down_ref), custom_call_target="tpu_custom_call" | custom-call | flops 110000000 | bytes 1048576 | tf_op jit(solution)/shard_map/pallas_call | solution.py:482
  65.4 1.9 %shard_map.284 = (bf16[512,512]{1,0:T(8,128)(2,1)}, f32[640,512]{1,0:T(8,128)S(1)}, bf16[512,512]{1,0:T(8,128)(2,1)S(1)}, bf16[640,512]{1,0:T(8,128)(2,1)S(1)}, f32[8,512]{1,0:T(8,128)S(1)}) custom-call(f32[640,128]{1,0:T(8,128)S(1)} %broadcast_in_dim.59.keep_ref, bf16[640,512]{1,0:T(8,128)(2,1)S(1)} %pad_maximum_fusion.cot_ref, ...), custom_call_target="tpu_custom_call" | custom-call | flops 110000000 | bytes 1048576 | tf_op jit(solution)/shard_map/pallas_call | solution.py:482
  67.3 2.5 %shard_map.286.gproj_b = bf16[256,1536]{1,0:T(8,128)(2,1)S(1)} custom-call(bf16[640,512]{1,0:T(8,128)(2,1)S(1)} %get-tuple-element.143.gmix_ref, bf16[640,1536]{1,0:T(8,128)(2,1)S(1)} %get-tuple-element.144.proj_ref, f32[20,2,32,256]{3,2,1,0:T(8,128)S(1)} %get-tuple-element.145.prob_ref), custom_call_target="tpu_custom_call" | custom-call | flops 110000000 | bytes 1048576 | tf_op jit(solution)/shard_map/pallas_call | solution.py:482
  69.7 2.5 %shard_map.285.gproj_a = bf16[256,1536]{1,0:T(8,128)(2,1)S(1)} custom-call(bf16[640,512]{1,0:T(8,128)(2,1)S(1)} %get-tuple-element.143.gmix_ref, bf16[640,1536]{1,0:T(8,128)(2,1)S(1)} %get-tuple-element.144.proj_ref, f32[20,2,32,256]{3,2,1,0:T(8,128)S(1)} %get-tuple-element.145.prob_ref), custom_call_target="tpu_custom_call" | custom-call | flops 110000000 | bytes 1048576 | tf_op jit(solution)/shard_map/pallas_call | solution.py:482
  72.2 1.5 %collective-permute-done.19 = bf16[8,64,512]{2,1,0:T(8,128)(2,1)S(1)} collective-permute-done((bf16[8,64,512]{2,1,0:T(8,128)(2,1)S(1)}, bf16[8,64,512]{2,1,0:T(8,128)(2,1)S(1)}, u32[]{:S(2)}, u32[]{:S(2)}) %collective-permute-start.19) | collective-permute-done | bytes 524320 | tf_op jit(solution)/shard_map/ppermute | solution.py:496
  74.0 1.5 %collective-permute-start.20 = (bf16[4,64,512]{2,1,0:T(8,128)(2,1)S(1)}, bf16[4,64,512]{2,1,0:T(8,128)(2,1)S(1)}, u32[]{:S(2)}, u32[]{:S(2)}) collective-permute-start(bf16[4,64,512]{2,1,0:T(8,128)(2,1)S(1)} %slice.150), channel_id=1, source_target_pairs={{0,2},{1,5},{2,0},{3,7},{4,6},{5,1},{6,4},{7,3},{8,10},{9,13},{10,... | collective-permute-start | bytes 786440 | tf_op jit(solution)/shard_map/ppermute | solution.py:496
  75.5 2.5 %shard_map.287 = (bf16[1040,512]{1,0:T(8,128)(2,1)S(1)}, bf16[208,512]{1,0:T(8,128)(2,1)S(1)}, bf16[208,512]{1,0:T(8,128)(2,1)S(1)}, bf16[208,512]{1,0:T(8,128)(...) custom-call(s32[32]{0:T(128)S(1)} %get-tuple-element.150.own_ref, ...), custom_call_target="tpu_custom_call" | custom-call | flops 110000000 | bytes 1048576 | tf_op jit(solution)/shard_map/pallas_call | solution.py:482
  78.6 1.8 %collective-permute-done.20 = bf16[4,64,512]{2,1,0:T(8,128)(2,1)S(1)} collective-permute-done((bf16[4,64,512]{2,1,0:T(8,128)(2,1)S(1)}, bf16[4,64,512]{2,1,0:T(8,128)(2,1)S(1)}, u32[]{:S(2)}, u32[]{:S(2)}) %collective-permute-start.20) | collective-permute-done | bytes 262176 | tf_op jit(solution)/shard_map/ppermute | solution.py:496
  82.5 1.2 %collective-permute-start.27 = (bf16[6,64,512]{2,1,0:T(8,128)(2,1)S(1)}, bf16[6,64,512]{2,1,0:T(8,128)(2,1)S(1)}, u32[]{:S(2)}, u32[]{:S(2)}) collective-permute-start(bf16[6,64,512]{2,1,0:T(8,128)(2,1)S(1)} %pad_maximum_fusion.3), channel_id=1, source_target_pairs={{0,16},{1,9},{2,18},{3,11},{4,20},{5,13},{6,22},{7,15},{8,24},{9,1... | collective-permute-start | bytes 1179656 | tf_op jit(solution)/shard_map/ppermute | solution.py:496
  84.0 1.6 %collective-permute-start.28 = (bf16[272,512]{1,0:T(8,128)(2,1)S(1)}, bf16[272,512]{1,0:T(8,128)(2,1)S(1)}, u32[]{:S(2)}, u32[]{:S(2)}) collective-permute-start(bf16[272,512]{1,0:T(8,128)(2,1)S(1)} %get-tuple-element.178), channel_id=1, source_target_pairs={{0,2},{1,3},{2,0},{3,1},{4,6},{5,7},{6,4},{7,5},{8,10},{9,11},{10,... | collective-permute-start | bytes 835592 | tf_op jit(solution)/shard_map/ppermute | solution.py:496
  87.6 2.2 %shard_map.288 = f32[512,512]{1,0:T(8,128)} custom-call(bf16[256,1536]{1,0:T(8,128)(2,1)S(1)} %shard_map.285.gproj_a, bf16[256,1536]{1,0:T(8,128)(2,1)S(1)} %shard_map.286.gproj_b, bf16[640,512]{1,0:T(8,128)(2,1)S(1)} %pad_maximum_fusion.1.x_ref, f32[640,512]{1,0:T(8,128)S(1)} %get-tuple-element.169.gres_ref, ...), custom_call_target="tpu_custom_call" | custom-call | flops 110000000 | bytes 1048576 | tf_op jit(solution)/shard_map/pallas_call | solution.py:482
  89.8 5.7 %collective-permute-done.27 = bf16[6,64,512]{2,1,0:T(8,128)(2,1)S(1)} collective-permute-done((bf16[6,64,512]{2,1,0:T(8,128)(2,1)S(1)}, bf16[6,64,512]{2,1,0:T(8,128)(2,1)S(1)}, u32[]{:S(2)}, u32[]{:S(2)}) %collective-permute-start.27) | collective-permute-done | bytes 393248 | tf_op jit(solution)/shard_map/ppermute | solution.py:496
  95.8 1.5 %collective-permute-start.35 = (bf16[1,64,512]{2,1,0:T(8,128)(2,1)S(1)}, bf16[1,64,512]{2,1,0:T(8,128)(2,1)S(1)}, u32[]{:S(2)}, u32[]{:S(2)}) collective-permute-start(bf16[1,64,512]{2,1,0:T(8,128)(2,1)S(1)} %get-tuple-element.197), channel_id=1, source_target_pairs={{0,2},{1,5},{2,0},{3,7},{4,6},{5,1},{6,4},{7,3},{8,10},{9,13},{10,... | collective-permute-start | bytes 196616 | tf_op jit(solution)/shard_map/ppermute | solution.py:496
  100.7 2.4 %collective-permute-start.32 = (bf16[80,512]{1,0:T(8,128)(2,1)S(1)}, bf16[80,512]{1,0:T(8,128)(2,1)S(1)}, u32[]{:S(2)}, u32[]{:S(2)}) collective-permute-start(bf16[80,512]{1,0:T(8,128)(2,1)S(1)} %get-tuple-element.186), channel_id=1, source_target_pairs={{0,16},{1,17},{2,18},{3,19},{4,20},{5,21},{6,22},{7,23},{8,24},{9,... | collective-permute-start | bytes 245768 | tf_op jit(solution)/shard_map/ppermute | solution.py:496
  103.5 1.7 %collective-permute-start.34 = (bf16[80,512]{1,0:T(8,128)(2,1)S(1)}, bf16[80,512]{1,0:T(8,128)(2,1)S(1)}, u32[]{:S(2)}, u32[]{:S(2)}) collective-permute-start(bf16[80,512]{1,0:T(8,128)(2,1)S(1)} %get-tuple-element.188), channel_id=1, source_target_pairs={{0,24},{1,25},{2,26},{3,27},{4,28},{5,29},{6,30},{7,31},{8,16},{9,... | collective-permute-start | bytes 245768 | tf_op jit(solution)/shard_map/ppermute | solution.py:496
  107.7 2.1 %collective-permute-done.34.refs_3_ = bf16[80,512]{1,0:T(8,128)(2,1)S(1)} collective-permute-done((bf16[80,512]{1,0:T(8,128)(2,1)S(1)}, bf16[80,512]{1,0:T(8,128)(2,1)S(1)}, u32[]{:S(2)}, u32[]{:S(2)}) %collective-permute-start.34) | collective-permute-done | bytes 81952 | tf_op jit(solution)/shard_map/ppermute | solution.py:496
  (129 shorter events, 20.3 us)
Async XLA Ops:
  2.4 12.2 %collective-permute-start.2 = (bf16[1,144,512]{2,1,0:T(8,128)(2,1)}, bf16[1,144,512]{2,1,0:T(8,128)(2,1)S(1)}, u32[]{:S(2)}, u32[]{:S(2)}) collective-permute-start(bf16[1,144,512]{2,1,0:T(8,128)(2,1)} %bitcast.31), channel_id=1, source_target_pairs={{0,24},{1,25},{2,26},{3,27},{4,28},{5,29},{6,30},{7,31},{8,16},{9,... | collective-permute-start | bytes 442376 | tf_op jit(solution)/shard_map/ppermute | solution.py:496
  7.5 8.4 %collective-permute-start.1 = (bf16[1,144,512]{2,1,0:T(8,128)(2,1)}, bf16[1,144,512]{2,1,0:T(8,128)(2,1)S(1)}, u32[]{:S(2)}, u32[]{:S(2)}) collective-permute-start(bf16[1,144,512]{2,1,0:T(8,128)(2,1)} %bitcast.32), channel_id=1, source_target_pairs={{0,8},{1,9},{2,10},{3,11},{4,12},{5,13},{6,14},{7,15},{8,0},{9,1},... | collective-permute-start | bytes 442376 | tf_op jit(solution)/shard_map/ppermute | solution.py:496
  7.5 12.7 %collective-permute-start = (bf16[1,144,512]{2,1,0:T(8,128)(2,1)}, bf16[1,144,512]{2,1,0:T(8,128)(2,1)S(1)}, u32[]{:S(2)}, u32[]{:S(2)}) collective-permute-start(bf16[1,144,512]{2,1,0:T(8,128)(2,1)} %bitcast.33), channel_id=1, source_target_pairs={{0,16},{1,17},{2,18},{3,19},{4,20},{5,21},{6,22},{7,23},{8,24},{9,... | collective-permute-start | bytes 442376 | tf_op jit(solution)/shard_map/ppermute | solution.py:496
  8.1 4.5 %collective-permute-start.3 = (bf16[1,64,512]{2,1,0:T(8,128)(2,1)}, bf16[1,64,512]{2,1,0:T(8,128)(2,1)S(1)}, u32[]{:S(2)}, u32[]{:S(2)}) collective-permute-start(bf16[1,64,512]{2,1,0:T(8,128)(2,1)} %bitcast.39), channel_id=1, source_target_pairs={{0,2},{1,5},{2,0},{3,7},{4,6},{5,1},{6,4},{7,3},{8,10},{9,13},{10,... | collective-permute-start | bytes 196616 | tf_op jit(solution)/shard_map/ppermute | solution.py:496
  10.8 11.9 %collective-permute-start.8 = (bf16[2,4,16,512]{3,2,1,0:T(8,128)(2,1)S(1)}, bf16[2,4,16,512]{3,2,1,0:T(8,128)(2,1)S(1)}, u32[]{:S(2)}, u32[]{:S(2)}) collective-permute-start(bf16[2,4,16,512]{3,2,1,0:T(8,128)(2,1)S(1)} %get-tuple-element.195), channel_id=1, source_target_pairs={{1,0},{2,1},{3,2},{5,4},{6,5},{7,6},{9,8},{10,9},{11,10},{13,12},{... | collective-permute-start | bytes 393224 | tf_op jit(solution)/shard_map/ppermute | solution.py:544
  12.6 7.6 %collective-permute-start.4 = (bf16[2,64,512]{2,1,0:T(8,128)(2,1)S(1)}, bf16[2,64,512]{2,1,0:T(8,128)(2,1)S(1)}, u32[]{:S(2)}, u32[]{:S(2)}) collective-permute-start(bf16[2,64,512]{2,1,0:T(8,128)(2,1)S(1)} %pad_maximum_fusion.6), channel_id=1, source_target_pairs={{0,4},{1,3},{2,6},{3,1},{4,0},{5,7},{6,2},{7,5},{8,12},{9,11},{10,... | collective-permute-start | bytes 393224 | tf_op jit(solution)/shard_map/ppermute | solution.py:496
  14.6 8.0 %collective-permute-start.7 = (bf16[2,4,16,512]{3,2,1,0:T(8,128)(2,1)S(1)}, bf16[2,4,16,512]{3,2,1,0:T(8,128)(2,1)S(1)}, u32[]{:S(2)}, u32[]{:S(2)}) collective-permute-start(bf16[2,4,16,512]{3,2,1,0:T(8,128)(2,1)S(1)} %get-tuple-element.196), channel_id=1, source_target_pairs={{0,1},{1,2},{2,3},{4,5},{5,6},{6,7},{8,9},{9,10},{10,11},{12,13},{... | collective-permute-start | bytes 393224 | tf_op jit(solution)/shard_map/ppermute | solution.py:543
  20.4 11.3 %collective-permute-start.5 = (bf16[4,144,512]{2,1,0:T(8,128)(2,1)S(1)}, bf16[4,144,512]{2,1,0:T(8,128)(2,1)S(1)}, u32[]{:S(2)}, u32[]{:S(2)}) collective-permute-start(bf16[4,144,512]{2,1,0:T(8,128)(2,1)S(1)} %pad_maximum_fusion.2), channel_id=1, source_target_pairs={{0,4},{1,3},{2,6},{3,1},{4,0},{5,7},{6,2},{7,5},{8,12},{9,11},{10,... | collective-permute-start | bytes 1769480 | tf_op jit(solution)/shard_map/ppermute | solution.py:496
  22.0 9.7 %collective-permute-start.6 = (bf16[4,64,512]{2,1,0:T(8,128)(2,1)S(1)}, bf16[4,64,512]{2,1,0:T(8,128)(2,1)S(1)}, u32[]{:S(2)}, u32[]{:S(2)}) collective-permute-start(bf16[4,64,512]{2,1,0:T(8,128)(2,1)S(1)} %constant_dynamic-update-slice_fusion), channel_id=1, source_target_pairs={{0,16},{1,9},{2,18},{3,11},{4,20},{5,13},{6,22},{7,15},{8,24},{9,1... | collective-permute-start | bytes 786440 | tf_op jit(solution)/shard_map/ppermute | solution.py:496
  31.8 11.3 %collective-permute-start.10 = (bf16[8,144,512]{2,1,0:T(8,128)(2,1)S(1)}, bf16[8,144,512]{2,1,0:T(8,128)(2,1)S(1)}, u32[]{:S(2)}, u32[]{:S(2)}) collective-permute-start(bf16[8,144,512]{2,1,0:T(8,128)(2,1)S(1)} %constant_dynamic-update-slice_fusion.4.refs_0_), channel_id=1, source_target_pairs={{0,1},{1,0},{2,3},{3,2},{4,5},{5,4},{6,7},{7,6},{8,9},{9,8},{10,11... | collective-permute-start | bytes 3538952 | tf_op jit(solution)/shard_map/ppermute | solution.py:496
  31.9 9.2 %collective-permute-start.9 = (bf16[8,64,512]{2,1,0:T(8,128)(2,1)S(1)}, bf16[8,64,512]{2,1,0:T(8,128)(2,1)S(1)}, u32[]{:S(2)}, u32[]{:S(2)}) collective-permute-start(bf16[8,64,512]{2,1,0:T(8,128)(2,1)S(1)} %slice.106), channel_id=1, source_target_pairs={{0,2},{1,5},{2,0},{3,7},{4,6},{5,1},{6,4},{7,3},{8,10},{9,13},{10,... | collective-permute-start | bytes 1572872 | tf_op jit(solution)/shard_map/ppermute | solution.py:496
  33.5 15.5 %collective-permute-start.12 = (bf16[8,80,512]{2,1,0:T(8,128)(2,1)S(1)}, bf16[8,80,512]{2,1,0:T(8,128)(2,1)S(1)}, u32[]{:S(2)}, u32[]{:S(2)}) collective-permute-start(bf16[8,80,512]{2,1,0:T(8,128)(2,1)S(1)} %slice.107), channel_id=1, source_target_pairs={{0,2},{1,5},{2,0},{3,7},{4,6},{5,1},{6,4},{7,3},{8,10},{9,13},{10,... | collective-permute-start | bytes 1966088 | tf_op jit(solution)/shard_map/ppermute | solution.py:496
  34.2 14.9 %collective-permute-start.13 = (bf16[8,64,512]{2,1,0:T(8,128)(2,1)S(1)}, bf16[8,64,512]{2,1,0:T(8,128)(2,1)S(1)}, u32[]{:S(2)}, u32[]{:S(2)}) collective-permute-start(bf16[8,64,512]{2,1,0:T(8,128)(2,1)S(1)} %constant_dynamic-update-slice_fusion.9.refs_0_), channel_id=1, source_target_pairs={{0,8},{1,17},{2,10},{3,19},{4,12},{5,21},{6,14},{7,23},{8,0},{9,25... | collective-permute-start | bytes 1572872 | tf_op jit(solution)/shard_map/ppermute | solution.py:496
  49.1 7.7 %collective-permute-start.15 = (bf16[8,64,512]{2,1,0:T(8,128)(2,1)S(1)}, bf16[8,64,512]{2,1,0:T(8,128)(2,1)S(1)}, u32[]{:S(2)}, u32[]{:S(2)}) collective-permute-start(bf16[8,64,512]{2,1,0:T(8,128)(2,1)S(1)} %constant_dynamic-update-slice_fusion.9.refs_0_), channel_id=1, source_target_pairs={{0,1},{1,0},{2,3},{3,2},{4,5},{5,4},{6,7},{7,6},{8,9},{9,8},{10,11... | collective-permute-start | bytes 1572872 | tf_op jit(solution)/shard_map/ppermute | solution.py:496
  49.6 7.1 %collective-permute-start.16 = (bf16[8,64,512]{2,1,0:T(8,128)(2,1)S(1)}, bf16[8,64,512]{2,1,0:T(8,128)(2,1)S(1)}, u32[]{:S(2)}, u32[]{:S(2)}) collective-permute-start(bf16[8,64,512]{2,1,0:T(8,128)(2,1)S(1)} %collective-permute-done.13.refs_1_), channel_id=1, source_target_pairs={{0,1},{1,0},{2,3},{3,2},{4,5},{5,4},{6,7},{7,6},{8,9},{9,8},{10,11... | collective-permute-start | bytes 1572872 | tf_op jit(solution)/shard_map/ppermute | solution.py:496
  56.6 4.5 %collective-permute-start.17 = (bf16[16,64,512]{2,1,0:T(8,128)(2,1)S(1)}, bf16[16,64,512]{2,1,0:T(8,128)(2,1)S(1)}, u32[]{:S(2)}, u32[]{:S(2)}) collective-permute-start(bf16[16,64,512]{2,1,0:T(8,128)(2,1)S(1)} %get-tuple-element.128), channel_id=1, source_target_pairs={{0,1},{1,0},{2,3},{3,2},{4,5},{5,4},{6,7},{7,6},{8,9},{9,8},{10,11... | collective-permute-start | bytes 3145736 | tf_op jit(solution)/shard_map/ppermute | solution.py:496
  60.6 3.5 %collective-permute-start.18 = (bf16[16,64,512]{2,1,0:T(8,128)(2,1)S(1)}, bf16[16,64,512]{2,1,0:T(8,128)(2,1)S(1)}, u32[]{:S(2)}, u32[]{:S(2)}) collective-permute-start(bf16[16,64,512]{2,1,0:T(8,128)(2,1)S(1)} %get-tuple-element.136), channel_id=1, source_target_pairs={{0,1},{1,0},{2,3},{3,2},{4,5},{5,4},{6,7},{7,6},{8,9},{9,8},{10,11... | collective-permute-start | bytes 3145736 | tf_op jit(solution)/shard_map/ppermute | solution.py:496
  64.5 9.2 %collective-permute-start.19 = (bf16[8,64,512]{2,1,0:T(8,128)(2,1)S(1)}, bf16[8,64,512]{2,1,0:T(8,128)(2,1)S(1)}, u32[]{:S(2)}, u32[]{:S(2)}) collective-permute-start(bf16[8,64,512]{2,1,0:T(8,128)(2,1)S(1)} %slice.147), channel_id=1, source_target_pairs={{0,4},{1,3},{2,6},{3,1},{4,0},{5,7},{6,2},{7,5},{8,12},{9,11},{10,... | collective-permute-start | bytes 1572872 | tf_op jit(solution)/shard_map/ppermute | solution.py:496
  65.4 15.1 %collective-permute-start.21 = (bf16[8,64,512]{2,1,0:T(8,128)(2,1)S(1)}, bf16[8,64,512]{2,1,0:T(8,128)(2,1)S(1)}, u32[]{:S(2)}, u32[]{:S(2)}) collective-permute-start(bf16[8,64,512]{2,1,0:T(8,128)(2,1)S(1)} %slice.148), channel_id=1, source_target_pairs={{0,8},{1,17},{2,10},{3,19},{4,12},{5,21},{6,14},{7,23},{8,0},{9,25... | collective-permute-start | bytes 1572872 | tf_op jit(solution)/shard_map/ppermute | solution.py:496
  74.0 6.4 %collective-permute-start.20 = (bf16[4,64,512]{2,1,0:T(8,128)(2,1)S(1)}, bf16[4,64,512]{2,1,0:T(8,128)(2,1)S(1)}, u32[]{:S(2)}, u32[]{:S(2)}) collective-permute-start(bf16[4,64,512]{2,1,0:T(8,128)(2,1)S(1)} %slice.150), channel_id=1, source_target_pairs={{0,2},{1,5},{2,0},{3,7},{4,6},{5,1},{6,4},{7,3},{8,10},{9,13},{10,... | collective-permute-start | bytes 786440 | tf_op jit(solution)/shard_map/ppermute | solution.py:496
  78.0 2.9 %collective-permute-start.22 = (bf16[208,512]{1,0:T(8,128)(2,1)S(1)}, bf16[208,512]{1,0:T(8,128)(2,1)S(1)}, u32[]{:S(2)}, u32[]{:S(2)}) collective-permute-start(bf16[208,512]{1,0:T(8,128)(2,1)S(1)} %get-tuple-element.161), channel_id=1, source_target_pairs={{0,1},{1,0},{2,3},{3,2},{4,5},{5,4},{6,7},{7,6},{8,9},{9,8},{10,11... | collective-permute-start | bytes 638984 | tf_op jit(solution)/shard_map/ppermute | solution.py:496
  82.5 12.9 %collective-permute-start.27 = (bf16[6,64,512]{2,1,0:T(8,128)(2,1)S(1)}, bf16[6,64,512]{2,1,0:T(8,128)(2,1)S(1)}, u32[]{:S(2)}, u32[]{:S(2)}) collective-permute-start(bf16[6,64,512]{2,1,0:T(8,128)(2,1)S(1)} %pad_maximum_fusion.3), channel_id=1, source_target_pairs={{0,16},{1,9},{2,18},{3,11},{4,20},{5,13},{6,22},{7,15},{8,24},{9,1... | collective-permute-start | bytes 1179656 | tf_op jit(solution)/shard_map/ppermute | solution.py:496
  84.0 13.3 %collective-permute-start.28 = (bf16[272,512]{1,0:T(8,128)(2,1)S(1)}, bf16[272,512]{1,0:T(8,128)(2,1)S(1)}, u32[]{:S(2)}, u32[]{:S(2)}) collective-permute-start(bf16[272,512]{1,0:T(8,128)(2,1)S(1)} %get-tuple-element.178), channel_id=1, source_target_pairs={{0,2},{1,3},{2,0},{3,1},{4,6},{5,7},{6,4},{7,5},{8,10},{9,11},{10,... | collective-permute-start | bytes 835592 | tf_op jit(solution)/shard_map/ppermute | solution.py:496
  85.6 12.6 %collective-permute-start.29 = (bf16[272,512]{1,0:T(8,128)(2,1)S(1)}, bf16[272,512]{1,0:T(8,128)(2,1)S(1)}, u32[]{:S(2)}, u32[]{:S(2)}) collective-permute-start(bf16[272,512]{1,0:T(8,128)(2,1)S(1)} %get-tuple-element.179), channel_id=1, source_target_pairs={{0,4},{1,5},{2,6},{3,7},{4,0},{5,1},{6,2},{7,3},{8,12},{9,13},{10,... | collective-permute-start | bytes 835592 | tf_op jit(solution)/shard_map/ppermute | solution.py:496
  86.6 14.0 %collective-permute-start.30 = (bf16[272,512]{1,0:T(8,128)(2,1)S(1)}, bf16[272,512]{1,0:T(8,128)(2,1)S(1)}, u32[]{:S(2)}, u32[]{:S(2)}) collective-permute-start(bf16[272,512]{1,0:T(8,128)(2,1)S(1)} %get-tuple-element.180), channel_id=1, source_target_pairs={{0,6},{1,7},{2,4},{3,5},{4,2},{5,3},{6,0},{7,1},{8,14},{9,15},{10,... | collective-permute-start | bytes 835592 | tf_op jit(solution)/shard_map/ppermute | solution.py:496
  95.7 4.9 %collective-permute-start.31 = (bf16[1,64,512]{2,1,0:T(8,128)(2,1)S(1)}, bf16[1,64,512]{2,1,0:T(8,128)(2,1)S(1)}, u32[]{:S(2)}, u32[]{:S(2)}) collective-permute-start(bf16[1,64,512]{2,1,0:T(8,128)(2,1)S(1)} %slice.152), channel_id=1, source_target_pairs={{0,8},{1,17},{2,10},{3,19},{4,12},{5,21},{6,14},{7,23},{8,0},{9,25... | collective-permute-start | bytes 196616 | tf_op jit(solution)/shard_map/ppermute | solution.py:496
  95.8 7.7 %collective-permute-start.35 = (bf16[1,64,512]{2,1,0:T(8,128)(2,1)S(1)}, bf16[1,64,512]{2,1,0:T(8,128)(2,1)S(1)}, u32[]{:S(2)}, u32[]{:S(2)}) collective-permute-start(bf16[1,64,512]{2,1,0:T(8,128)(2,1)S(1)} %get-tuple-element.197), channel_id=1, source_target_pairs={{0,2},{1,5},{2,0},{3,7},{4,6},{5,1},{6,4},{7,3},{8,10},{9,13},{10,... | collective-permute-start | bytes 196616 | tf_op jit(solution)/shard_map/ppermute | solution.py:496
  97.3 7.9 %collective-permute-start.37 = (bf16[1,64,512]{2,1,0:T(8,128)(2,1)S(1)}, bf16[1,64,512]{2,1,0:T(8,128)(2,1)S(1)}, u32[]{:S(2)}, u32[]{:S(2)}) collective-permute-start(bf16[1,64,512]{2,1,0:T(8,128)(2,1)S(1)} %get-tuple-element.198), channel_id=1, source_target_pairs={{0,6},{1,7},{2,4},{3,5},{4,2},{5,3},{6,0},{7,1},{8,14},{9,15},{10,... | collective-permute-start | bytes 196616 | tf_op jit(solution)/shard_map/ppermute | solution.py:496
  98.3 6.9 %collective-permute-start.36 = (bf16[1,64,512]{2,1,0:T(8,128)(2,1)S(1)}, bf16[1,64,512]{2,1,0:T(8,128)(2,1)S(1)}, u32[]{:S(2)}, u32[]{:S(2)}) collective-permute-start(bf16[1,64,512]{2,1,0:T(8,128)(2,1)S(1)} %get-tuple-element.199), channel_id=1, source_target_pairs={{0,4},{1,3},{2,6},{3,1},{4,0},{5,7},{6,2},{7,5},{8,12},{9,11},{10,... | collective-permute-start | bytes 196616 | tf_op jit(solution)/shard_map/ppermute | solution.py:496
  100.7 6.7 %collective-permute-start.32 = (bf16[80,512]{1,0:T(8,128)(2,1)S(1)}, bf16[80,512]{1,0:T(8,128)(2,1)S(1)}, u32[]{:S(2)}, u32[]{:S(2)}) collective-permute-start(bf16[80,512]{1,0:T(8,128)(2,1)S(1)} %get-tuple-element.186), channel_id=1, source_target_pairs={{0,16},{1,17},{2,18},{3,19},{4,20},{5,21},{6,22},{7,23},{8,24},{9,... | collective-permute-start | bytes 245768 | tf_op jit(solution)/shard_map/ppermute | solution.py:496
  103.1 4.6 %collective-permute-start.33 = (bf16[80,512]{1,0:T(8,128)(2,1)S(1)}, bf16[80,512]{1,0:T(8,128)(2,1)S(1)}, u32[]{:S(2)}, u32[]{:S(2)}) collective-permute-start(bf16[80,512]{1,0:T(8,128)(2,1)S(1)} %get-tuple-element.187), channel_id=1, source_target_pairs={{0,8},{1,9},{2,10},{3,11},{4,12},{5,13},{6,14},{7,15},{8,0},{9,1},... | collective-permute-start | bytes 245768 | tf_op jit(solution)/shard_map/ppermute | solution.py:496
  103.5 6.3 %collective-permute-start.34 = (bf16[80,512]{1,0:T(8,128)(2,1)S(1)}, bf16[80,512]{1,0:T(8,128)(2,1)S(1)}, u32[]{:S(2)}, u32[]{:S(2)}) collective-permute-start(bf16[80,512]{1,0:T(8,128)(2,1)S(1)} %get-tuple-element.188), channel_id=1, source_target_pairs={{0,24},{1,25},{2,26},{3,27},{4,28},{5,29},{6,30},{7,31},{8,16},{9,... | collective-permute-start | bytes 245768 | tf_op jit(solution)/shard_map/ppermute | solution.py:496
  (17 other events, 138.5 us)

commit v5 on v4

--- a/solution.py
+++ b/solution.py
@@ -21,6 +21,7 @@
 SCALE = HEAD ** (-0.5)
 INV_ROOT_TWO = 0.7071067811865476
 INV_ROOT_TAU = 0.3989422804014327
+HALF_LOG2_E = -0.7213475204444817
 
 BOTH = ("dp", "tensor")
 SLOTS = 32
@@ -248,7 +249,7 @@
             here = slice(step * 16, step * 16 + 16)
             pre = pre_ref[here, ring] + vec_ref[8 + chunk : 9 + chunk, :]
             phi = 0.5 + 0.5 * lax.erf(pre * INV_ROOT_TWO)
-            slope_ref[here, columns] = (phi + pre * (jnp.exp(-0.5 * pre * pre) * INV_ROOT_TAU)).astype(bf16)
+            slope_ref[here, columns] = (phi + pre * (jnp.exp2((pre * HALF_LOG2_E) * pre) * INV_ROOT_TAU)).astype(bf16)
             hid_ref[here, columns] = (pre * phi).astype(bf16)
             if step % 10 == 9:
                 yield
@@ -500,10 +501,15 @@
 ALONG_XY = (ALONG_Y, ALONG_X, ALONG_Y ^ ALONG_X)
 
 
+AT_XY = (ALONG_XY[2], ALONG_Y, ALONG_X)
+
+
 def owners(device, swapped, line_first=True, turn=None, second_first=True):
     def one(second_core):
         first = ALONG_X if swapped and bool(second_core) == second_first else ALONG_Y
         plane = [0, first, first ^ ALONG_XY[2], ALONG_XY[2]]
+        if not swapped:
+            plane = [0, *AT_XY]
         line = [0, *ALONG_Z]
         if turn is not None and second_core != turn:
             line = [line[0], line[2], line[1], line[3]]
@@ -694,7 +700,7 @@
         )
         dn_sum = dn_sum[: NEAR // 2] + wide(dn_arrived)
         up_sum = up_sum[:PIECE] + wide(up_arrived)
-        at_arrived = [swap(piece, mask) for piece, mask in zip(at_rest, ALONG_XY)]
+        at_arrived = [swap(piece, mask) for piece, mask in zip(at_rest, AT_XY)]
         ff_arrived = jnp.concatenate([dn_sum[PIECE:], up_sum[2:]], axis=0).astype(bf16)
         ff_arrived = swap(ff_arrived, ALONG_Z[0], ALONG_Z[1])
         ff_arrived, gtok = lax.optimization_barrier((ff_arrived, gtok))

time: 111 us -> 110 us (level)
  no operation moved by 1% of the time
where the time goes in v5:
time: 110 us
  waiting for transfers between devices  38.7 us (35%)
  starting transfers between devices  34.1 us (31%)
  Pallas kernels  31.1 us (28%)
  other arithmetic  3.89 us (4%)
  between operations  1.26 us (1%)
    ppermute x36, waiting for transfers between devices, swap(): lax.ppermute(array, BOTH, [(device, device ^ masks[device % 2]) for devic...  38.7 us
    ppermute x36, starting transfers between devices, swap(): lax.ppermute(array, BOTH, [(device, device ^ masks[device % 2]) for devic...  31.5 us
    pallas_call x12, Pallas kernels, call(): pl.pallas_call(kernel, out_shape=[jax.ShapeDtypeStruct(s, t) for s, t in...  29.5 us
  transfers between devices with their start and end apart: 38, of which 16 were waited for; matrix products, arithmetic and copies ran while one was open for 4% of the time, Pallas kernels for 26%

profile of v5, /device:TPU:0, one launch (start us, length us, event | category | flops | bytes accessed | tf_op | source)
XLA Modules:
  0.0 110.1 jit_solution(11007321826254811596)
XLA Ops:
  0.7 1.6 %shard_map.279 = bf16[144,512]{1,0:T(8,128)(2,1)} custom-call(bf16[48,512]{1,0:T(8,128)(2,1)} %bitcast.41, bf16[12,16]{1,0:T(8,128)(2,1)} %vec_ref.1, bf16[16,512]{1,0:T(8,128)(2,1)} %bitcast.42, bf16[64,512]{1,0:T(8,128)(2,1)} %up_ref.1), custom_call_target="tpu_custom_call" | custom-call | tf_op jit(solution)/shard_map/pallas_call | solution.py:572
  2.4 5.1 %collective-permute-start.2 = (bf16[1,144,512]{2,1,0:T(8,128)(2,1)}, bf16[1,144,512]{2,1,0:T(8,128)(2,1)S(1)}, u32[]{:S(2)}, u32[]{:S(2)}) collective-permute-start(bf16[1,144,512]{2,1,0:T(8,128)(2,1)} %bitcast.31), channel_id=1, source_target_pairs={{0,24},{1,25},{2,26},{3,27},{4,28},{5,29},{6,30},{7,31},{8,16},{9,... | collective-permute-start | bytes 442376 | tf_op jit(solution)/shard_map/ppermute | solution.py:497
  8.1 1.7 %collective-permute-start.3 = (bf16[1,64,512]{2,1,0:T(8,128)(2,1)}, bf16[1,64,512]{2,1,0:T(8,128)(2,1)S(1)}, u32[]{:S(2)}, u32[]{:S(2)}) collective-permute-start(bf16[1,64,512]{2,1,0:T(8,128)(2,1)} %bitcast.39), channel_id=1, source_target_pairs={{0,2},{1,5},{2,0},{3,7},{4,6},{5,1},{6,4},{7,3},{8,10},{9,13},{10,... | collective-permute-start | bytes 196616 | tf_op jit(solution)/shard_map/ppermute | solution.py:497
  10.8 1.3 %collective-permute-start.8 = (bf16[2,4,16,512]{3,2,1,0:T(8,128)(2,1)S(1)}, bf16[2,4,16,512]{3,2,1,0:T(8,128)(2,1)S(1)}, u32[]{:S(2)}, u32[]{:S(2)}) collective-permute-start(bf16[2,4,16,512]{3,2,1,0:T(8,128)(2,1)S(1)} %get-tuple-element.195), channel_id=1, source_target_pairs={{1,0},{2,1},{3,2},{5,4},{6,5},{7,6},{9,8},{10,9},{11,10},{13,12},{... | collective-permute-start | bytes 393224 | tf_op jit(solution)/shard_map/ppermute | solution.py:550
  12.6 1.7 %collective-permute-start.4 = (bf16[2,64,512]{2,1,0:T(8,128)(2,1)S(1)}, bf16[2,64,512]{2,1,0:T(8,128)(2,1)S(1)}, u32[]{:S(2)}, u32[]{:S(2)}) collective-permute-start(bf16[2,64,512]{2,1,0:T(8,128)(2,1)S(1)} %pad_maximum_fusion.6), channel_id=1, source_target_pairs={{0,4},{1,3},{2,6},{3,1},{4,0},{5,7},{6,2},{7,5},{8,12},{9,11},{10,... | collective-permute-start | bytes 393224 | tf_op jit(solution)/shard_map/ppermute | solution.py:497
  14.6 1.3 %collective-permute-start.7 = (bf16[2,4,16,512]{3,2,1,0:T(8,128)(2,1)S(1)}, bf16[2,4,16,512]{3,2,1,0:T(8,128)(2,1)S(1)}, u32[]{:S(2)}, u32[]{:S(2)}) collective-permute-start(bf16[2,4,16,512]{3,2,1,0:T(8,128)(2,1)S(1)} %get-tuple-element.196), channel_id=1, source_target_pairs={{0,1},{1,2},{2,3},{4,5},{5,6},{6,7},{8,9},{9,10},{10,11},{12,13},{... | collective-permute-start | bytes 393224 | tf_op jit(solution)/shard_map/ppermute | solution.py:549
  15.9 4.3 %collective-permute-done = bf16[1,144,512]{2,1,0:T(8,128)(2,1)S(1)} collective-permute-done((bf16[1,144,512]{2,1,0:T(8,128)(2,1)}, bf16[1,144,512]{2,1,0:T(8,128)(2,1)S(1)}, u32[]{:S(2)}, u32[]{:S(2)}) %collective-permute-start) | collective-permute-done | bytes 147488 | tf_op jit(solution)/shard_map/ppermute | solution.py:497
  20.4 1.6 %collective-permute-start.5 = (bf16[4,144,512]{2,1,0:T(8,128)(2,1)S(1)}, bf16[4,144,512]{2,1,0:T(8,128)(2,1)S(1)}, u32[]{:S(2)}, u32[]{:S(2)}) collective-permute-start(bf16[4,144,512]{2,1,0:T(8,128)(2,1)S(1)} %pad_maximum_fusion.2), channel_id=1, source_target_pairs={{0,4},{1,3},{2,6},{3,1},{4,0},{5,7},{6,2},{7,5},{8,12},{9,11},{10,... | collective-permute-start | bytes 1769480 | tf_op jit(solution)/shard_map/ppermute | solution.py:497
  22.7 9.1 %collective-permute-done.6 = bf16[4,64,512]{2,1,0:T(8,128)(2,1)S(1)} collective-permute-done((bf16[4,64,512]{2,1,0:T(8,128)(2,1)S(1)}, bf16[4,64,512]{2,1,0:T(8,128)(2,1)S(1)}, u32[]{:S(2)}, u32[]{:S(2)}) %collective-permute-start.6) | collective-permute-done | bytes 262176 | tf_op jit(solution)/shard_map/ppermute | solution.py:497
  31.9 1.6 %collective-permute-start.9 = (bf16[8,64,512]{2,1,0:T(8,128)(2,1)S(1)}, bf16[8,64,512]{2,1,0:T(8,128)(2,1)S(1)}, u32[]{:S(2)}, u32[]{:S(2)}) collective-permute-start(bf16[8,64,512]{2,1,0:T(8,128)(2,1)S(1)} %slice.106), channel_id=1, source_target_pairs={{0,2},{1,5},{2,0},{3,7},{4,6},{5,1},{6,4},{7,3},{8,10},{9,13},{10,... | collective-permute-start | bytes 1572872 | tf_op jit(solution)/shard_map/ppermute | solution.py:497
  34.2 6.9 %collective-permute-done.9.refs_1_ = bf16[8,64,512]{2,1,0:T(8,128)(2,1)S(1)} collective-permute-done((bf16[8,64,512]{2,1,0:T(8,128)(2,1)S(1)}, bf16[8,64,512]{2,1,0:T(8,128)(2,1)S(1)}, u32[]{:S(2)}, u32[]{:S(2)}) %collective-permute-start.9) | collective-permute-done | bytes 524320 | tf_op jit(solution)/shard_map/ppermute | solution.py:497
  41.3 1.8 %collective-permute-done.11.refs_3_ = bf16[8,64,512]{2,1,0:T(8,128)(2,1)S(1)} collective-permute-done((bf16[8,64,512]{2,1,0:T(8,128)(2,1)S(1)}, bf16[8,64,512]{2,1,0:T(8,128)(2,1)S(1)}, u32[]{:S(2)}, u32[]{:S(2)}) %collective-permute-start.11) | collective-permute-done | bytes 524320 | tf_op jit(solution)/shard_map/ppermute | solution.py:497
  43.1 5.1 %shard_map.280 = (bf16[640,1536]{1,0:T(8,128)(2,1)S(1)}, f32[20,2,32,256]{3,2,1,0:T(8,128)S(1)}, bf16[640,512]{1,0:T(8,128)(2,1)S(1)}, bf16[640,512]{1,0:T(8,128...) custom-call(s32[32]{0:T(128)S(1)} %get-tuple-element.109.own_ref, ...), custom_call_target="tpu_custom_call" | custom-call | flops 110000000 | bytes 1048576 | tf_op jit(solution)/shard_map/pallas_call | solution.py:483
  49.7 1.4 %collective-permute-done.14.refs_3_ = bf16[8,80,512]{2,1,0:T(8,128)(2,1)S(1)} collective-permute-done((bf16[8,80,512]{2,1,0:T(8,128)(2,1)S(1)}, bf16[8,80,512]{2,1,0:T(8,128)(2,1)S(1)}, u32[]{:S(2)}, u32[]{:S(2)}) %collective-permute-start.14) | collective-permute-done | bytes 655392 | tf_op jit(solution)/shard_map/ppermute | solution.py:497
  51.1 5.3 %shard_map.281 = (bf16[16,64,512]{2,1,0:T(8,128)(2,1)S(1)}, bf16[16,64,512]{2,1,0:T(8,128)(2,1)S(1)}, f32[640,512]{1,0:T(8,128)S(1)}, bf16[640,2048]{1,0:T(8,128...) custom-call(s32[32]{0:T(128)S(1)} %get-tuple-element.109.own_ref, ...), custom_call_target="tpu_custom_call" | custom-call | flops 8800000000 | bytes 1048576 | tf_op jit(solution)/shard_map/pallas_call | solution.py:483
  56.6 3.8 %shard_map.282 = (bf16[16,64,512]{2,1,0:T(8,128)(2,1)S(1)}, bf16[16,64,512]{2,1,0:T(8,128)(2,1)S(1)}, bf16[640,2048]{1,0:T(8,128)(2,1)S(1)}, bf16[512,2048]{1,0:T(8,128)(2,1)S(1)}, f32[8,512]{1,0:T(8,128)S(1)}) custom-call(s32[32]{0:T(128)S(1)} %get-tuple-element.120.own_ref, s32[32]{0:T(128)S(1)} %get-tuple-element.112.own_down_ref, ...), custom_call_target="tpu_custom_call" | custom-call | flops 8800000000 | bytes 1048576 | tf_op jit(solution)/shard_map/pallas_call | solution.py:483
  61.3 2.6 %shard_map.283 = (f32[512,512]{1,0:T(8,128)S(1)}, f32[640,512]{1,0:T(8,128)S(1)}) custom-call(bf16[640,2048]{1,0:T(8,128)(2,1)S(1)} %get-tuple-element.119.hid_ref, bf16[640,2048]{1,0:T(8,128)(2,1)S(1)} %get-tuple-element.130.gpre_ref, bf16[512,2048]{1,0:T(8,128)(2,1)S(1)} %get-tuple-element.131.up_ref, bf16[512,2048]{1,0:T(8,128)(2,1)S(1)} %get-tuple-element.132.down_ref), custom_call_target="tpu_custom_call" | custom-call | flops 110000000 | bytes 1048576 | tf_op jit(solution)/shard_map/pallas_call | solution.py:483
  65.2 1.9 %shard_map.284 = (bf16[512,512]{1,0:T(8,128)(2,1)}, f32[640,512]{1,0:T(8,128)S(1)}, bf16[512,512]{1,0:T(8,128)(2,1)S(1)}, bf16[640,512]{1,0:T(8,128)(2,1)S(1)}, f32[8,512]{1,0:T(8,128)S(1)}) custom-call(f32[640,128]{1,0:T(8,128)S(1)} %broadcast_in_dim.59.keep_ref, bf16[640,512]{1,0:T(8,128)(2,1)S(1)} %pad_maximum_fusion.cot_ref, ...), custom_call_target="tpu_custom_call" | custom-call | flops 110000000 | bytes 1048576 | tf_op jit(solution)/shard_map/pallas_call | solution.py:483
  67.1 2.5 %shard_map.286.gproj_b = bf16[256,1536]{1,0:T(8,128)(2,1)S(1)} custom-call(bf16[640,512]{1,0:T(8,128)(2,1)S(1)} %get-tuple-element.143.gmix_ref, bf16[640,1536]{1,0:T(8,128)(2,1)S(1)} %get-tuple-element.144.proj_ref, f32[20,2,32,256]{3,2,1,0:T(8,128)S(1)} %get-tuple-element.145.prob_ref), custom_call_target="tpu_custom_call" | custom-call | flops 110000000 | bytes 1048576 | tf_op jit(solution)/shard_map/pallas_call | solution.py:483
  69.6 2.5 %shard_map.285.gproj_a = bf16[256,1536]{1,0:T(8,128)(2,1)S(1)} custom-call(bf16[640,512]{1,0:T(8,128)(2,1)S(1)} %get-tuple-element.143.gmix_ref, bf16[640,1536]{1,0:T(8,128)(2,1)S(1)} %get-tuple-element.144.proj_ref, f32[20,2,32,256]{3,2,1,0:T(8,128)S(1)} %get-tuple-element.145.prob_ref), custom_call_target="tpu_custom_call" | custom-call | flops 110000000 | bytes 1048576 | tf_op jit(solution)/shard_map/pallas_call | solution.py:483
  72.1 1.5 %collective-permute-done.19 = bf16[8,64,512]{2,1,0:T(8,128)(2,1)S(1)} collective-permute-done((bf16[8,64,512]{2,1,0:T(8,128)(2,1)S(1)}, bf16[8,64,512]{2,1,0:T(8,128)(2,1)S(1)}, u32[]{:S(2)}, u32[]{:S(2)}) %collective-permute-start.19) | collective-permute-done | bytes 524320 | tf_op jit(solution)/shard_map/ppermute | solution.py:497
  73.8 1.5 %collective-permute-start.20 = (bf16[4,64,512]{2,1,0:T(8,128)(2,1)S(1)}, bf16[4,64,512]{2,1,0:T(8,128)(2,1)S(1)}, u32[]{:S(2)}, u32[]{:S(2)}) collective-permute-start(bf16[4,64,512]{2,1,0:T(8,128)(2,1)S(1)} %slice.150), channel_id=1, source_target_pairs={{0,2},{1,5},{2,0},{3,7},{4,6},{5,1},{6,4},{7,3},{8,10},{9,13},{10,... | collective-permute-start | bytes 786440 | tf_op jit(solution)/shard_map/ppermute | solution.py:497
  75.3 2.5 %shard_map.287 = (bf16[1040,512]{1,0:T(8,128)(2,1)S(1)}, bf16[208,512]{1,0:T(8,128)(2,1)S(1)}, bf16[208,512]{1,0:T(8,128)(2,1)S(1)}, bf16[208,512]{1,0:T(8,128)(...) custom-call(s32[32]{0:T(128)S(1)} %get-tuple-element.150.own_ref, ...), custom_call_target="tpu_custom_call" | custom-call | flops 110000000 | bytes 1048576 | tf_op jit(solution)/shard_map/pallas_call | solution.py:483
  78.5 1.8 %collective-permute-done.20 = bf16[4,64,512]{2,1,0:T(8,128)(2,1)S(1)} collective-permute-done((bf16[4,64,512]{2,1,0:T(8,128)(2,1)S(1)}, bf16[4,64,512]{2,1,0:T(8,128)(2,1)S(1)}, u32[]{:S(2)}, u32[]{:S(2)}) %collective-permute-start.20) | collective-permute-done | bytes 262176 | tf_op jit(solution)/shard_map/ppermute | solution.py:497
  83.9 2.0 %collective-permute-start.28 = (bf16[272,512]{1,0:T(8,128)(2,1)S(1)}, bf16[272,512]{1,0:T(8,128)(2,1)S(1)}, u32[]{:S(2)}, u32[]{:S(2)}) collective-permute-start(bf16[272,512]{1,0:T(8,128)(2,1)S(1)} %get-tuple-element.178), channel_id=1, source_target_pairs={{0,6},{1,7},{2,4},{3,5},{4,2},{5,3},{6,0},{7,1},{8,14},{9,15},{10,... | collective-permute-start | bytes 835592 | tf_op jit(solution)/shard_map/ppermute | solution.py:497
  87.4 2.2 %shard_map.288 = f32[512,512]{1,0:T(8,128)} custom-call(bf16[256,1536]{1,0:T(8,128)(2,1)S(1)} %shard_map.285.gproj_a, bf16[256,1536]{1,0:T(8,128)(2,1)S(1)} %shard_map.286.gproj_b, bf16[640,512]{1,0:T(8,128)(2,1)S(1)} %pad_maximum_fusion.1.x_ref, f32[640,512]{1,0:T(8,128)S(1)} %get-tuple-element.169.gres_ref, ...), custom_call_target="tpu_custom_call" | custom-call | flops 110000000 | bytes 1048576 | tf_op jit(solution)/shard_map/pallas_call | solution.py:483
  89.6 5.7 %collective-permute-done.27 = bf16[6,64,512]{2,1,0:T(8,128)(2,1)S(1)} collective-permute-done((bf16[6,64,512]{2,1,0:T(8,128)(2,1)S(1)}, bf16[6,64,512]{2,1,0:T(8,128)(2,1)S(1)}, u32[]{:S(2)}, u32[]{:S(2)}) %collective-permute-start.27) | collective-permute-done | bytes 393248 | tf_op jit(solution)/shard_map/ppermute | solution.py:497
  95.6 1.5 %collective-permute-start.35 = (bf16[1,64,512]{2,1,0:T(8,128)(2,1)S(1)}, bf16[1,64,512]{2,1,0:T(8,128)(2,1)S(1)}, u32[]{:S(2)}, u32[]{:S(2)}) collective-permute-start(bf16[1,64,512]{2,1,0:T(8,128)(2,1)S(1)} %get-tuple-element.197), channel_id=1, source_target_pairs={{0,2},{1,5},{2,0},{3,7},{4,6},{5,1},{6,4},{7,3},{8,10},{9,13},{10,... | collective-permute-start | bytes 196616 | tf_op jit(solution)/shard_map/ppermute | solution.py:497
  98.7 1.4 %collective-permute-start.36 = (bf16[1,64,512]{2,1,0:T(8,128)(2,1)S(1)}, bf16[1,64,512]{2,1,0:T(8,128)(2,1)S(1)}, u32[]{:S(2)}, u32[]{:S(2)}) collective-permute-start(bf16[1,64,512]{2,1,0:T(8,128)(2,1)S(1)} %get-tuple-element.199), channel_id=1, source_target_pairs={{0,4},{1,3},{2,6},{3,1},{4,0},{5,7},{6,2},{7,5},{8,12},{9,11},{10,... | collective-permute-start | bytes 196616 | tf_op jit(solution)/shard_map/ppermute | solution.py:497
  100.3 1.9 %collective-permute-start.32 = (bf16[80,512]{1,0:T(8,128)(2,1)S(1)}, bf16[80,512]{1,0:T(8,128)(2,1)S(1)}, u32[]{:S(2)}, u32[]{:S(2)}) collective-permute-start(bf16[80,512]{1,0:T(8,128)(2,1)S(1)} %get-tuple-element.186), channel_id=1, source_target_pairs={{0,16},{1,17},{2,18},{3,19},{4,20},{5,21},{6,22},{7,23},{8,24},{9,... | collective-permute-start | bytes 245768 | tf_op jit(solution)/shard_map/ppermute | solution.py:497
  103.0 1.8 %collective-permute-start.34 = (bf16[80,512]{1,0:T(8,128)(2,1)S(1)}, bf16[80,512]{1,0:T(8,128)(2,1)S(1)}, u32[]{:S(2)}, u32[]{:S(2)}) collective-permute-start(bf16[80,512]{1,0:T(8,128)(2,1)S(1)} %get-tuple-element.188), channel_id=1, source_target_pairs={{0,24},{1,25},{2,26},{3,27},{4,28},{5,29},{6,30},{7,31},{8,16},{9,... | collective-permute-start | bytes 245768 | tf_op jit(solution)/shard_map/ppermute | solution.py:497
  106.2 2.3 %collective-permute-done.32.refs_1_ = bf16[80,512]{1,0:T(8,128)(2,1)S(1)} collective-permute-done((bf16[80,512]{1,0:T(8,128)(2,1)S(1)}, bf16[80,512]{1,0:T(8,128)(2,1)S(1)}, u32[]{:S(2)}, u32[]{:S(2)}) %collective-permute-start.32) | collective-permute-done | bytes 81952 | tf_op jit(solution)/shard_map/ppermute | solution.py:497
  (129 shorter events, 19.8 us)
Async XLA Ops:
  2.4 12.2 %collective-permute-start.2 = (bf16[1,144,512]{2,1,0:T(8,128)(2,1)}, bf16[1,144,512]{2,1,0:T(8,128)(2,1)S(1)}, u32[]{:S(2)}, u32[]{:S(2)}) collective-permute-start(bf16[1,144,512]{2,1,0:T(8,128)(2,1)} %bitcast.31), channel_id=1, source_target_pairs={{0,24},{1,25},{2,26},{3,27},{4,28},{5,29},{6,30},{7,31},{8,16},{9,... | collective-permute-start | bytes 442376 | tf_op jit(solution)/shard_map/ppermute | solution.py:497
  7.5 8.4 %collective-permute-start.1 = (bf16[1,144,512]{2,1,0:T(8,128)(2,1)}, bf16[1,144,512]{2,1,0:T(8,128)(2,1)S(1)}, u32[]{:S(2)}, u32[]{:S(2)}) collective-permute-start(bf16[1,144,512]{2,1,0:T(8,128)(2,1)} %bitcast.32), channel_id=1, source_target_pairs={{0,8},{1,9},{2,10},{3,11},{4,12},{5,13},{6,14},{7,15},{8,0},{9,1},... | collective-permute-start | bytes 442376 | tf_op jit(solution)/shard_map/ppermute | solution.py:497
  7.5 12.7 %collective-permute-start = (bf16[1,144,512]{2,1,0:T(8,128)(2,1)}, bf16[1,144,512]{2,1,0:T(8,128)(2,1)S(1)}, u32[]{:S(2)}, u32[]{:S(2)}) collective-permute-start(bf16[1,144,512]{2,1,0:T(8,128)(2,1)} %bitcast.33), channel_id=1, source_target_pairs={{0,16},{1,17},{2,18},{3,19},{4,20},{5,21},{6,22},{7,23},{8,24},{9,... | collective-permute-start | bytes 442376 | tf_op jit(solution)/shard_map/ppermute | solution.py:497
  8.1 4.5 %collective-permute-start.3 = (bf16[1,64,512]{2,1,0:T(8,128)(2,1)}, bf16[1,64,512]{2,1,0:T(8,128)(2,1)S(1)}, u32[]{:S(2)}, u32[]{:S(2)}) collective-permute-start(bf16[1,64,512]{2,1,0:T(8,128)(2,1)} %bitcast.39), channel_id=1, source_target_pairs={{0,2},{1,5},{2,0},{3,7},{4,6},{5,1},{6,4},{7,3},{8,10},{9,13},{10,... | collective-permute-start | bytes 196616 | tf_op jit(solution)/shard_map/ppermute | solution.py:497
  10.8 11.9 %collective-permute-start.8 = (bf16[2,4,16,512]{3,2,1,0:T(8,128)(2,1)S(1)}, bf16[2,4,16,512]{3,2,1,0:T(8,128)(2,1)S(1)}, u32[]{:S(2)}, u32[]{:S(2)}) collective-permute-start(bf16[2,4,16,512]{3,2,1,0:T(8,128)(2,1)S(1)} %get-tuple-element.195), channel_id=1, source_target_pairs={{1,0},{2,1},{3,2},{5,4},{6,5},{7,6},{9,8},{10,9},{11,10},{13,12},{... | collective-permute-start | bytes 393224 | tf_op jit(solution)/shard_map/ppermute | solution.py:550
  12.6 7.6 %collective-permute-start.4 = (bf16[2,64,512]{2,1,0:T(8,128)(2,1)S(1)}, bf16[2,64,512]{2,1,0:T(8,128)(2,1)S(1)}, u32[]{:S(2)}, u32[]{:S(2)}) collective-permute-start(bf16[2,64,512]{2,1,0:T(8,128)(2,1)S(1)} %pad_maximum_fusion.6), channel_id=1, source_target_pairs={{0,4},{1,3},{2,6},{3,1},{4,0},{5,7},{6,2},{7,5},{8,12},{9,11},{10,... | collective-permute-start | bytes 393224 | tf_op jit(solution)/shard_map/ppermute | solution.py:497
  14.6 8.0 %collective-permute-start.7 = (bf16[2,4,16,512]{3,2,1,0:T(8,128)(2,1)S(1)}, bf16[2,4,16,512]{3,2,1,0:T(8,128)(2,1)S(1)}, u32[]{:S(2)}, u32[]{:S(2)}) collective-permute-start(bf16[2,4,16,512]{3,2,1,0:T(8,128)(2,1)S(1)} %get-tuple-element.196), channel_id=1, source_target_pairs={{0,1},{1,2},{2,3},{4,5},{5,6},{6,7},{8,9},{9,10},{10,11},{12,13},{... | collective-permute-start | bytes 393224 | tf_op jit(solution)/shard_map/ppermute | solution.py:549
  20.4 11.3 %collective-permute-start.5 = (bf16[4,144,512]{2,1,0:T(8,128)(2,1)S(1)}, bf16[4,144,512]{2,1,0:T(8,128)(2,1)S(1)}, u32[]{:S(2)}, u32[]{:S(2)}) collective-permute-start(bf16[4,144,512]{2,1,0:T(8,128)(2,1)S(1)} %pad_maximum_fusion.2), channel_id=1, source_target_pairs={{0,4},{1,3},{2,6},{3,1},{4,0},{5,7},{6,2},{7,5},{8,12},{9,11},{10,... | collective-permute-start | bytes 1769480 | tf_op jit(solution)/shard_map/ppermute | solution.py:497
  22.0 9.7 %collective-permute-start.6 = (bf16[4,64,512]{2,1,0:T(8,128)(2,1)S(1)}, bf16[4,64,512]{2,1,0:T(8,128)(2,1)S(1)}, u32[]{:S(2)}, u32[]{:S(2)}) collective-permute-start(bf16[4,64,512]{2,1,0:T(8,128)(2,1)S(1)} %constant_dynamic-update-slice_fusion), channel_id=1, source_target_pairs={{0,16},{1,9},{2,18},{3,11},{4,20},{5,13},{6,22},{7,15},{8,24},{9,1... | collective-permute-start | bytes 786440 | tf_op jit(solution)/shard_map/ppermute | solution.py:497
  31.8 11.3 %collective-permute-start.10 = (bf16[8,144,512]{2,1,0:T(8,128)(2,1)S(1)}, bf16[8,144,512]{2,1,0:T(8,128)(2,1)S(1)}, u32[]{:S(2)}, u32[]{:S(2)}) collective-permute-start(bf16[8,144,512]{2,1,0:T(8,128)(2,1)S(1)} %constant_dynamic-update-slice_fusion.4.refs_0_), channel_id=1, source_target_pairs={{0,1},{1,0},{2,3},{3,2},{4,5},{5,4},{6,7},{7,6},{8,9},{9,8},{10,11... | collective-permute-start | bytes 3538952 | tf_op jit(solution)/shard_map/ppermute | solution.py:497
  31.9 9.2 %collective-permute-start.9 = (bf16[8,64,512]{2,1,0:T(8,128)(2,1)S(1)}, bf16[8,64,512]{2,1,0:T(8,128)(2,1)S(1)}, u32[]{:S(2)}, u32[]{:S(2)}) collective-permute-start(bf16[8,64,512]{2,1,0:T(8,128)(2,1)S(1)} %slice.106), channel_id=1, source_target_pairs={{0,2},{1,5},{2,0},{3,7},{4,6},{5,1},{6,4},{7,3},{8,10},{9,13},{10,... | collective-permute-start | bytes 1572872 | tf_op jit(solution)/shard_map/ppermute | solution.py:497
  33.5 15.5 %collective-permute-start.12 = (bf16[8,80,512]{2,1,0:T(8,128)(2,1)S(1)}, bf16[8,80,512]{2,1,0:T(8,128)(2,1)S(1)}, u32[]{:S(2)}, u32[]{:S(2)}) collective-permute-start(bf16[8,80,512]{2,1,0:T(8,128)(2,1)S(1)} %slice.107), channel_id=1, source_target_pairs={{0,2},{1,5},{2,0},{3,7},{4,6},{5,1},{6,4},{7,3},{8,10},{9,13},{10,... | collective-permute-start | bytes 1966088 | tf_op jit(solution)/shard_map/ppermute | solution.py:497
  34.2 14.9 %collective-permute-start.13 = (bf16[8,64,512]{2,1,0:T(8,128)(2,1)S(1)}, bf16[8,64,512]{2,1,0:T(8,128)(2,1)S(1)}, u32[]{:S(2)}, u32[]{:S(2)}) collective-permute-start(bf16[8,64,512]{2,1,0:T(8,128)(2,1)S(1)} %constant_dynamic-update-slice_fusion.9.refs_0_), channel_id=1, source_target_pairs={{0,8},{1,17},{2,10},{3,19},{4,12},{5,21},{6,14},{7,23},{8,0},{9,25... | collective-permute-start | bytes 1572872 | tf_op jit(solution)/shard_map/ppermute | solution.py:497
  49.1 7.6 %collective-permute-start.15 = (bf16[8,64,512]{2,1,0:T(8,128)(2,1)S(1)}, bf16[8,64,512]{2,1,0:T(8,128)(2,1)S(1)}, u32[]{:S(2)}, u32[]{:S(2)}) collective-permute-start(bf16[8,64,512]{2,1,0:T(8,128)(2,1)S(1)} %constant_dynamic-update-slice_fusion.9.refs_0_), channel_id=1, source_target_pairs={{0,1},{1,0},{2,3},{3,2},{4,5},{5,4},{6,7},{7,6},{8,9},{9,8},{10,11... | collective-permute-start | bytes 1572872 | tf_op jit(solution)/shard_map/ppermute | solution.py:497
  49.6 7.0 %collective-permute-start.16 = (bf16[8,64,512]{2,1,0:T(8,128)(2,1)S(1)}, bf16[8,64,512]{2,1,0:T(8,128)(2,1)S(1)}, u32[]{:S(2)}, u32[]{:S(2)}) collective-permute-start(bf16[8,64,512]{2,1,0:T(8,128)(2,1)S(1)} %collective-permute-done.13.refs_1_), channel_id=1, source_target_pairs={{0,1},{1,0},{2,3},{3,2},{4,5},{5,4},{6,7},{7,6},{8,9},{9,8},{10,11... | collective-permute-start | bytes 1572872 | tf_op jit(solution)/shard_map/ppermute | solution.py:497
  56.4 4.5 %collective-permute-start.17 = (bf16[16,64,512]{2,1,0:T(8,128)(2,1)S(1)}, bf16[16,64,512]{2,1,0:T(8,128)(2,1)S(1)}, u32[]{:S(2)}, u32[]{:S(2)}) collective-permute-start(bf16[16,64,512]{2,1,0:T(8,128)(2,1)S(1)} %get-tuple-element.128), channel_id=1, source_target_pairs={{0,1},{1,0},{2,3},{3,2},{4,5},{5,4},{6,7},{7,6},{8,9},{9,8},{10,11... | collective-permute-start | bytes 3145736 | tf_op jit(solution)/shard_map/ppermute | solution.py:497
  60.5 3.5 %collective-permute-start.18 = (bf16[16,64,512]{2,1,0:T(8,128)(2,1)S(1)}, bf16[16,64,512]{2,1,0:T(8,128)(2,1)S(1)}, u32[]{:S(2)}, u32[]{:S(2)}) collective-permute-start(bf16[16,64,512]{2,1,0:T(8,128)(2,1)S(1)} %get-tuple-element.136), channel_id=1, source_target_pairs={{0,1},{1,0},{2,3},{3,2},{4,5},{5,4},{6,7},{7,6},{8,9},{9,8},{10,11... | collective-permute-start | bytes 3145736 | tf_op jit(solution)/shard_map/ppermute | solution.py:497
  64.4 9.2 %collective-permute-start.19 = (bf16[8,64,512]{2,1,0:T(8,128)(2,1)S(1)}, bf16[8,64,512]{2,1,0:T(8,128)(2,1)S(1)}, u32[]{:S(2)}, u32[]{:S(2)}) collective-permute-start(bf16[8,64,512]{2,1,0:T(8,128)(2,1)S(1)} %slice.147), channel_id=1, source_target_pairs={{0,4},{1,3},{2,6},{3,1},{4,0},{5,7},{6,2},{7,5},{8,12},{9,11},{10,... | collective-permute-start | bytes 1572872 | tf_op jit(solution)/shard_map/ppermute | solution.py:497
  65.2 15.0 %collective-permute-start.21 = (bf16[8,64,512]{2,1,0:T(8,128)(2,1)S(1)}, bf16[8,64,512]{2,1,0:T(8,128)(2,1)S(1)}, u32[]{:S(2)}, u32[]{:S(2)}) collective-permute-start(bf16[8,64,512]{2,1,0:T(8,128)(2,1)S(1)} %slice.148), channel_id=1, source_target_pairs={{0,8},{1,17},{2,10},{3,19},{4,12},{5,21},{6,14},{7,23},{8,0},{9,25... | collective-permute-start | bytes 1572872 | tf_op jit(solution)/shard_map/ppermute | solution.py:497
  73.8 6.4 %collective-permute-start.20 = (bf16[4,64,512]{2,1,0:T(8,128)(2,1)S(1)}, bf16[4,64,512]{2,1,0:T(8,128)(2,1)S(1)}, u32[]{:S(2)}, u32[]{:S(2)}) collective-permute-start(bf16[4,64,512]{2,1,0:T(8,128)(2,1)S(1)} %slice.150), channel_id=1, source_target_pairs={{0,2},{1,5},{2,0},{3,7},{4,6},{5,1},{6,4},{7,3},{8,10},{9,13},{10,... | collective-permute-start | bytes 786440 | tf_op jit(solution)/shard_map/ppermute | solution.py:497
  77.8 3.0 %collective-permute-start.22 = (bf16[208,512]{1,0:T(8,128)(2,1)S(1)}, bf16[208,512]{1,0:T(8,128)(2,1)S(1)}, u32[]{:S(2)}, u32[]{:S(2)}) collective-permute-start(bf16[208,512]{1,0:T(8,128)(2,1)S(1)} %get-tuple-element.161), channel_id=1, source_target_pairs={{0,1},{1,0},{2,3},{3,2},{4,5},{5,4},{6,7},{7,6},{8,9},{9,8},{10,11... | collective-permute-start | bytes 638984 | tf_op jit(solution)/shard_map/ppermute | solution.py:497
  82.4 13.0 %collective-permute-start.27 = (bf16[6,64,512]{2,1,0:T(8,128)(2,1)S(1)}, bf16[6,64,512]{2,1,0:T(8,128)(2,1)S(1)}, u32[]{:S(2)}, u32[]{:S(2)}) collective-permute-start(bf16[6,64,512]{2,1,0:T(8,128)(2,1)S(1)} %pad_maximum_fusion.3), channel_id=1, source_target_pairs={{0,16},{1,9},{2,18},{3,11},{4,20},{5,13},{6,22},{7,15},{8,24},{9,1... | collective-permute-start | bytes 1179656 | tf_op jit(solution)/shard_map/ppermute | solution.py:497
  83.9 13.3 %collective-permute-start.28 = (bf16[272,512]{1,0:T(8,128)(2,1)S(1)}, bf16[272,512]{1,0:T(8,128)(2,1)S(1)}, u32[]{:S(2)}, u32[]{:S(2)}) collective-permute-start(bf16[272,512]{1,0:T(8,128)(2,1)S(1)} %get-tuple-element.178), channel_id=1, source_target_pairs={{0,6},{1,7},{2,4},{3,5},{4,2},{5,3},{6,0},{7,1},{8,14},{9,15},{10,... | collective-permute-start | bytes 835592 | tf_op jit(solution)/shard_map/ppermute | solution.py:497
  85.9 12.8 %collective-permute-start.29 = (bf16[272,512]{1,0:T(8,128)(2,1)S(1)}, bf16[272,512]{1,0:T(8,128)(2,1)S(1)}, u32[]{:S(2)}, u32[]{:S(2)}) collective-permute-start(bf16[272,512]{1,0:T(8,128)(2,1)S(1)} %get-tuple-element.179), channel_id=1, source_target_pairs={{0,2},{1,3},{2,0},{3,1},{4,6},{5,7},{6,4},{7,5},{8,10},{9,11},{10,... | collective-permute-start | bytes 835592 | tf_op jit(solution)/shard_map/ppermute | solution.py:497
  86.9 13.3 %collective-permute-start.30 = (bf16[272,512]{1,0:T(8,128)(2,1)S(1)}, bf16[272,512]{1,0:T(8,128)(2,1)S(1)}, u32[]{:S(2)}, u32[]{:S(2)}) collective-permute-start(bf16[272,512]{1,0:T(8,128)(2,1)S(1)} %get-tuple-element.180), channel_id=1, source_target_pairs={{0,4},{1,5},{2,6},{3,7},{4,0},{5,1},{6,2},{7,3},{8,12},{9,13},{10,... | collective-permute-start | bytes 835592 | tf_op jit(solution)/shard_map/ppermute | solution.py:497
  95.5 4.7 %collective-permute-start.31 = (bf16[1,64,512]{2,1,0:T(8,128)(2,1)S(1)}, bf16[1,64,512]{2,1,0:T(8,128)(2,1)S(1)}, u32[]{:S(2)}, u32[]{:S(2)}) collective-permute-start(bf16[1,64,512]{2,1,0:T(8,128)(2,1)S(1)} %slice.152), channel_id=1, source_target_pairs={{0,8},{1,17},{2,10},{3,19},{4,12},{5,21},{6,14},{7,23},{8,0},{9,25... | collective-permute-start | bytes 196616 | tf_op jit(solution)/shard_map/ppermute | solution.py:497
  95.6 7.4 %collective-permute-start.35 = (bf16[1,64,512]{2,1,0:T(8,128)(2,1)S(1)}, bf16[1,64,512]{2,1,0:T(8,128)(2,1)S(1)}, u32[]{:S(2)}, u32[]{:S(2)}) collective-permute-start(bf16[1,64,512]{2,1,0:T(8,128)(2,1)S(1)} %get-tuple-element.197), channel_id=1, source_target_pairs={{0,2},{1,5},{2,0},{3,7},{4,6},{5,1},{6,4},{7,3},{8,10},{9,13},{10,... | collective-permute-start | bytes 196616 | tf_op jit(solution)/shard_map/ppermute | solution.py:497
  97.1 7.7 %collective-permute-start.37 = (bf16[1,64,512]{2,1,0:T(8,128)(2,1)S(1)}, bf16[1,64,512]{2,1,0:T(8,128)(2,1)S(1)}, u32[]{:S(2)}, u32[]{:S(2)}) collective-permute-start(bf16[1,64,512]{2,1,0:T(8,128)(2,1)S(1)} %get-tuple-element.198), channel_id=1, source_target_pairs={{0,6},{1,7},{2,4},{3,5},{4,2},{5,3},{6,0},{7,1},{8,14},{9,15},{10,... | collective-permute-start | bytes 196616 | tf_op jit(solution)/shard_map/ppermute | solution.py:497
  98.7 6.1 %collective-permute-start.36 = (bf16[1,64,512]{2,1,0:T(8,128)(2,1)S(1)}, bf16[1,64,512]{2,1,0:T(8,128)(2,1)S(1)}, u32[]{:S(2)}, u32[]{:S(2)}) collective-permute-start(bf16[1,64,512]{2,1,0:T(8,128)(2,1)S(1)} %get-tuple-element.199), channel_id=1, source_target_pairs={{0,4},{1,3},{2,6},{3,1},{4,0},{5,7},{6,2},{7,5},{8,12},{9,11},{10,... | collective-permute-start | bytes 196616 | tf_op jit(solution)/shard_map/ppermute | solution.py:497
  100.3 8.1 %collective-permute-start.32 = (bf16[80,512]{1,0:T(8,128)(2,1)S(1)}, bf16[80,512]{1,0:T(8,128)(2,1)S(1)}, u32[]{:S(2)}, u32[]{:S(2)}) collective-permute-start(bf16[80,512]{1,0:T(8,128)(2,1)S(1)} %get-tuple-element.186), channel_id=1, source_target_pairs={{0,16},{1,17},{2,18},{3,19},{4,20},{5,21},{6,22},{7,23},{8,24},{9,... | collective-permute-start | bytes 245768 | tf_op jit(solution)/shard_map/ppermute | solution.py:497
  102.2 6.2 %collective-permute-start.33 = (bf16[80,512]{1,0:T(8,128)(2,1)S(1)}, bf16[80,512]{1,0:T(8,128)(2,1)S(1)}, u32[]{:S(2)}, u32[]{:S(2)}) collective-permute-start(bf16[80,512]{1,0:T(8,128)(2,1)S(1)} %get-tuple-element.187), channel_id=1, source_target_pairs={{0,8},{1,9},{2,10},{3,11},{4,12},{5,13},{6,14},{7,15},{8,0},{9,1},... | collective-permute-start | bytes 245768 | tf_op jit(solution)/shard_map/ppermute | solution.py:497
  103.0 6.4 %collective-permute-start.34 = (bf16[80,512]{1,0:T(8,128)(2,1)S(1)}, bf16[80,512]{1,0:T(8,128)(2,1)S(1)}, u32[]{:S(2)}, u32[]{:S(2)}) collective-permute-start(bf16[80,512]{1,0:T(8,128)(2,1)S(1)} %get-tuple-element.188), channel_id=1, source_target_pairs={{0,24},{1,25},{2,26},{3,27},{4,28},{5,29},{6,30},{7,31},{8,16},{9,... | collective-permute-start | bytes 245768 | tf_op jit(solution)/shard_map/ppermute | solution.py:497
  (17 other events, 138.5 us)

commit v6 on v5

--- a/solution.py
+++ b/solution.py
@@ -708,7 +708,7 @@
         up_arrived = swap(up_sum[1:].astype(bf16), ALONG_Z[1], ALONG_Z[0])
         dn_rest = dn_sum.astype(bf16)
         dn_arrived = [
-            swap(dn_rest[1:2], ALONG_Y, ALONG_X), swap(dn_rest[2:3], ALONG_X, ALONG_Y), swap(dn_rest[3:], ALONG_XY[2]),
+            swap(dn_rest[3:], ALONG_XY[2]), swap(dn_rest[1:2], ALONG_Y, ALONG_X), swap(dn_rest[2:3], ALONG_X, ALONG_Y),
         ]
         at_arrived, up_arrived = lax.optimization_barrier((at_arrived, up_arrived))
         at_sum, *at_rest = call(

time: 110 us -> 111 us (level)
  transfers between devices with their start and end apart: 38 -> 38, of which waited for: 16 -> 15; matrix products, arithmetic and copies ran while one was open for 4% -> 4% of each run, Pallas kernels for 26% -> 26%
where the time goes in v6:
time: 111 us
  waiting for transfers between devices  38.8 us (35%)
  starting transfers between devices  34.8 us (31%)
  Pallas kernels  31.1 us (28%)
  other arithmetic  3.89 us (4%)
  between operations  1.26 us (1%)
    ppermute x36, waiting for transfers between devices, swap(): lax.ppermute(array, BOTH, [(device, device ^ masks[device % 2]) for devic...  38.8 us
    ppermute x36, starting transfers between devices, swap(): lax.ppermute(array, BOTH, [(device, device ^ masks[device % 2]) for devic...  32.2 us
    pallas_call x12, Pallas kernels, call(): pl.pallas_call(kernel, out_shape=[jax.ShapeDtypeStruct(s, t) for s, t in...  29.5 us
  transfers between devices with their start and end apart: 38, of which 15 were waited for; matrix products, arithmetic and copies ran while one was open for 4% of the time, Pallas kernels for 26%

profile of v6, /device:TPU:0, one launch (start us, length us, event | category | flops | bytes accessed | tf_op | source)
XLA Modules:
  0.0 110.9 jit_solution(8249694725970989912)
XLA Ops:
  0.7 1.6 %shard_map.279 = bf16[144,512]{1,0:T(8,128)(2,1)} custom-call(bf16[48,512]{1,0:T(8,128)(2,1)} %bitcast.41, bf16[12,16]{1,0:T(8,128)(2,1)} %vec_ref.1, bf16[16,512]{1,0:T(8,128)(2,1)} %bitcast.42, bf16[64,512]{1,0:T(8,128)(2,1)} %up_ref.1), custom_call_target="tpu_custom_call" | custom-call | tf_op jit(solution)/shard_map/pallas_call | solution.py:572
  2.4 5.1 %collective-permute-start.2 = (bf16[1,144,512]{2,1,0:T(8,128)(2,1)}, bf16[1,144,512]{2,1,0:T(8,128)(2,1)S(1)}, u32[]{:S(2)}, u32[]{:S(2)}) collective-permute-start(bf16[1,144,512]{2,1,0:T(8,128)(2,1)} %bitcast.31), channel_id=1, source_target_pairs={{0,24},{1,25},{2,26},{3,27},{4,28},{5,29},{6,30},{7,31},{8,16},{9,... | collective-permute-start | bytes 442376 | tf_op jit(solution)/shard_map/ppermute | solution.py:497
  8.1 1.7 %collective-permute-start.3 = (bf16[1,64,512]{2,1,0:T(8,128)(2,1)}, bf16[1,64,512]{2,1,0:T(8,128)(2,1)S(1)}, u32[]{:S(2)}, u32[]{:S(2)}) collective-permute-start(bf16[1,64,512]{2,1,0:T(8,128)(2,1)} %bitcast.39), channel_id=1, source_target_pairs={{0,2},{1,5},{2,0},{3,7},{4,6},{5,1},{6,4},{7,3},{8,10},{9,13},{10,... | collective-permute-start | bytes 196616 | tf_op jit(solution)/shard_map/ppermute | solution.py:497
  10.8 1.3 %collective-permute-start.8 = (bf16[2,4,16,512]{3,2,1,0:T(8,128)(2,1)S(1)}, bf16[2,4,16,512]{3,2,1,0:T(8,128)(2,1)S(1)}, u32[]{:S(2)}, u32[]{:S(2)}) collective-permute-start(bf16[2,4,16,512]{3,2,1,0:T(8,128)(2,1)S(1)} %get-tuple-element.195), channel_id=1, source_target_pairs={{1,0},{2,1},{3,2},{5,4},{6,5},{7,6},{9,8},{10,9},{11,10},{13,12},{... | collective-permute-start | bytes 393224 | tf_op jit(solution)/shard_map/ppermute | solution.py:550
  12.6 1.7 %collective-permute-start.4 = (bf16[2,64,512]{2,1,0:T(8,128)(2,1)S(1)}, bf16[2,64,512]{2,1,0:T(8,128)(2,1)S(1)}, u32[]{:S(2)}, u32[]{:S(2)}) collective-permute-start(bf16[2,64,512]{2,1,0:T(8,128)(2,1)S(1)} %pad_maximum_fusion.6), channel_id=1, source_target_pairs={{0,4},{1,3},{2,6},{3,1},{4,0},{5,7},{6,2},{7,5},{8,12},{9,11},{10,... | collective-permute-start | bytes 393224 | tf_op jit(solution)/shard_map/ppermute | solution.py:497
  14.6 1.3 %collective-permute-start.7 = (bf16[2,4,16,512]{3,2,1,0:T(8,128)(2,1)S(1)}, bf16[2,4,16,512]{3,2,1,0:T(8,128)(2,1)S(1)}, u32[]{:S(2)}, u32[]{:S(2)}) collective-permute-start(bf16[2,4,16,512]{3,2,1,0:T(8,128)(2,1)S(1)} %get-tuple-element.196), channel_id=1, source_target_pairs={{0,1},{1,2},{2,3},{4,5},{5,6},{6,7},{8,9},{9,10},{10,11},{12,13},{... | collective-permute-start | bytes 393224 | tf_op jit(solution)/shard_map/ppermute | solution.py:549
  15.9 4.3 %collective-permute-done = bf16[1,144,512]{2,1,0:T(8,128)(2,1)S(1)} collective-permute-done((bf16[1,144,512]{2,1,0:T(8,128)(2,1)}, bf16[1,144,512]{2,1,0:T(8,128)(2,1)S(1)}, u32[]{:S(2)}, u32[]{:S(2)}) %collective-permute-start) | collective-permute-done | bytes 147488 | tf_op jit(solution)/shard_map/ppermute | solution.py:497
  20.4 1.6 %collective-permute-start.5 = (bf16[4,144,512]{2,1,0:T(8,128)(2,1)S(1)}, bf16[4,144,512]{2,1,0:T(8,128)(2,1)S(1)}, u32[]{:S(2)}, u32[]{:S(2)}) collective-permute-start(bf16[4,144,512]{2,1,0:T(8,128)(2,1)S(1)} %pad_maximum_fusion.2), channel_id=1, source_target_pairs={{0,4},{1,3},{2,6},{3,1},{4,0},{5,7},{6,2},{7,5},{8,12},{9,11},{10,... | collective-permute-start | bytes 1769480 | tf_op jit(solution)/shard_map/ppermute | solution.py:497
  22.7 9.1 %collective-permute-done.6 = bf16[4,64,512]{2,1,0:T(8,128)(2,1)S(1)} collective-permute-done((bf16[4,64,512]{2,1,0:T(8,128)(2,1)S(1)}, bf16[4,64,512]{2,1,0:T(8,128)(2,1)S(1)}, u32[]{:S(2)}, u32[]{:S(2)}) %collective-permute-start.6) | collective-permute-done | bytes 262176 | tf_op jit(solution)/shard_map/ppermute | solution.py:497
  31.9 1.6 %collective-permute-start.9 = (bf16[8,64,512]{2,1,0:T(8,128)(2,1)S(1)}, bf16[8,64,512]{2,1,0:T(8,128)(2,1)S(1)}, u32[]{:S(2)}, u32[]{:S(2)}) collective-permute-start(bf16[8,64,512]{2,1,0:T(8,128)(2,1)S(1)} %slice.106), channel_id=1, source_target_pairs={{0,2},{1,5},{2,0},{3,7},{4,6},{5,1},{6,4},{7,3},{8,10},{9,13},{10,... | collective-permute-start | bytes 1572872 | tf_op jit(solution)/shard_map/ppermute | solution.py:497
  34.2 6.9 %collective-permute-done.9.refs_1_ = bf16[8,64,512]{2,1,0:T(8,128)(2,1)S(1)} collective-permute-done((bf16[8,64,512]{2,1,0:T(8,128)(2,1)S(1)}, bf16[8,64,512]{2,1,0:T(8,128)(2,1)S(1)}, u32[]{:S(2)}, u32[]{:S(2)}) %collective-permute-start.9) | collective-permute-done | bytes 524320 | tf_op jit(solution)/shard_map/ppermute | solution.py:497
  41.3 1.8 %collective-permute-done.11.refs_3_ = bf16[8,64,512]{2,1,0:T(8,128)(2,1)S(1)} collective-permute-done((bf16[8,64,512]{2,1,0:T(8,128)(2,1)S(1)}, bf16[8,64,512]{2,1,0:T(8,128)(2,1)S(1)}, u32[]{:S(2)}, u32[]{:S(2)}) %collective-permute-start.11) | collective-permute-done | bytes 524320 | tf_op jit(solution)/shard_map/ppermute | solution.py:497
  43.1 5.1 %shard_map.280 = (bf16[640,1536]{1,0:T(8,128)(2,1)S(1)}, f32[20,2,32,256]{3,2,1,0:T(8,128)S(1)}, bf16[640,512]{1,0:T(8,128)(2,1)S(1)}, bf16[640,512]{1,0:T(8,128...) custom-call(s32[32]{0:T(128)S(1)} %get-tuple-element.109.own_ref, ...), custom_call_target="tpu_custom_call" | custom-call | flops 110000000 | bytes 1048576 | tf_op jit(solution)/shard_map/pallas_call | solution.py:483
  49.7 1.4 %collective-permute-done.14.refs_3_ = bf16[8,80,512]{2,1,0:T(8,128)(2,1)S(1)} collective-permute-done((bf16[8,80,512]{2,1,0:T(8,128)(2,1)S(1)}, bf16[8,80,512]{2,1,0:T(8,128)(2,1)S(1)}, u32[]{:S(2)}, u32[]{:S(2)}) %collective-permute-start.14) | collective-permute-done | bytes 655392 | tf_op jit(solution)/shard_map/ppermute | solution.py:497
  51.1 5.3 %shard_map.281 = (bf16[16,64,512]{2,1,0:T(8,128)(2,1)S(1)}, bf16[16,64,512]{2,1,0:T(8,128)(2,1)S(1)}, f32[640,512]{1,0:T(8,128)S(1)}, bf16[640,2048]{1,0:T(8,128...) custom-call(s32[32]{0:T(128)S(1)} %get-tuple-element.109.own_ref, ...), custom_call_target="tpu_custom_call" | custom-call | flops 8800000000 | bytes 1048576 | tf_op jit(solution)/shard_map/pallas_call | solution.py:483
  56.6 3.8 %shard_map.282 = (bf16[16,64,512]{2,1,0:T(8,128)(2,1)S(1)}, bf16[16,64,512]{2,1,0:T(8,128)(2,1)S(1)}, bf16[640,2048]{1,0:T(8,128)(2,1)S(1)}, bf16[512,2048]{1,0:T(8,128)(2,1)S(1)}, f32[8,512]{1,0:T(8,128)S(1)}) custom-call(s32[32]{0:T(128)S(1)} %get-tuple-element.120.own_ref, s32[32]{0:T(128)S(1)} %get-tuple-element.112.own_down_ref, ...), custom_call_target="tpu_custom_call" | custom-call | flops 8800000000 | bytes 1048576 | tf_op jit(solution)/shard_map/pallas_call | solution.py:483
  61.3 2.6 %shard_map.283 = (f32[512,512]{1,0:T(8,128)S(1)}, f32[640,512]{1,0:T(8,128)S(1)}) custom-call(bf16[640,2048]{1,0:T(8,128)(2,1)S(1)} %get-tuple-element.119.hid_ref, bf16[640,2048]{1,0:T(8,128)(2,1)S(1)} %get-tuple-element.130.gpre_ref, bf16[512,2048]{1,0:T(8,128)(2,1)S(1)} %get-tuple-element.131.up_ref, bf16[512,2048]{1,0:T(8,128)(2,1)S(1)} %get-tuple-element.132.down_ref), custom_call_target="tpu_custom_call" | custom-call | flops 110000000 | bytes 1048576 | tf_op jit(solution)/shard_map/pallas_call | solution.py:483
  65.2 1.9 %shard_map.284 = (bf16[512,512]{1,0:T(8,128)(2,1)}, f32[640,512]{1,0:T(8,128)S(1)}, bf16[512,512]{1,0:T(8,128)(2,1)S(1)}, bf16[640,512]{1,0:T(8,128)(2,1)S(1)}, f32[8,512]{1,0:T(8,128)S(1)}) custom-call(f32[640,128]{1,0:T(8,128)S(1)} %broadcast_in_dim.59.keep_ref, bf16[640,512]{1,0:T(8,128)(2,1)S(1)} %pad_maximum_fusion.cot_ref, ...), custom_call_target="tpu_custom_call" | custom-call | flops 110000000 | bytes 1048576 | tf_op jit(solution)/shard_map/pallas_call | solution.py:483
  67.1 2.5 %shard_map.286.gproj_b = bf16[256,1536]{1,0:T(8,128)(2,1)S(1)} custom-call(bf16[640,512]{1,0:T(8,128)(2,1)S(1)} %get-tuple-element.143.gmix_ref, bf16[640,1536]{1,0:T(8,128)(2,1)S(1)} %get-tuple-element.144.proj_ref, f32[20,2,32,256]{3,2,1,0:T(8,128)S(1)} %get-tuple-element.145.prob_ref), custom_call_target="tpu_custom_call" | custom-call | flops 110000000 | bytes 1048576 | tf_op jit(solution)/shard_map/pallas_call | solution.py:483
  69.6 2.5 %shard_map.285.gproj_a = bf16[256,1536]{1,0:T(8,128)(2,1)S(1)} custom-call(bf16[640,512]{1,0:T(8,128)(2,1)S(1)} %get-tuple-element.143.gmix_ref, bf16[640,1536]{1,0:T(8,128)(2,1)S(1)} %get-tuple-element.144.proj_ref, f32[20,2,32,256]{3,2,1,0:T(8,128)S(1)} %get-tuple-element.145.prob_ref), custom_call_target="tpu_custom_call" | custom-call | flops 110000000 | bytes 1048576 | tf_op jit(solution)/shard_map/pallas_call | solution.py:483
  72.1 1.5 %collective-permute-done.19 = bf16[8,64,512]{2,1,0:T(8,128)(2,1)S(1)} collective-permute-done((bf16[8,64,512]{2,1,0:T(8,128)(2,1)S(1)}, bf16[8,64,512]{2,1,0:T(8,128)(2,1)S(1)}, u32[]{:S(2)}, u32[]{:S(2)}) %collective-permute-start.19) | collective-permute-done | bytes 524320 | tf_op jit(solution)/shard_map/ppermute | solution.py:497
  73.8 1.5 %collective-permute-start.20 = (bf16[4,64,512]{2,1,0:T(8,128)(2,1)S(1)}, bf16[4,64,512]{2,1,0:T(8,128)(2,1)S(1)}, u32[]{:S(2)}, u32[]{:S(2)}) collective-permute-start(bf16[4,64,512]{2,1,0:T(8,128)(2,1)S(1)} %slice.150), channel_id=1, source_target_pairs={{0,2},{1,5},{2,0},{3,7},{4,6},{5,1},{6,4},{7,3},{8,10},{9,13},{10,... | collective-permute-start | bytes 786440 | tf_op jit(solution)/shard_map/ppermute | solution.py:497
  75.3 2.5 %shard_map.287 = (bf16[1040,512]{1,0:T(8,128)(2,1)S(1)}, bf16[208,512]{1,0:T(8,128)(2,1)S(1)}, bf16[208,512]{1,0:T(8,128)(2,1)S(1)}, bf16[208,512]{1,0:T(8,128)(...) custom-call(s32[32]{0:T(128)S(1)} %get-tuple-element.150.own_ref, ...), custom_call_target="tpu_custom_call" | custom-call | flops 110000000 | bytes 1048576 | tf_op jit(solution)/shard_map/pallas_call | solution.py:483
  78.5 1.8 %collective-permute-done.20 = bf16[4,64,512]{2,1,0:T(8,128)(2,1)S(1)} collective-permute-done((bf16[4,64,512]{2,1,0:T(8,128)(2,1)S(1)}, bf16[4,64,512]{2,1,0:T(8,128)(2,1)S(1)}, u32[]{:S(2)}, u32[]{:S(2)}) %collective-permute-start.20) | collective-permute-done | bytes 262176 | tf_op jit(solution)/shard_map/ppermute | solution.py:497
  83.9 2.0 %collective-permute-start.28 = (bf16[272,512]{1,0:T(8,128)(2,1)S(1)}, bf16[272,512]{1,0:T(8,128)(2,1)S(1)}, u32[]{:S(2)}, u32[]{:S(2)}) collective-permute-start(bf16[272,512]{1,0:T(8,128)(2,1)S(1)} %get-tuple-element.178), channel_id=1, source_target_pairs={{0,6},{1,7},{2,4},{3,5},{4,2},{5,3},{6,0},{7,1},{8,14},{9,15},{10,... | collective-permute-start | bytes 835592 | tf_op jit(solution)/shard_map/ppermute | solution.py:497
  87.4 2.2 %shard_map.288 = f32[512,512]{1,0:T(8,128)} custom-call(bf16[256,1536]{1,0:T(8,128)(2,1)S(1)} %shard_map.285.gproj_a, bf16[256,1536]{1,0:T(8,128)(2,1)S(1)} %shard_map.286.gproj_b, bf16[640,512]{1,0:T(8,128)(2,1)S(1)} %pad_maximum_fusion.1.x_ref, f32[640,512]{1,0:T(8,128)S(1)} %get-tuple-element.169.gres_ref, ...), custom_call_target="tpu_custom_call" | custom-call | flops 110000000 | bytes 1048576 | tf_op jit(solution)/shard_map/pallas_call | solution.py:483
  89.6 5.7 %collective-permute-done.27 = bf16[6,64,512]{2,1,0:T(8,128)(2,1)S(1)} collective-permute-done((bf16[6,64,512]{2,1,0:T(8,128)(2,1)S(1)}, bf16[6,64,512]{2,1,0:T(8,128)(2,1)S(1)}, u32[]{:S(2)}, u32[]{:S(2)}) %collective-permute-start.27) | collective-permute-done | bytes 393248 | tf_op jit(solution)/shard_map/ppermute | solution.py:497
  95.6 1.8 %collective-permute-start.35 = (bf16[1,64,512]{2,1,0:T(8,128)(2,1)S(1)}, bf16[1,64,512]{2,1,0:T(8,128)(2,1)S(1)}, u32[]{:S(2)}, u32[]{:S(2)}) collective-permute-start(bf16[1,64,512]{2,1,0:T(8,128)(2,1)S(1)} %get-tuple-element.197), channel_id=1, source_target_pairs={{0,6},{1,7},{2,4},{3,5},{4,2},{5,3},{6,0},{7,1},{8,14},{9,15},{10,... | collective-permute-start | bytes 196616 | tf_op jit(solution)/shard_map/ppermute | solution.py:497
  99.5 1.5 %collective-permute-start.36 = (bf16[1,64,512]{2,1,0:T(8,128)(2,1)S(1)}, bf16[1,64,512]{2,1,0:T(8,128)(2,1)S(1)}, u32[]{:S(2)}, u32[]{:S(2)}) collective-permute-start(bf16[1,64,512]{2,1,0:T(8,128)(2,1)S(1)} %get-tuple-element.199), channel_id=1, source_target_pairs={{0,2},{1,5},{2,0},{3,7},{4,6},{5,1},{6,4},{7,3},{8,10},{9,13},{10,... | collective-permute-start | bytes 196616 | tf_op jit(solution)/shard_map/ppermute | solution.py:497
  101.2 1.9 %collective-permute-start.32 = (bf16[80,512]{1,0:T(8,128)(2,1)S(1)}, bf16[80,512]{1,0:T(8,128)(2,1)S(1)}, u32[]{:S(2)}, u32[]{:S(2)}) collective-permute-start(bf16[80,512]{1,0:T(8,128)(2,1)S(1)} %get-tuple-element.186), channel_id=1, source_target_pairs={{0,16},{1,17},{2,18},{3,19},{4,20},{5,21},{6,22},{7,23},{8,24},{9,... | collective-permute-start | bytes 245768 | tf_op jit(solution)/shard_map/ppermute | solution.py:497
  103.9 1.7 %collective-permute-start.34 = (bf16[80,512]{1,0:T(8,128)(2,1)S(1)}, bf16[80,512]{1,0:T(8,128)(2,1)S(1)}, u32[]{:S(2)}, u32[]{:S(2)}) collective-permute-start(bf16[80,512]{1,0:T(8,128)(2,1)S(1)} %get-tuple-element.188), channel_id=1, source_target_pairs={{0,24},{1,25},{2,26},{3,27},{4,28},{5,29},{6,30},{7,31},{8,16},{9,... | collective-permute-start | bytes 245768 | tf_op jit(solution)/shard_map/ppermute | solution.py:497
  107.0 2.2 %collective-permute-done.32.refs_1_ = bf16[80,512]{1,0:T(8,128)(2,1)S(1)} collective-permute-done((bf16[80,512]{1,0:T(8,128)(2,1)S(1)}, bf16[80,512]{1,0:T(8,128)(2,1)S(1)}, u32[]{:S(2)}, u32[]{:S(2)}) %collective-permute-start.32) | collective-permute-done | bytes 81952 | tf_op jit(solution)/shard_map/ppermute | solution.py:497
  (129 shorter events, 20.3 us)
Async XLA Ops:
  2.4 12.2 %collective-permute-start.2 = (bf16[1,144,512]{2,1,0:T(8,128)(2,1)}, bf16[1,144,512]{2,1,0:T(8,128)(2,1)S(1)}, u32[]{:S(2)}, u32[]{:S(2)}) collective-permute-start(bf16[1,144,512]{2,1,0:T(8,128)(2,1)} %bitcast.31), channel_id=1, source_target_pairs={{0,24},{1,25},{2,26},{3,27},{4,28},{5,29},{6,30},{7,31},{8,16},{9,... | collective-permute-start | bytes 442376 | tf_op jit(solution)/shard_map/ppermute | solution.py:497
  7.5 8.4 %collective-permute-start.1 = (bf16[1,144,512]{2,1,0:T(8,128)(2,1)}, bf16[1,144,512]{2,1,0:T(8,128)(2,1)S(1)}, u32[]{:S(2)}, u32[]{:S(2)}) collective-permute-start(bf16[1,144,512]{2,1,0:T(8,128)(2,1)} %bitcast.32), channel_id=1, source_target_pairs={{0,8},{1,9},{2,10},{3,11},{4,12},{5,13},{6,14},{7,15},{8,0},{9,1},... | collective-permute-start | bytes 442376 | tf_op jit(solution)/shard_map/ppermute | solution.py:497
  7.5 12.7 %collective-permute-start = (bf16[1,144,512]{2,1,0:T(8,128)(2,1)}, bf16[1,144,512]{2,1,0:T(8,128)(2,1)S(1)}, u32[]{:S(2)}, u32[]{:S(2)}) collective-permute-start(bf16[1,144,512]{2,1,0:T(8,128)(2,1)} %bitcast.33), channel_id=1, source_target_pairs={{0,16},{1,17},{2,18},{3,19},{4,20},{5,21},{6,22},{7,23},{8,24},{9,... | collective-permute-start | bytes 442376 | tf_op jit(solution)/shard_map/ppermute | solution.py:497
  8.1 4.5 %collective-permute-start.3 = (bf16[1,64,512]{2,1,0:T(8,128)(2,1)}, bf16[1,64,512]{2,1,0:T(8,128)(2,1)S(1)}, u32[]{:S(2)}, u32[]{:S(2)}) collective-permute-start(bf16[1,64,512]{2,1,0:T(8,128)(2,1)} %bitcast.39), channel_id=1, source_target_pairs={{0,2},{1,5},{2,0},{3,7},{4,6},{5,1},{6,4},{7,3},{8,10},{9,13},{10,... | collective-permute-start | bytes 196616 | tf_op jit(solution)/shard_map/ppermute | solution.py:497
  10.8 11.9 %collective-permute-start.8 = (bf16[2,4,16,512]{3,2,1,0:T(8,128)(2,1)S(1)}, bf16[2,4,16,512]{3,2,1,0:T(8,128)(2,1)S(1)}, u32[]{:S(2)}, u32[]{:S(2)}) collective-permute-start(bf16[2,4,16,512]{3,2,1,0:T(8,128)(2,1)S(1)} %get-tuple-element.195), channel_id=1, source_target_pairs={{1,0},{2,1},{3,2},{5,4},{6,5},{7,6},{9,8},{10,9},{11,10},{13,12},{... | collective-permute-start | bytes 393224 | tf_op jit(solution)/shard_map/ppermute | solution.py:550
  12.6 7.6 %collective-permute-start.4 = (bf16[2,64,512]{2,1,0:T(8,128)(2,1)S(1)}, bf16[2,64,512]{2,1,0:T(8,128)(2,1)S(1)}, u32[]{:S(2)}, u32[]{:S(2)}) collective-permute-start(bf16[2,64,512]{2,1,0:T(8,128)(2,1)S(1)} %pad_maximum_fusion.6), channel_id=1, source_target_pairs={{0,4},{1,3},{2,6},{3,1},{4,0},{5,7},{6,2},{7,5},{8,12},{9,11},{10,... | collective-permute-start | bytes 393224 | tf_op jit(solution)/shard_map/ppermute | solution.py:497
  14.6 8.0 %collective-permute-start.7 = (bf16[2,4,16,512]{3,2,1,0:T(8,128)(2,1)S(1)}, bf16[2,4,16,512]{3,2,1,0:T(8,128)(2,1)S(1)}, u32[]{:S(2)}, u32[]{:S(2)}) collective-permute-start(bf16[2,4,16,512]{3,2,1,0:T(8,128)(2,1)S(1)} %get-tuple-element.196), channel_id=1, source_target_pairs={{0,1},{1,2},{2,3},{4,5},{5,6},{6,7},{8,9},{9,10},{10,11},{12,13},{... | collective-permute-start | bytes 393224 | tf_op jit(solution)/shard_map/ppermute | solution.py:549
  20.4 11.3 %collective-permute-start.5 = (bf16[4,144,512]{2,1,0:T(8,128)(2,1)S(1)}, bf16[4,144,512]{2,1,0:T(8,128)(2,1)S(1)}, u32[]{:S(2)}, u32[]{:S(2)}) collective-permute-start(bf16[4,144,512]{2,1,0:T(8,128)(2,1)S(1)} %pad_maximum_fusion.2), channel_id=1, source_target_pairs={{0,4},{1,3},{2,6},{3,1},{4,0},{5,7},{6,2},{7,5},{8,12},{9,11},{10,... | collective-permute-start | bytes 1769480 | tf_op jit(solution)/shard_map/ppermute | solution.py:497
  22.0 9.7 %collective-permute-start.6 = (bf16[4,64,512]{2,1,0:T(8,128)(2,1)S(1)}, bf16[4,64,512]{2,1,0:T(8,128)(2,1)S(1)}, u32[]{:S(2)}, u32[]{:S(2)}) collective-permute-start(bf16[4,64,512]{2,1,0:T(8,128)(2,1)S(1)} %constant_dynamic-update-slice_fusion), channel_id=1, source_target_pairs={{0,16},{1,9},{2,18},{3,11},{4,20},{5,13},{6,22},{7,15},{8,24},{9,1... | collective-permute-start | bytes 786440 | tf_op jit(solution)/shard_map/ppermute | solution.py:497
  31.8 11.3 %collective-permute-start.10 = (bf16[8,144,512]{2,1,0:T(8,128)(2,1)S(1)}, bf16[8,144,512]{2,1,0:T(8,128)(2,1)S(1)}, u32[]{:S(2)}, u32[]{:S(2)}) collective-permute-start(bf16[8,144,512]{2,1,0:T(8,128)(2,1)S(1)} %constant_dynamic-update-slice_fusion.4.refs_0_), channel_id=1, source_target_pairs={{0,1},{1,0},{2,3},{3,2},{4,5},{5,4},{6,7},{7,6},{8,9},{9,8},{10,11... | collective-permute-start | bytes 3538952 | tf_op jit(solution)/shard_map/ppermute | solution.py:497
  31.9 9.2 %collective-permute-start.9 = (bf16[8,64,512]{2,1,0:T(8,128)(2,1)S(1)}, bf16[8,64,512]{2,1,0:T(8,128)(2,1)S(1)}, u32[]{:S(2)}, u32[]{:S(2)}) collective-permute-start(bf16[8,64,512]{2,1,0:T(8,128)(2,1)S(1)} %slice.106), channel_id=1, source_target_pairs={{0,2},{1,5},{2,0},{3,7},{4,6},{5,1},{6,4},{7,3},{8,10},{9,13},{10,... | collective-permute-start | bytes 1572872 | tf_op jit(solution)/shard_map/ppermute | solution.py:497
  33.5 15.5 %collective-permute-start.12 = (bf16[8,80,512]{2,1,0:T(8,128)(2,1)S(1)}, bf16[8,80,512]{2,1,0:T(8,128)(2,1)S(1)}, u32[]{:S(2)}, u32[]{:S(2)}) collective-permute-start(bf16[8,80,512]{2,1,0:T(8,128)(2,1)S(1)} %slice.107), channel_id=1, source_target_pairs={{0,2},{1,5},{2,0},{3,7},{4,6},{5,1},{6,4},{7,3},{8,10},{9,13},{10,... | collective-permute-start | bytes 1966088 | tf_op jit(solution)/shard_map/ppermute | solution.py:497
  34.2 14.9 %collective-permute-start.13 = (bf16[8,64,512]{2,1,0:T(8,128)(2,1)S(1)}, bf16[8,64,512]{2,1,0:T(8,128)(2,1)S(1)}, u32[]{:S(2)}, u32[]{:S(2)}) collective-permute-start(bf16[8,64,512]{2,1,0:T(8,128)(2,1)S(1)} %constant_dynamic-update-slice_fusion.9.refs_0_), channel_id=1, source_target_pairs={{0,8},{1,17},{2,10},{3,19},{4,12},{5,21},{6,14},{7,23},{8,0},{9,25... | collective-permute-start | bytes 1572872 | tf_op jit(solution)/shard_map/ppermute | solution.py:497
  49.1 7.6 %collective-permute-start.15 = (bf16[8,64,512]{2,1,0:T(8,128)(2,1)S(1)}, bf16[8,64,512]{2,1,0:T(8,128)(2,1)S(1)}, u32[]{:S(2)}, u32[]{:S(2)}) collective-permute-start(bf16[8,64,512]{2,1,0:T(8,128)(2,1)S(1)} %constant_dynamic-update-slice_fusion.9.refs_0_), channel_id=1, source_target_pairs={{0,1},{1,0},{2,3},{3,2},{4,5},{5,4},{6,7},{7,6},{8,9},{9,8},{10,11... | collective-permute-start | bytes 1572872 | tf_op jit(solution)/shard_map/ppermute | solution.py:497
  49.6 7.0 %collective-permute-start.16 = (bf16[8,64,512]{2,1,0:T(8,128)(2,1)S(1)}, bf16[8,64,512]{2,1,0:T(8,128)(2,1)S(1)}, u32[]{:S(2)}, u32[]{:S(2)}) collective-permute-start(bf16[8,64,512]{2,1,0:T(8,128)(2,1)S(1)} %collective-permute-done.13.refs_1_), channel_id=1, source_target_pairs={{0,1},{1,0},{2,3},{3,2},{4,5},{5,4},{6,7},{7,6},{8,9},{9,8},{10,11... | collective-permute-start | bytes 1572872 | tf_op jit(solution)/shard_map/ppermute | solution.py:497
  56.4 4.5 %collective-permute-start.17 = (bf16[16,64,512]{2,1,0:T(8,128)(2,1)S(1)}, bf16[16,64,512]{2,1,0:T(8,128)(2,1)S(1)}, u32[]{:S(2)}, u32[]{:S(2)}) collective-permute-start(bf16[16,64,512]{2,1,0:T(8,128)(2,1)S(1)} %get-tuple-element.128), channel_id=1, source_target_pairs={{0,1},{1,0},{2,3},{3,2},{4,5},{5,4},{6,7},{7,6},{8,9},{9,8},{10,11... | collective-permute-start | bytes 3145736 | tf_op jit(solution)/shard_map/ppermute | solution.py:497
  60.5 3.5 %collective-permute-start.18 = (bf16[16,64,512]{2,1,0:T(8,128)(2,1)S(1)}, bf16[16,64,512]{2,1,0:T(8,128)(2,1)S(1)}, u32[]{:S(2)}, u32[]{:S(2)}) collective-permute-start(bf16[16,64,512]{2,1,0:T(8,128)(2,1)S(1)} %get-tuple-element.136), channel_id=1, source_target_pairs={{0,1},{1,0},{2,3},{3,2},{4,5},{5,4},{6,7},{7,6},{8,9},{9,8},{10,11... | collective-permute-start | bytes 3145736 | tf_op jit(solution)/shard_map/ppermute | solution.py:497
  64.4 9.2 %collective-permute-start.19 = (bf16[8,64,512]{2,1,0:T(8,128)(2,1)S(1)}, bf16[8,64,512]{2,1,0:T(8,128)(2,1)S(1)}, u32[]{:S(2)}, u32[]{:S(2)}) collective-permute-start(bf16[8,64,512]{2,1,0:T(8,128)(2,1)S(1)} %slice.147), channel_id=1, source_target_pairs={{0,4},{1,3},{2,6},{3,1},{4,0},{5,7},{6,2},{7,5},{8,12},{9,11},{10,... | collective-permute-start | bytes 1572872 | tf_op jit(solution)/shard_map/ppermute | solution.py:497
  65.2 15.0 %collective-permute-start.21 = (bf16[8,64,512]{2,1,0:T(8,128)(2,1)S(1)}, bf16[8,64,512]{2,1,0:T(8,128)(2,1)S(1)}, u32[]{:S(2)}, u32[]{:S(2)}) collective-permute-start(bf16[8,64,512]{2,1,0:T(8,128)(2,1)S(1)} %slice.148), channel_id=1, source_target_pairs={{0,8},{1,17},{2,10},{3,19},{4,12},{5,21},{6,14},{7,23},{8,0},{9,25... | collective-permute-start | bytes 1572872 | tf_op jit(solution)/shard_map/ppermute | solution.py:497
  73.8 6.4 %collective-permute-start.20 = (bf16[4,64,512]{2,1,0:T(8,128)(2,1)S(1)}, bf16[4,64,512]{2,1,0:T(8,128)(2,1)S(1)}, u32[]{:S(2)}, u32[]{:S(2)}) collective-permute-start(bf16[4,64,512]{2,1,0:T(8,128)(2,1)S(1)} %slice.150), channel_id=1, source_target_pairs={{0,2},{1,5},{2,0},{3,7},{4,6},{5,1},{6,4},{7,3},{8,10},{9,13},{10,... | collective-permute-start | bytes 786440 | tf_op jit(solution)/shard_map/ppermute | solution.py:497
  77.8 3.0 %collective-permute-start.22 = (bf16[208,512]{1,0:T(8,128)(2,1)S(1)}, bf16[208,512]{1,0:T(8,128)(2,1)S(1)}, u32[]{:S(2)}, u32[]{:S(2)}) collective-permute-start(bf16[208,512]{1,0:T(8,128)(2,1)S(1)} %get-tuple-element.161), channel_id=1, source_target_pairs={{0,1},{1,0},{2,3},{3,2},{4,5},{5,4},{6,7},{7,6},{8,9},{9,8},{10,11... | collective-permute-start | bytes 638984 | tf_op jit(solution)/shard_map/ppermute | solution.py:497
  82.4 13.0 %collective-permute-start.27 = (bf16[6,64,512]{2,1,0:T(8,128)(2,1)S(1)}, bf16[6,64,512]{2,1,0:T(8,128)(2,1)S(1)}, u32[]{:S(2)}, u32[]{:S(2)}) collective-permute-start(bf16[6,64,512]{2,1,0:T(8,128)(2,1)S(1)} %pad_maximum_fusion.3), channel_id=1, source_target_pairs={{0,16},{1,9},{2,18},{3,11},{4,20},{5,13},{6,22},{7,15},{8,24},{9,1... | collective-permute-start | bytes 1179656 | tf_op jit(solution)/shard_map/ppermute | solution.py:497
  83.9 13.6 %collective-permute-start.28 = (bf16[272,512]{1,0:T(8,128)(2,1)S(1)}, bf16[272,512]{1,0:T(8,128)(2,1)S(1)}, u32[]{:S(2)}, u32[]{:S(2)}) collective-permute-start(bf16[272,512]{1,0:T(8,128)(2,1)S(1)} %get-tuple-element.178), channel_id=1, source_target_pairs={{0,6},{1,7},{2,4},{3,5},{4,2},{5,3},{6,0},{7,1},{8,14},{9,15},{10,... | collective-permute-start | bytes 835592 | tf_op jit(solution)/shard_map/ppermute | solution.py:497
  85.9 13.6 %collective-permute-start.29 = (bf16[272,512]{1,0:T(8,128)(2,1)S(1)}, bf16[272,512]{1,0:T(8,128)(2,1)S(1)}, u32[]{:S(2)}, u32[]{:S(2)}) collective-permute-start(bf16[272,512]{1,0:T(8,128)(2,1)S(1)} %get-tuple-element.179), channel_id=1, source_target_pairs={{0,2},{1,3},{2,0},{3,1},{4,6},{5,7},{6,4},{7,5},{8,10},{9,11},{10,... | collective-permute-start | bytes 835592 | tf_op jit(solution)/shard_map/ppermute | solution.py:497
  86.9 14.1 %collective-permute-start.30 = (bf16[272,512]{1,0:T(8,128)(2,1)S(1)}, bf16[272,512]{1,0:T(8,128)(2,1)S(1)}, u32[]{:S(2)}, u32[]{:S(2)}) collective-permute-start(bf16[272,512]{1,0:T(8,128)(2,1)S(1)} %get-tuple-element.180), channel_id=1, source_target_pairs={{0,4},{1,5},{2,6},{3,7},{4,0},{5,1},{6,2},{7,3},{8,12},{9,13},{10,... | collective-permute-start | bytes 835592 | tf_op jit(solution)/shard_map/ppermute | solution.py:497
  95.5 5.5 %collective-permute-start.31 = (bf16[1,64,512]{2,1,0:T(8,128)(2,1)S(1)}, bf16[1,64,512]{2,1,0:T(8,128)(2,1)S(1)}, u32[]{:S(2)}, u32[]{:S(2)}) collective-permute-start(bf16[1,64,512]{2,1,0:T(8,128)(2,1)S(1)} %slice.152), channel_id=1, source_target_pairs={{0,8},{1,17},{2,10},{3,19},{4,12},{5,21},{6,14},{7,23},{8,0},{9,25... | collective-permute-start | bytes 196616 | tf_op jit(solution)/shard_map/ppermute | solution.py:497
  95.6 8.3 %collective-permute-start.35 = (bf16[1,64,512]{2,1,0:T(8,128)(2,1)S(1)}, bf16[1,64,512]{2,1,0:T(8,128)(2,1)S(1)}, u32[]{:S(2)}, u32[]{:S(2)}) collective-permute-start(bf16[1,64,512]{2,1,0:T(8,128)(2,1)S(1)} %get-tuple-element.197), channel_id=1, source_target_pairs={{0,6},{1,7},{2,4},{3,5},{4,2},{5,3},{6,0},{7,1},{8,14},{9,15},{10,... | collective-permute-start | bytes 196616 | tf_op jit(solution)/shard_map/ppermute | solution.py:497
  97.4 8.2 %collective-permute-start.37 = (bf16[1,64,512]{2,1,0:T(8,128)(2,1)S(1)}, bf16[1,64,512]{2,1,0:T(8,128)(2,1)S(1)}, u32[]{:S(2)}, u32[]{:S(2)}) collective-permute-start(bf16[1,64,512]{2,1,0:T(8,128)(2,1)S(1)} %get-tuple-element.198), channel_id=1, source_target_pairs={{0,4},{1,3},{2,6},{3,1},{4,0},{5,7},{6,2},{7,5},{8,12},{9,11},{10,... | collective-permute-start | bytes 196616 | tf_op jit(solution)/shard_map/ppermute | solution.py:497
  99.5 6.1 %collective-permute-start.36 = (bf16[1,64,512]{2,1,0:T(8,128)(2,1)S(1)}, bf16[1,64,512]{2,1,0:T(8,128)(2,1)S(1)}, u32[]{:S(2)}, u32[]{:S(2)}) collective-permute-start(bf16[1,64,512]{2,1,0:T(8,128)(2,1)S(1)} %get-tuple-element.199), channel_id=1, source_target_pairs={{0,2},{1,5},{2,0},{3,7},{4,6},{5,1},{6,4},{7,3},{8,10},{9,13},{10,... | collective-permute-start | bytes 196616 | tf_op jit(solution)/shard_map/ppermute | solution.py:497
  101.2 8.0 %collective-permute-start.32 = (bf16[80,512]{1,0:T(8,128)(2,1)S(1)}, bf16[80,512]{1,0:T(8,128)(2,1)S(1)}, u32[]{:S(2)}, u32[]{:S(2)}) collective-permute-start(bf16[80,512]{1,0:T(8,128)(2,1)S(1)} %get-tuple-element.186), channel_id=1, source_target_pairs={{0,16},{1,17},{2,18},{3,19},{4,20},{5,21},{6,22},{7,23},{8,24},{9,... | collective-permute-start | bytes 245768 | tf_op jit(solution)/shard_map/ppermute | solution.py:497
  103.1 6.1 %collective-permute-start.33 = (bf16[80,512]{1,0:T(8,128)(2,1)S(1)}, bf16[80,512]{1,0:T(8,128)(2,1)S(1)}, u32[]{:S(2)}, u32[]{:S(2)}) collective-permute-start(bf16[80,512]{1,0:T(8,128)(2,1)S(1)} %get-tuple-element.187), channel_id=1, source_target_pairs={{0,8},{1,9},{2,10},{3,11},{4,12},{5,13},{6,14},{7,15},{8,0},{9,1},... | collective-permute-start | bytes 245768 | tf_op jit(solution)/shard_map/ppermute | solution.py:497
  103.9 6.3 %collective-permute-start.34 = (bf16[80,512]{1,0:T(8,128)(2,1)S(1)}, bf16[80,512]{1,0:T(8,128)(2,1)S(1)}, u32[]{:S(2)}, u32[]{:S(2)}) collective-permute-start(bf16[80,512]{1,0:T(8,128)(2,1)S(1)} %get-tuple-element.188), channel_id=1, source_target_pairs={{0,24},{1,25},{2,26},{3,27},{4,28},{5,29},{6,30},{7,31},{8,16},{9,... | collective-permute-start | bytes 245768 | tf_op jit(solution)/shard_map/ppermute | solution.py:497
  (17 other events, 138.5 us)
